TPU v7x, 256 devices: a whole 4x4x8 slice. The times are simulated.
256 devices in a mesh: gx: 4 (over x), gy: 8 (over z), gz: 8 (over y, core).
Axes of the slice: x: 4, y: 4, z: 8, core: 2. Of those that a mesh axis runs over, the one named last changes fastest.
Arguments:
- residual: bfloat16 [4, 8, 8, 512, 1536], P('gx', 'gy', 'gz'), may hold values from -6 to 6
- schur_inverse: bfloat16 [4, 8, 8, 1536, 1536], P('gx', 'gy', 'gz'), may hold values from -0.15625 to 0.15625
- coarse_basis: bfloat16 [4, 8, 8, 128, 1536], P('gx', 'gy', 'gz'), may hold values from -0.25 to 0.25
- coarse_index: int32 [4, 8, 8, 128], P('gx', 'gy', 'gz'), may hold values from 0 to 511
- block_slot: int32 [4, 8, 8, 12], P('gx', 'gy', 'gz'), may hold values from 0 to 1, as said below
- group_inverse: float32 [4, 8, 512, 512], P('gx', 'gy'), may hold values from -0.25 to 0.25
- group_restrict: float32 [4, 8, 512, 512], P('gx', 'gy'), may hold values from -0.25 to 0.25
- top_inverse: float32 [512, 512], replicated, may hold values from -0.046875 to 0.046875
Outputs:
- correction: bfloat16 [4, 8, 8, 512, 1536], P('gx', 'gy', 'gz')
Inputs may be any that keep to these rules, and one draw needn't show every extreme that they name: `block_slot`: for every subdomain and face, the 2 entries of that face are a permutation of 0 to 1.
All inputs are finite; a program needn't handle non-finite values.
Results may differ from a plain program's by a relative error of at most 0.0055.
Values may be sent and summed in bfloat16 or wider, within the bound.
No kernel may reach another device: no remote copies, remote signals or barrier semaphores. Data moves between devices by JAX's collectives and lax.ppermute only.
A program may use at most 64 MiB of HBM per device.

v0:
```python
import jax
import jax.numpy as jnp
from jax import lax
from jax.sharding import PartitionSpec as P

BW = 128
FB = 2
NI = 1536


exact_prec = lax.Precision.HIGHEST


def with_halo(cells, sides, width):
    for axis, dim in sides:
        count = lax.axis_size(axis)
        ends = count - 1
        head = lax.slice_in_dim(cells, 0, width, axis=dim)
        tail = lax.slice_in_dim(cells, cells.shape[dim] - width, cells.shape[dim], axis=dim)
        cells = jnp.concatenate(
            [
                lax.ppermute(tail, axis, [(i, (i + 1) % count) for i in range(ends)]),
                cells,
                lax.ppermute(head, axis, [((i + 1) % count, i) for i in range(ends)]),
            ],
            axis=dim,
        )
    return cells


def face_pair(slotted, lower_face):
    return jnp.stack([slotted[:, lower_face], slotted[:, lower_face + 1]], axis=0)


def assemble_pair(padded, slotted, lower_face, place, length):
    own_low = slotted[:, lower_face].astype(jnp.float32)
    own_high = slotted[:, lower_face + 1].astype(jnp.float32)
    weight_low = jnp.where(place > 0, 0.5, 1.0).astype(jnp.float32)
    weight_high = jnp.where(place < length - 1, 0.5, 1.0).astype(jnp.float32)
    low_sum = weight_low * (own_low + padded[0].astype(jnp.float32))
    high_sum = weight_high * (own_high + padded[3].astype(jnp.float32))
    return [low_sum, high_sum]


def per_device(
    residual,
    schur_inverse,
    coarse_basis,
    coarse_index,
    block_slot,
    group_inverse,
    group_restrict,
    top_inverse,
):
    res_rows = residual[0, 0, 0]
    schur_block = schur_inverse[0, 0, 0]
    basis_rows = coarse_basis[0, 0, 0]
    index_row = coarse_index[0, 0, 0]
    slot_map = block_slot[0, 0, 0]
    group_inv = group_inverse[0, 0]
    restrict = group_restrict[0, 0]
    rhs_count = res_rows.shape[0]
    group_width = group_inv.shape[0]
    contract_last = (((1,), (1,)), ((), ()))
    coarse_part = lax.dot_general(
        res_rows, basis_rows, contract_last, preferred_element_type=jnp.float32
    )
    onehot = (index_row[:, None] == jnp.arange(group_width, dtype=jnp.int32)[None, :]).astype(
        jnp.float32
    )
    assembled = jnp.dot(coarse_part, onehot, precision=exact_prec)
    group_res = lax.psum(assembled, "gz")
    top_res = lax.psum(jnp.dot(group_res, restrict, precision=exact_prec), ("gx", "gy"))
    local_sol = jnp.dot(res_rows, schur_block, preferred_element_type=jnp.float32)
    top_sol = jnp.dot(top_res, top_inverse, precision=exact_prec)
    group_sol = jnp.dot(group_res, group_inv, precision=exact_prec)
    group_sol = group_sol + lax.dot_general(top_sol, restrict, contract_last, precision=exact_prec)
    local_coarse = lax.dot_general(group_sol, onehot, contract_last, precision=exact_prec).astype(
        jnp.bfloat16
    )
    update = (
        local_sol + jnp.dot(local_coarse, basis_rows, preferred_element_type=jnp.float32)
    ).astype(jnp.bfloat16)
    blocks = update.reshape(rhs_count, 6, FB, BW)
    slot_onehot = (
        slot_map.reshape(6, FB)[:, :, None] == jnp.arange(FB, dtype=jnp.int32)[None, None, :]
    ).astype(jnp.bfloat16)
    slotted = jnp.einsum(
        "rfbw,fbk->rfkw", blocks, slot_onehot, preferred_element_type=jnp.float32
    ).astype(jnp.bfloat16)
    padded_x = with_halo(face_pair(slotted, 0), (("gx", 0),), 1)
    padded_y = with_halo(face_pair(slotted, 2), (("gy", 0),), 1)
    padded_z = with_halo(face_pair(slotted, 4), (("gz", 0),), 1)
    face_list = assemble_pair(padded_x, slotted, 0, lax.axis_index("gx"), lax.axis_size("gx"))
    face_list = face_list + assemble_pair(
        padded_y, slotted, 2, lax.axis_index("gy"), lax.axis_size("gy")
    )
    face_list = face_list + assemble_pair(
        padded_z, slotted, 4, lax.axis_index("gz"), lax.axis_size("gz")
    )
    shared = jnp.stack(face_list, axis=1)
    placed = jnp.einsum(
        "rfkw,fbk->rfbw", shared, slot_onehot.astype(jnp.float32), precision=exact_prec
    )
    return placed.reshape(1, 1, 1, rhs_count, NI).astype(jnp.bfloat16)


def solution(mesh):
    return jax.shard_map(
        per_device,
        mesh=mesh,
        in_specs=(
            P("gx", "gy", "gz", None, None),
            P("gx", "gy", "gz", None, None),
            P("gx", "gy", "gz", None, None),
            P("gx", "gy", "gz", None),
            P("gx", "gy", "gz", None),
            P("gx", "gy", None, None),
            P("gx", "gy", None, None),
            P(),
        ),
        out_specs=P("gx", "gy", "gz", None, None),
        check_vma=False,
    )
```

profile of v0, /device:TPU:1, one launch (start us, length us, event | category | flops | bytes accessed | tf_op | source)
XLA Modules:
  0.0 290.0 jit_solution(17047966601257523573)
XLA Ops:
  6.5 0.0 copy-start
  6.5 0.0 copy-start.2
  6.5 0.0 all-reduce.3.cloned.1.call-start
  6.5 1.4 copy-done
  7.9 1.6 fusion.3
  9.5 0.0 copy-start.8
  9.5 2.3 fusion.30
  11.8 0.0 all-reduce.3.cloned.1.call-update
  11.8 0.0 all-reduce.5.cloned.1.call-start
  11.9 69.5 %all-reduce.3.cloned.1.call-done = f32[512,512]{1,0:T(8,128)} async-done(((f32[512,512]{1,0:T(8,128)}), f32[512,512]{1,0:T(8,128)}) %all-reduce.3.cloned.1.call-update) | async-done | bytes 1048592 | tf_op jit(solution)/shard_map/psum | solution.py:72
  81.4 0.0 copy-done.2
  81.4 4.1 %fusion.12 = f32[512,512]{1,0:T(8,128)} fusion(f32[512,512]{1,0:T(8,128)} %all-reduce.3.cloned.1.call-done, f32[1,1,512,512]{3,2,1,0:T(8,128)S(1)} %copy-done.2), kind=kOutput, calls=%fused_computation.15 | convolution fusion | flops 1610612736 | bytes 3145728 | tf_op jit(solution)/shard_map/dot_general | solution.py:73
  85.4 0.0 all-reduce.5.cloned.1.call-update
  85.5 0.5 broadcast.9
  86.0 0.0 copy-done.8
  86.0 0.7 reduce.3
  86.6 0.1 eq.30
  86.7 0.0 copy-start.1
  86.7 0.0 copy-start.6
  86.7 6.7 %fusion = f32[512,1536]{1,0:T(8,128)} fusion(bf16[1,1,1,1536,1536]{4,3,2,1,0:T(8,128)(2,1)} %param.9, bf16[1,1,1,512,1536]{4,3,2,1,0:T(8,128)(2,1)S(1)} %copy-done), kind=kOutput, calls=%fused_computation | convolution fusion | flops 2415919104 | bytes 9437184 | tf_op jit(solution)/shard_map/dot_general | solution.py:74
  93.4 0.0 copy-done.1
  93.4 0.0 copy-done.6
  93.4 2.8 fusion.14
  96.3 0.0 copy-start.7
  96.3 135.5 %all-reduce.5.cloned.1.call-done = f32[512,512]{1,0:T(8,128)} async-done(((f32[512,512]{1,0:T(8,128)}), f32[512,512]{1,0:T(8,128)}) %all-reduce.5.cloned.1.call-update) | async-done | bytes 1048592 | tf_op jit(solution)/shard_map/psum | solution.py:73
  231.7 0.0 copy-start.3
  231.7 3.5 %fusion.35 = f32[512,512]{1,0:T(8,128)S(1)} fusion(f32[512,512]{1,0:T(8,128)} %all-reduce.5.cloned.1.call-done, f32[512,512]{1,0:T(8,128)} %param.15), kind=kOutput, calls=%fused_computation.52 | convolution fusion | flops 1610612736 | bytes 3145728 | tf_op jit(solution)/shard_map/dot_general | solution.py:75
  235.2 0.0 copy-done.3
  235.2 0.0 copy-start.4
  235.2 0.0 copy-start.5
  235.3 1.9 convolution_add_fusion.1
  237.1 0.0 copy-done.7
  237.1 0.7 convolution_convert_fusion.2
  237.8 0.0 copy-done.4
  237.8 0.0 copy-done.5
  237.8 0.6 fusion.2
  238.4 1.5 reshape.91
  239.9 4.0 %fusion.8 = bf16[512,6,2,128]{3,2,0,1:T(2,128)(2,1)S(1)} fusion(bf16[512,6,2,128]{3,2,1,0:T(2,128)(2,1)} %reshape.91, s32[6,2]{1,0:T(8,128)S(1)} %eq.30), kind=kOutput, calls=%fused_computation.11 | convolution fusion | flops 3932184 | bytes 3145776 | tf_op jit(solution)/shard_map/rfbw,fbk->rfkw/dot_general | solution.py:88
  243.9 2.0 slice_bitcast_fusion.1
  245.9 3.3 %collective-permute-start = (bf16[1,512,2,128]{3,2,1,0:T(2,128)(2,1)}, bf16[1,512,2,128]{3,2,1,0:T(2,128)(2,1)}, u32[]{:S(2)}, u32[]{:S(2)}) collective-permute-start(bf16[1,512,2,128]{3,2,1,0:T(2,128)(2,1)} %get-tuple-element.10), channel_id=1, source_target_pairs={{0,64},{64,128},{128,192},{1,65},{65,129},{129,193},{2,66},{66,130... | collective-permute-start | bytes 786440 | tf_op jit(solution)/shard_map/ppermute | solution.py:22
  249.2 1.3 collective-permute-start.1
  250.5 2.1 collective-permute-start.2
  252.7 1.3 collective-permute-start.3
  254.0 8.7 %collective-permute-start.4 = (bf16[1,512,2,128]{3,2,1,0:T(2,128)(2,1)}, bf16[1,512,2,128]{3,2,1,0:T(2,128)(2,1)S(1)}, u32[]{:S(2)}, u32[]{:S(2)}) collective-permute-start(bf16[1,512,2,128]{3,2,1,0:T(2,128)(2,1)} %get-tuple-element.8), channel_id=1, source_target_pairs={{0,1},{1,2},{2,3},{3,4},{4,5},{5,6},{6,7},{8,9},{9,10},{10,11},{11... | collective-permute-start | bytes 786440 | tf_op jit(solution)/shard_map/ppermute | solution.py:22
  262.7 0.0 collective-permute-done
  262.7 1.9 collective-permute-start.5
  264.6 1.2 fusion.27
  265.8 0.0 collective-permute-done.1
  265.8 1.3 fusion.25
  267.1 0.0 collective-permute-done.2
  267.1 0.3 fusion.23
  267.4 0.0 collective-permute-done.3
  267.5 0.3 fusion.21
  267.8 0.0 collective-permute-done.4
  267.8 0.3 fusion.19
  268.1 2.3 collective-permute-done.5
  270.4 0.3 fusion.17
  270.7 7.3 %fusion.7 = bf16[512,6,2,128]{3,2,0,1:T(2,128)(2,1)} fusion(f32[512,6,2,128]{3,2,0,1:T(2,128)S(1)} %fusion.17, s32[6,2]{1,0:T(8,128)S(1)} %eq.30), kind=kOutput, calls=%fused_computation.10 | convolution fusion | flops 19660824 | bytes 4718640 | tf_op jit(solution)/shard_map/rfkw,fbk->rfbw/dot_general | solution.py:102
  278.0 3.6 %copy.13 = bf16[512,6,2,128]{0,3,2,1:T(8,128)(2,1)S(1)} copy(bf16[512,6,2,128]{3,2,0,1:T(2,128)(2,1)} %fusion.7) | data formatting | bytes 3145728 | tf_op jit(solution)/shard_map/convert_element_type | solution.py:105
  281.6 1.6 copy.14
Async XLA Ops:
  6.5 1.4 copy-start
  6.5 74.8 %copy-start.2 = (f32[1,1,512,512]{3,2,1,0:T(8,128)S(1)}, f32[1,1,512,512]{3,2,1,0:T(8,128)}, u32[]{:S(2)}) copy-start(f32[1,1,512,512]{3,2,1,0:T(8,128)} %param.14) | copy-start | bytes 3145732
  6.5 74.8 %all-reduce.3.cloned.1.call-start = ((), (), s32[]{:S(2)}) async-start(), calls=%async_computation | async-start | bytes 2097152 | tf_op jit(solution)/shard_map/psum | solution.py:72
  9.5 76.5 %copy-start.8 = (s32[1,1,1,12]{3,2,1,0:T(1,128)S(1)}, s32[1,1,1,12]{3,2,1,0:T(1,128)}, u32[]{:S(2)}) copy-start(s32[1,1,1,12]{3,2,1,0:T(1,128)} %param.12) | copy-start | bytes 148
  11.8 219.9 %all-reduce.5.cloned.1.call-start = ((), (), s32[]{:S(2)}) async-start(), calls=%async_computation.1 | async-start | bytes 2097152 | tf_op jit(solution)/shard_map/psum | solution.py:73
  86.7 6.7 %copy-start.1 = (f32[512,512]{1,0:T(8,128)S(1)}, f32[512,512]{1,0:T(8,128)}, u32[]{:S(2)}) copy-start(f32[512,512]{1,0:T(8,128)} %all-reduce.3.cloned.1.call-done) | copy-start | bytes 3145732
  86.7 6.7 %copy-start.6 = (f32[1,1,512,512]{3,2,1,0:T(8,128)S(1)}, f32[1,1,512,512]{3,2,1,0:T(8,128)}, u32[]{:S(2)}) copy-start(f32[1,1,512,512]{3,2,1,0:T(8,128)} %param.13) | copy-start | bytes 3145732
  96.3 140.9 %copy-start.7 = (s32[1,1,1,128]{3,2,1,0:T(1,128)S(1)}, s32[1,1,1,128]{3,2,1,0:T(1,128)}, u32[]{:S(2)}) copy-start(s32[1,1,1,128]{3,2,1,0:T(1,128)} %param.11) | copy-start | bytes 1540
  231.7 3.5 %copy-start.3 = (f32[512,512]{1,0:T(8,128)S(1)}, f32[512,512]{1,0:T(8,128)}, u32[]{:S(2)}) copy-start(f32[512,512]{1,0:T(8,128)} %fusion.14) | copy-start | bytes 3145732
  235.2 2.6 copy-start.4
  235.2 2.6 copy-start.5
  245.9 16.8 %collective-permute-start = (bf16[1,512,2,128]{3,2,1,0:T(2,128)(2,1)}, bf16[1,512,2,128]{3,2,1,0:T(2,128)(2,1)}, u32[]{:S(2)}, u32[]{:S(2)}) collective-permute-start(bf16[1,512,2,128]{3,2,1,0:T(2,128)(2,1)} %get-tuple-element.10), channel_id=1, source_target_pairs={{0,64},{64,128},{128,192},{1,65},{65,129},{129,193},{2,66},{66,130... | collective-permute-start | bytes 786440 | tf_op jit(solution)/shard_map/ppermute | solution.py:22
  249.2 16.6 %collective-permute-start.1 = (bf16[1,512,2,128]{3,2,1,0:T(2,128)(2,1)}, bf16[1,512,2,128]{3,2,1,0:T(2,128)(2,1)}, u32[]{:S(2)}, u32[]{:S(2)}) collective-permute-start(bf16[1,512,2,128]{3,2,1,0:T(2,128)(2,1)} %get-tuple-element.6), channel_id=1, source_target_pairs={{64,0},{128,64},{192,128},{65,1},{129,65},{193,129},{66,2},{130,66... | collective-permute-start | bytes 786440 | tf_op jit(solution)/shard_map/ppermute | solution.py:24
  250.5 16.6 %collective-permute-start.2 = (bf16[1,512,2,128]{3,2,1,0:T(2,128)(2,1)}, bf16[1,512,2,128]{3,2,1,0:T(2,128)(2,1)S(1)}, u32[]{:S(2)}, u32[]{:S(2)}) collective-permute-start(bf16[1,512,2,128]{3,2,1,0:T(2,128)(2,1)} %get-tuple-element.9), channel_id=1, source_target_pairs={{0,8},{8,16},{16,24},{24,32},{32,40},{40,48},{48,56},{1,9},{9,17},... | collective-permute-start | bytes 786440 | tf_op jit(solution)/shard_map/ppermute | solution.py:22
  252.7 14.8 %collective-permute-start.3 = (bf16[1,512,2,128]{3,2,1,0:T(2,128)(2,1)}, bf16[1,512,2,128]{3,2,1,0:T(2,128)(2,1)S(1)}, u32[]{:S(2)}, u32[]{:S(2)}) collective-permute-start(bf16[1,512,2,128]{3,2,1,0:T(2,128)(2,1)} %get-tuple-element.7), channel_id=1, source_target_pairs={{8,0},{16,8},{24,16},{32,24},{40,32},{48,40},{56,48},{9,1},{17,9},... | collective-permute-start | bytes 786440 | tf_op jit(solution)/shard_map/ppermute | solution.py:24
  254.0 13.8 %collective-permute-start.4 = (bf16[1,512,2,128]{3,2,1,0:T(2,128)(2,1)}, bf16[1,512,2,128]{3,2,1,0:T(2,128)(2,1)S(1)}, u32[]{:S(2)}, u32[]{:S(2)}) collective-permute-start(bf16[1,512,2,128]{3,2,1,0:T(2,128)(2,1)} %get-tuple-element.8), channel_id=1, source_target_pairs={{0,1},{1,2},{2,3},{3,4},{4,5},{5,6},{6,7},{8,9},{9,10},{10,11},{11... | collective-permute-start | bytes 786440 | tf_op jit(solution)/shard_map/ppermute | solution.py:22
  262.7 7.7 %collective-permute-start.5 = (bf16[1,512,2,128]{3,2,1,0:T(2,128)(2,1)S(1)}, bf16[1,512,2,128]{3,2,1,0:T(2,128)(2,1)S(1)}, u32[]{:S(2)}, u32[]{:S(2)}) collective-permute-start(bf16[1,512,2,128]{3,2,1,0:T(2,128)(2,1)S(1)} %get-tuple-element.5), channel_id=1, source_target_pairs={{1,0},{2,1},{3,2},{4,3},{5,4},{6,5},{7,6},{9,8},{10,9},{11,10},{12... | collective-permute-start | bytes 786440 | tf_op jit(solution)/shard_map/ppermute | solution.py:24
Sparse Core Ops, SparseCore 0:
  11.9 69.3 all-reduce.2
  85.6 146.1 all-reduce.4
where the time goes:
time: 292 us; the launch traced here: 290 us
  waiting for transfers between devices  207 us (71%)
  matrix products  35.3 us (12%)
  starting transfers between devices  18.7 us (6%)
  between operations  13.6 us (5%)
  local copies, waits for them, and re-layouts  10.7 us (4%)
  other arithmetic  4.44 us (2%)
    psum x1, waiting for transfers between devices, per_device(): lax.psum(jnp.dot(group_res, restrict, precision=exact_prec), ('gx', 'gy'))  135 us
    psum x1, waiting for transfers between devices, per_device(): group_res = lax.psum(assembled, 'gz')  69.5 us
    ppermute x3, starting transfers between devices, with_halo(): lax.ppermute(tail, axis, [(i, (i + 1) % count) for i in range(ends)])  14.1 us
    dot_general x1, matrix products, per_device(): jnp.einsum('rfkw,fbk->rfbw', shared, slot_onehot.astype(jnp.float32), pre...  7.32 us
    dot_general x1, matrix products, per_device(): jnp.dot(res_rows, schur_block, preferred_element_type=jnp.float32)  6.72 us
  transfers between devices with their start and end apart: 8, of which 3 were waited for; matrix products, arithmetic and copies ran while one was open for 5% of the time, Pallas kernels for 0%

commit v1 on v0

v1 whole, which is shorter than its diff:
```python
import functools

import jax
import jax.numpy as jnp
from jax import lax
from jax.experimental import pallas as pl
from jax.experimental.pallas import tpu as pltpu
from jax.sharding import PartitionSpec as P

BW = 128
FACE = 256
FACES = 6
NI = 1536
NC = 128
C2 = 512
R = 512
SX, SY, SZ = 4, 8, 8
RX = R // (SX * SZ)
RZ = R // SZ
TAIL = 16
PACK = RZ + TAIL
BASE = 16

LAST = (((1,), (1,)), ((), ()))
FIRST = (((0,), (0,)), ((), ()))
f32 = jnp.float32
bf16 = jnp.bfloat16


def mm(a, b):
    return jnp.dot(a, b, preferred_element_type=f32)


def split(x):
    hi = x.astype(bf16)
    return hi, (x - hi.astype(f32)).astype(bf16)


def mm3(a, b):
    a_hi, a_lo = split(a)
    b_hi, b_lo = split(b)
    return mm(a_hi, b_hi) + (mm(a_hi, b_lo) + mm(a_lo, b_hi))


def swap_halves(x, swap):
    return jnp.where(swap, jnp.concatenate([x[:, BW:], x[:, :BW]], axis=1), x)


def call(body, out_shape, flops, size, vmem=24, **kw):
    return pl.pallas_call(
        body,
        out_shape=out_shape,
        cost_estimate=pl.CostEstimate(flops=flops, bytes_accessed=size, transcendentals=0),
        compiler_params=pltpu.CompilerParams(vmem_limit_bytes=vmem << 20),
        **kw,
    )


def whole(shape):
    return pl.BlockSpec(shape, lambda *_: (0,) * len(shape))


SMEM = pl.BlockSpec(memory_space=pltpu.SMEM)
VMEM = pl.BlockSpec(memory_space=pltpu.VMEM)


def coarse_body(idx_ref, res_ref, basis_ref, out_ref):
    step = pl.program_id(0)
    part = lax.dot_general(res_ref[...], basis_ref[...], LAST, preferred_element_type=f32)
    start = pl.multiple_of(step * RX, RX)
    out_ref[:, pl.ds(start, RX), :] = part.astype(bf16).reshape(SZ, RX, NC)

    @pl.when(step == 0)
    def _():
        idx = idx_ref[...]
        row = lax.broadcasted_iota(jnp.int32, (TAIL, NC), 0)
        digits = jnp.where(row == 0, idx >> 4, jnp.where(row == 1, idx & (BASE - 1), 0))
        digits = digits.astype(f32).astype(bf16)
        out_ref[:, RZ:, :] = jnp.broadcast_to(digits[None], (SZ, TAIL, NC))


def coarse_kernel(idx, res, basis):
    return call(
        coarse_body,
        jax.ShapeDtypeStruct((SZ, PACK, NC), bf16),
        2 * R * NI * NC,
        2 * R * NI + 2 * NC * NI,
        grid=(SX,),
        in_specs=[
            whole((1, NC)),
            pl.BlockSpec((R // SX, NI), lambda i: (i, 0)),
            whole((NC, NI)),
        ],
        out_specs=whole((SZ, PACK, NC)),
    )(idx, res, basis)


def local_body(res_ref, schur_ref, out_ref):
    out_ref[...] = mm(res_ref[...], schur_ref[...])


def local_kernel(res, schur):
    return call(
        local_body,
        jax.ShapeDtypeStruct((R, NI), f32),
        2 * R * NI * NI,
        2 * R * NI + 2 * NI * NI + 4 * R * NI,
        grid=(FACES,),
        in_specs=[whole((R, NI)), pl.BlockSpec((NI, FACE), lambda i: (0, i))],
        out_specs=pl.BlockSpec((R, FACE), lambda i: (0, i)),
    )(res, schur)


def member_onehot(pack_ref):
    digits = pack_ref[:, RZ:, :].astype(f32)
    column = lax.broadcasted_iota(jnp.int32, (C2, NC), 0).astype(f32)
    parts = []
    for c in range(SZ):
        idx = digits[c, 0:1, :] * float(BASE) + digits[c, 1:2, :]
        parts.append((column == idx).astype(bf16))
    return jnp.concatenate(parts, axis=1)


def group_body(pack_ref, restrict_ref, res_ref, top_ref):
    onehot = member_onehot(pack_ref)
    rows = jnp.concatenate([pack_ref[c, :RZ, :] for c in range(SZ)], axis=1)
    group_res = lax.dot_general(rows, onehot, LAST, preferred_element_type=f32)
    res_ref[...] = group_res
    top_ref[...] = mm3(group_res, restrict_ref[...]).astype(bf16).reshape(SX, RX, C2)


def group_kernel(pack, restrict):
    return call(
        group_body,
        (jax.ShapeDtypeStruct((RZ, C2), f32), jax.ShapeDtypeStruct((SX, RX, C2), bf16)),
        2 * RZ * C2 * (1024 + 3 * C2),
        4 * C2 * C2,
        in_specs=[VMEM] * 2,
        out_specs=(VMEM, VMEM),
    )(pack, restrict)


def back_body(pack_ref, res_ref, inv_ref, out_ref):
    onehot = member_onehot(pack_ref)
    sol = mm3(res_ref[...], inv_ref[...]).astype(bf16)
    picked = mm(sol, onehot).astype(bf16)
    for c in range(SZ):
        out_ref[c] = picked[:, c * NC : (c + 1) * NC]


def back_kernel(pack, group_res, group_inv):
    return call(
        back_body,
        jax.ShapeDtypeStruct((SZ, RZ, NC), bf16),
        2 * RZ * C2 * (1024 + 3 * C2),
        4 * C2 * C2,
        in_specs=[VMEM] * 3,
        out_specs=VMEM,
    )(pack, group_res, group_inv)


def fan_body(copies, in_ref, out_ref):
    total = jnp.sum(in_ref[...].astype(f32), axis=0).astype(bf16)
    out_ref[...] = jnp.broadcast_to(total[None], (copies,) + total.shape)


def fan_kernel(x, copies):
    n, rows, width = x.shape
    return call(
        functools.partial(fan_body, copies),
        jax.ShapeDtypeStruct((copies, rows, width), bf16),
        n * rows * width,
        2 * (n + copies) * rows * width,
        in_specs=[VMEM],
        out_specs=VMEM,
    )(x)


def face_body(slot_ref, idx_ref, back_ref, basis_ref, local_ref, restrict_ref, own_a_ref, own_k_ref, *rest):
    sends, rows_ref = rest[:FACES], rest[FACES]
    for c in range(SZ):
        for a in range(SX):
            start = (a * SZ + c) * RX
            rows_ref[start : start + RX, :] = back_ref[c, a * RX : (a + 1) * RX, :]
    rows = rows_ref[...]
    column = lax.broadcasted_iota(jnp.int32, (C2, NC), 0)
    onehot = (column == idx_ref[...]).astype(bf16)
    r_hi, r_lo = split(restrict_ref[...])
    m_hi = lax.dot_general(r_hi, onehot, FIRST, preferred_element_type=f32).astype(bf16)
    m_lo = lax.dot_general(r_lo, onehot, FIRST, preferred_element_type=f32).astype(bf16)
    for f in range(FACES):
        cols = slice(f * FACE, (f + 1) * FACE)
        swap = slot_ref[0, 2 * f] == 1
        basis = basis_ref[:, cols]
        own_a = local_ref[:, cols] + mm(rows, basis)
        own_k = (mm(m_hi, basis) + mm(m_lo, basis)).astype(bf16)
        own_a_ref[:, cols] = own_a
        own_k_ref[:, cols] = own_k
        sends[f][:C2, :] = swap_halves(own_k.astype(f32), swap).astype(bf16)
        sends[f][C2:, :] = swap_halves(own_a, swap).astype(bf16)


def face_kernel(slots, idx, back, basis, local, restrict):
    return call(
        face_body,
        (
            jax.ShapeDtypeStruct((R, NI), f32),
            jax.ShapeDtypeStruct((C2, NI), bf16),
        )
        + (jax.ShapeDtypeStruct((C2 + R, FACE), bf16),) * FACES,
        2 * R * NC * NI * 3,
        8 * R * NI,
        in_specs=[SMEM] + [VMEM] * 5,
        out_specs=(VMEM,) * (2 + FACES),
        scratch_shapes=[pltpu.VMEM((R, NC), bf16)],
    )(slots, idx, back, basis, local, restrict)


def blend_body(slot_ref, weight_ref, a_ref, k_ref, inv_ref, *rest):
    gots, out_a_ref, out_w_ref = rest[:FACES], rest[FACES], rest[FACES + 1]
    i_hi, i_lo = split(inv_ref[...])
    for f in range(FACES):
        cols = slice(f * FACE, (f + 1) * FACE)
        swap = slot_ref[0, 2 * f] == 1
        weight = weight_ref[0, f]
        got_k = swap_halves(gots[f][:C2, :].astype(f32), swap)
        got_a = swap_halves(gots[f][C2:, :].astype(f32), swap)
        k = (weight * (k_ref[:, cols].astype(f32) + got_k)).astype(bf16)
        out_a_ref[:, cols] = weight * (a_ref[:, cols] + got_a)
        out_w_ref[:, cols] = (mm(i_hi, k) + mm(i_lo, k)).astype(bf16)


def blend_kernel(slots, weights, own_a, own_k, inv, gots):
    return call(
        blend_body,
        (jax.ShapeDtypeStruct((R, NI), f32), jax.ShapeDtypeStruct((C2, NI), bf16)),
        2 * C2 * C2 * NI * 2,
        12 * R * NI,
        vmem=32,
        in_specs=[SMEM] * 2 + [VMEM] * (3 + FACES),
        out_specs=(VMEM, VMEM),
    )(slots, weights, own_a, own_k, inv, *gots)


def last_body(top_ref, w_ref, a_ref, out_ref):
    out_ref[...] = (a_ref[...] + mm(top_ref[...], w_ref[...])).astype(bf16)


def last_kernel(top, w, a):
    rows = 128
    return call(
        last_body,
        jax.ShapeDtypeStruct((R, NI), bf16),
        2 * R * C2 * NI,
        8 * R * NI,
        grid=(R // rows,),
        in_specs=[
            pl.BlockSpec((rows, C2), lambda i: (i, 0)),
            whole((C2, NI)),
            pl.BlockSpec((rows, NI), lambda i: (i, 0)),
        ],
        out_specs=pl.BlockSpec((rows, NI), lambda i: (i, 0)),
    )(top, w, a)


def per_device(
    residual,
    schur_inverse,
    coarse_basis,
    coarse_index,
    block_slot,
    group_inverse,
    group_restrict,
    top_inverse,
):
    res = residual[0, 0, 0]
    schur = schur_inverse[0, 0, 0]
    basis = coarse_basis[0, 0, 0]
    idx = coarse_index.reshape(1, NC)
    slots = block_slot.reshape(1, 2 * FACES)
    group_inv = group_inverse[0, 0]
    restrict = group_restrict[0, 0]

    pack = coarse_kernel(idx, res, basis)
    pack = lax.all_to_all(pack, "gz", 0, 0)
    local = local_kernel(res, schur)
    group_res, part = group_kernel(pack, restrict)
    part = lax.all_to_all(part, "gx", 0, 0)
    back = back_kernel(pack, group_res, group_inv)
    back = lax.all_to_all(back, "gz", 0, 0)
    part = lax.all_to_all(fan_kernel(part, SY), "gy", 0, 0)
    own_a, own_k, *sends = face_kernel(slots, idx, back, basis, local, restrict)
    top = lax.all_to_all(fan_kernel(part, SX * SZ), ("gx", "gz"), 0, 0).reshape(R, C2)

    gots, weights = [], []
    for axis, count, f in (("gx", SX, 0), ("gy", SY, 2), ("gz", SZ, 4)):
        up = [(i, i + 1) for i in range(count - 1)]
        down = [(i + 1, i) for i in range(count - 1)]
        place = lax.axis_index(axis)
        gots.append(lax.ppermute(sends[f + 1], axis, up))
        gots.append(lax.ppermute(sends[f], axis, down))
        weights.append(jnp.where(place > 0, 0.5, 1.0).astype(f32))
        weights.append(jnp.where(place < count - 1, 0.5, 1.0).astype(f32))
    weights = jnp.stack(weights).reshape(1, FACES)
    a, w = blend_kernel(slots, weights, own_a, own_k, top_inverse, gots)
    return last_kernel(top, w, a).reshape(1, 1, 1, R, NI)


def solution(mesh):
    return jax.shard_map(
        per_device,
        mesh=mesh,
        in_specs=(
            P("gx", "gy", "gz", None, None),
            P("gx", "gy", "gz", None, None),
            P("gx", "gy", "gz", None, None),
            P("gx", "gy", "gz", None),
            P("gx", "gy", "gz", None),
            P("gx", "gy", None, None),
            P("gx", "gy", None, None),
            P(),
        ),
        out_specs=P("gx", "gy", "gz", None, None),
        check_vma=False,
    )
```

time: 292 us -> 117 us (0.40)
  waiting for transfers between devices: 207 us -> 0.02 us
  matrix products: 35.3 us -> 0 us
  blocking collectives: 0 us -> 26.3 us
  local copies, waits for them, and re-layouts: 10.7 us -> 33.3 us
  Pallas kernels: 0 us -> 19.3 us
  starting transfers between devices: 18.7 us -> 36.5 us
  between operations: 13.6 us -> 0.24 us
  other arithmetic: 4.44 us -> 0 us
    psum x2 -> x0, waiting for transfers between devices: 205 us -> none  [the longest x1 135 us: per_device(): lax.psum(jnp.dot(group_res, restrict, precision=exact_prec), ('gx', 'gy'))]
    dot_general x11 -> x0, matrix products: 35.3 us -> none  [the longest x1 7.32 us: per_device(): jnp.einsum('rfkw,fbk->rfbw', shared, slot_onehot.astype(jnp.float32), pre...]
    unnamed x19 -> x74, local copies, waits for them, and re-layouts: 1.95 us -> 33.2 us
    all_to_all x0 -> x2, blocking collectives: none -> 26.3 us  [the longest x1 14.9 us: per_device(): part = lax.all_to_all(part, 'gx', 0, 0)]
    all_to_all x0 -> x3, starting transfers between devices: none -> 20.2 us  [the longest x1 8.18 us: per_device(): part = lax.all_to_all(fan_kernel(part, SY), 'gy', 0, 0)]
    pallas_call x0 -> x9, Pallas kernels: none -> 19.3 us  [the longest x1 4.08 us: last_kernel(): call(last_body, jax.ShapeDtypeStruct((R, NI), bf16), 2 * R * C2 * NI, 8 *...]
    convert_element_type x2 -> x0, local copies, waits for them, and re-layouts: 5.15 us -> none  [per_device(): return placed.reshape(1, 1, 1, rhs_count, NI).astype(jnp.bfloat16)]
    unnamed x6 -> x0, other arithmetic: 4.12 us -> none
  transfers between devices with their start and end apart: 8 -> 9, of which waited for: 3 -> 0; matrix products, arithmetic and copies ran while one was open for 5% -> 0% of each run, Pallas kernels for 0% -> 8%
where the time goes in v1:
time: 117 us; the launch traced here: 116 us
  starting transfers between devices  36.5 us (31%)
  local copies, waits for them, and re-layouts  33.3 us (28%)
  blocking collectives  26.3 us (22%)
  Pallas kernels  19.3 us (16%)
    unnamed x74, local copies, waits for them, and re-layouts  33.2 us
    all_to_all x1, blocking collectives, per_device(): part = lax.all_to_all(part, 'gx', 0, 0)  14.9 us
    ppermute x3, starting transfers between devices, per_device(): gots.append(lax.ppermute(sends[f + 1], axis, up))  11.8 us
    all_to_all x1, blocking collectives, per_device(): pack = lax.all_to_all(pack, 'gz', 0, 0)  11.3 us
    all_to_all x1, starting transfers between devices, per_device(): part = lax.all_to_all(fan_kernel(part, SY), 'gy', 0, 0)  8.18 us
    all_to_all x1, starting transfers between devices, per_device(): lax.all_to_all(fan_kernel(part, SX * SZ), ('gx', 'gz'), 0, 0).reshape(R, C2)  7.21 us
    all_to_all x1, starting transfers between devices, per_device(): back = lax.all_to_all(back, 'gz', 0, 0)  4.78 us
    ppermute x3, starting transfers between devices, per_device(): gots.append(lax.ppermute(sends[f], axis, down))  4.49 us
  transfers between devices with their start and end apart: 9, of which 0 were waited for; matrix products, arithmetic and copies ran while one was open for 0% of the time, Pallas kernels for 8%

profile of v1, /device:TPU:1, one launch (start us, length us, event | category | flops | bytes accessed | tf_op | source)
XLA Modules:
  0.0 115.5 jit_solution(7844754279530254815)
XLA Ops:
  0.0 1.4 %copy-done = bf16[1,1,1,512,1536]{4,3,2,1,0:T(8,128)(2,1)S(1)} copy-done((bf16[1,1,1,512,1536]{4,3,2,1,0:T(8,128)(2,1)S(1)}, bf16[1,1,1,512,1536]{4,3,2,1,0:T(8,128)(2,1)}, u32[]{:S(2)}) %copy-start) | copy-done | bytes 1572888
  1.4 1.0 copy-done.9
  2.4 0.7 copy-done.29
  3.1 1.1 shard_map.82
  4.2 11.3 %all_to_all.25.pack_ref = bf16[8,80,128]{2,1,0:T(8,128)(2,1)S(1)} all-to-all(bf16[8,80,128]{2,1,0:T(8,128)(2,1)S(1)} %shard_map.82), channel_id=1, replica_groups=mesh['gx'=4,'gy'=8,'gz'=8] {'gz'}, dimensions={0} | all-to-all | bytes 327680 | tf_op jit(solution)/shard_map/all_to_all | solution.py:285
  15.5 1.2 %copy-done.3 = f32[1,1,512,512]{3,2,1,0:T(8,128)S(1)} copy-done((f32[1,1,512,512]{3,2,1,0:T(8,128)S(1)}, f32[1,1,512,512]{3,2,1,0:T(8,128)}, u32[]{:S(2)}) %copy-start.3) | copy-done | bytes 1048600
  16.7 0.8 shard_map.83
  17.5 0.0 copy-start.27
  17.6 0.6 copy-done.27
  18.2 1.3 %shard_map.86 = bf16[8,64,128]{2,1,0:T(8,128)(2,1)} custom-call(bf16[8,80,128]{2,1,0:T(8,128)(2,1)S(1)} %all_to_all.25.pack_ref, f32[64,512]{1,0:T(8,128)S(1)} %get-tuple-element.18.res_ref, f32[512,512]{1,0:T(8,128)S(1)} %bitcast.23), custom_call_target="tpu_custom_call" | custom-call | flops 167772160 | bytes 1048576 | tf_op jit(solution)/shard_map/pallas_call | solution.py:152
  19.5 4.8 %all-to-all-start.4 = ((bf16[8,64,128]{2,1,0:T(8,128)(2,1)}), bf16[8,64,128]{2,1,0:T(8,128)(2,1)}, u32[]{:S(2)}, u32[]{:S(2)}) async-start(bf16[8,64,128]{2,1,0:T(8,128)(2,1)} %shard_map.86), calls=%async_computation.4 | async-start | bytes 262144 | tf_op jit(solution)/shard_map/all_to_all | solution.py:290
  24.3 1.4 %copy-done.1 = bf16[1,1,1,512,1536]{4,3,2,1,0:T(8,128)(2,1)S(1)} copy-done((bf16[1,1,1,512,1536]{4,3,2,1,0:T(8,128)(2,1)S(1)}, bf16[1,1,1,512,1536]{4,3,2,1,0:T(8,128)(2,1)}, u32[]{:S(2)}) %copy-start.1) | copy-done | bytes 1572888
  25.7 2.3 %copy-done.2 = bf16[1,1,1,1536,1536]{4,3,2,1,0:T(8,128)(2,1)S(1)} copy-done((bf16[1,1,1,1536,1536]{4,3,2,1,0:T(8,128)(2,1)S(1)}, bf16[1,1,1,1536,1536]{4,3,2,1,0:T(8,128)(2,1)}, u32[]{:S(2)}) %copy-start.2) | copy-done | bytes 4718616
  28.0 4.0 %shard_map.87.local_ref = f32[512,1536]{1,0:T(8,128)S(1)} custom-call(bf16[512,1536]{1,0:T(8,128)(2,1)S(1)} %bitcast.17, bf16[1536,1536]{1,0:T(8,128)(2,1)S(1)} %bitcast.18), custom_call_target="tpu_custom_call" | custom-call | flops 2415919104 | bytes 9437184 | tf_op jit(solution)/shard_map/pallas_call | solution.py:103
  32.0 0.0 all-to-all-done.4.back_ref
  32.1 0.0 copy-start.4
  32.1 1.2 %copy-done.4 = f32[1,1,512,512]{3,2,1,0:T(8,128)S(1)} copy-done((f32[1,1,512,512]{3,2,1,0:T(8,128)S(1)}, f32[1,1,512,512]{3,2,1,0:T(8,128)}, u32[]{:S(2)}) %copy-start.4) | copy-done | bytes 1048600
  33.3 3.1 %shard_map.88 = (f32[512,1536]{1,0:T(8,128)S(1)}, bf16[512,1536]{1,0:T(8,128)(2,1)S(1)}, bf16[1024,256]{1,0:T(8,128)(2,1)S(1)}, bf16[1024,256]{1,0:T(8,128)(2,1)...) custom-call(s32[1,12]{1,0:T(1,128)S(1)} %bitcast.26, ...), custom_call_target="tpu_custom_call" | custom-call | flops 603979776 | bytes 6291456 | tf_op jit(solution)/shard_map/pallas_call | solution.py:204
  36.4 1.6 %copy-done.5 = f32[512,1536]{1,0:T(8,128)} copy-done((f32[512,1536]{1,0:T(8,128)}, f32[512,1536]{1,0:T(8,128)S(1)}, u32[]{:S(2)}) %copy-start.5) | copy-done | bytes 3145752
  38.0 1.1 copy-done.7
  39.2 0.8 copy-done.33
  40.0 0.8 copy-done.34
  40.8 0.8 copy-done.35
  41.6 0.8 copy-done.36
  42.4 3.1 %collective-permute-start = (bf16[1024,256]{1,0:T(8,128)(2,1)}, bf16[1024,256]{1,0:T(8,128)(2,1)S(1)}, u32[]{:S(2)}, u32[]{:S(2)}) collective-permute-start(bf16[1024,256]{1,0:T(8,128)(2,1)} %get-tuple-element.21), channel_id=1, source_target_pairs={{0,64},{64,128},{128,192},{1,65},{65,129},{129,193},{2,66},{66,130... | collective-permute-start | bytes 1572872 | tf_op jit(solution)/shard_map/ppermute | solution.py:300
  45.5 14.9 %all_to_all.26.in_ref = bf16[4,16,512]{2,1,0:T(8,128)(2,1)S(1)} all-to-all(bf16[4,16,512]{2,1,0:T(8,128)(2,1)S(1)} %copy-done.28), channel_id=1, replica_groups=mesh['gx'=4,'gy'=8,'gz'=8] {'gx'}, dimensions={0} | all-to-all | bytes 131072 | tf_op jit(solution)/shard_map/all_to_all | solution.py:288
  60.5 0.0 copy-done.32
  60.5 0.7 shard_map.84
  61.1 8.2 %all-to-all-start.2 = ((bf16[8,16,512]{2,1,0:T(8,128)(2,1)}), bf16[8,16,512]{2,1,0:T(8,128)(2,1)S(1)}, u32[]{:S(2)}, u32[]{:S(2)}) async-start(bf16[8,16,512]{2,1,0:T(8,128)(2,1)} %shard_map.84), calls=%async_computation.2 | async-start | bytes 262144 | tf_op jit(solution)/shard_map/all_to_all | solution.py:291
  69.3 1.3 %collective-permute-start.1 = (bf16[1024,256]{1,0:T(8,128)(2,1)}, bf16[1024,256]{1,0:T(8,128)(2,1)S(1)}, u32[]{:S(2)}, u32[]{:S(2)}) collective-permute-start(bf16[1024,256]{1,0:T(8,128)(2,1)} %copy-done.36), channel_id=1, source_target_pairs={{64,0},{128,64},{192,128},{65,1},{129,65},{193,129},{66,2},{130,66... | collective-permute-start | bytes 1572872 | tf_op jit(solution)/shard_map/ppermute | solution.py:301
  70.6 3.4 %collective-permute-start.2 = (bf16[1024,256]{1,0:T(8,128)(2,1)}, bf16[1024,256]{1,0:T(8,128)(2,1)S(1)}, u32[]{:S(2)}, u32[]{:S(2)}) collective-permute-start(bf16[1024,256]{1,0:T(8,128)(2,1)} %copy-done.35), channel_id=1, source_target_pairs={{0,8},{8,16},{16,24},{24,32},{32,40},{40,48},{48,56},{1,9},{9,17},... | collective-permute-start | bytes 1572872 | tf_op jit(solution)/shard_map/ppermute | solution.py:300
  74.0 1.3 %collective-permute-start.3 = (bf16[1024,256]{1,0:T(8,128)(2,1)}, bf16[1024,256]{1,0:T(8,128)(2,1)S(1)}, u32[]{:S(2)}, u32[]{:S(2)}) collective-permute-start(bf16[1024,256]{1,0:T(8,128)(2,1)} %copy-done.34), channel_id=1, source_target_pairs={{8,0},{16,8},{24,16},{32,24},{40,32},{48,40},{56,48},{9,1},{17,9},... | collective-permute-start | bytes 1572872 | tf_op jit(solution)/shard_map/ppermute | solution.py:301
  75.3 5.3 %collective-permute-start.4 = (bf16[1024,256]{1,0:T(8,128)(2,1)}, bf16[1024,256]{1,0:T(8,128)(2,1)S(1)}, u32[]{:S(2)}, u32[]{:S(2)}) collective-permute-start(bf16[1024,256]{1,0:T(8,128)(2,1)} %copy-done.33), channel_id=1, source_target_pairs={{0,1},{1,2},{2,3},{3,4},{4,5},{5,6},{6,7},{8,9},{9,10},{10,11},{11... | collective-permute-start | bytes 1572872 | tf_op jit(solution)/shard_map/ppermute | solution.py:300
  80.6 0.0 collective-permute-done.rest_0_
  80.6 1.9 %collective-permute-start.5 = (bf16[1024,256]{1,0:T(8,128)(2,1)}, bf16[1024,256]{1,0:T(8,128)(2,1)S(1)}, u32[]{:S(2)}, u32[]{:S(2)}) collective-permute-start(bf16[1024,256]{1,0:T(8,128)(2,1)} %copy-done.32), channel_id=1, source_target_pairs={{1,0},{2,1},{3,2},{4,3},{5,4},{6,5},{7,6},{9,8},{10,9},{11,10},{12... | collective-permute-start | bytes 1572872 | tf_op jit(solution)/shard_map/ppermute | solution.py:301
  82.5 0.0 all-to-all-done.2.in_ref
  82.5 0.9 shard_map.85
  83.4 7.2 %all-to-all-start.3 = ((bf16[32,16,512]{2,1,0:T(8,128)(2,1)}), bf16[32,16,512]{2,1,0:T(8,128)(2,1)}, u32[]{:S(2)}, u32[]{:S(2)}) async-start(bf16[32,16,512]{2,1,0:T(8,128)(2,1)} %shard_map.85), calls=%async_computation.3 | async-start | bytes 1048576 | tf_op jit(solution)/shard_map/all_to_all | solution.py:293
  90.7 0.1 stack.27
  90.7 0.0 collective-permute-done.1.rest_1_
  90.7 0.8 copy-done.17
  91.5 0.0 collective-permute-done.2.rest_2_
  91.6 0.8 copy-done.19
  92.3 0.0 collective-permute-done.3.rest_3_
  92.3 0.8 copy-done.21
  93.1 0.0 collective-permute-done.4.rest_4_
  93.2 0.8 copy-done.23
  94.0 0.0 collective-permute-done.5.rest_5_
  94.0 0.8 copy-done.25
  94.8 1.9 %copy-done.6 = f32[512,1536]{1,0:T(8,128)S(1)} copy-done((f32[512,1536]{1,0:T(8,128)S(1)}, f32[512,1536]{1,0:T(8,128)}, u32[]{:S(2)}) %copy-start.6) | copy-done | bytes 3145752
  96.7 1.4 %copy-done.8 = bf16[512,1536]{1,0:T(8,128)(2,1)S(1)} copy-done((bf16[512,1536]{1,0:T(8,128)(2,1)S(1)}, bf16[512,1536]{1,0:T(8,128)(2,1)}, u32[]{:S(2)}) %copy-start.8) | copy-done | bytes 1572888
  98.1 1.2 %copy-done.13 = f32[512,512]{1,0:T(8,128)S(1)} copy-done((f32[512,512]{1,0:T(8,128)S(1)}, f32[512,512]{1,0:T(8,128)}, u32[]{:S(2)}) %copy-start.13) | copy-done | bytes 1048600
  99.3 1.0 copy-done.16
  100.4 1.0 copy-done.18
  101.4 1.0 copy-done.20
  102.4 1.0 copy-done.22
  103.5 1.0 copy-done.24
  104.5 1.0 copy-done.26
  105.6 3.3 %shard_map.89 = (f32[512,1536]{1,0:T(8,128)S(1)}, bf16[512,1536]{1,0:T(8,128)(2,1)S(1)}) custom-call(s32[1,12]{1,0:T(1,128)S(1)} %bitcast.27, f32[1,6]{1,0:T(1,128)S(1)} %bitcast.28, f32[512,1536]{1,0:T(8,128)S(1)} %copy-done.6, bf16[512,1536]{1,0:T(8,128)(2,1)S(1)} %copy-done.8, f32[512,512]{1,0:T(8,128)S(1)} %copy-done.13, ...), custom_call_target="tpu_custom_call" | custom-call | flops 1610612736 | bytes 9437184 | tf_op jit(solution)/shard_map/pallas_call | solution.py:234
  108.9 0.0 copy-start.11
  108.9 1.1 copy-done.11
  110.0 0.0 all-to-all-done.3
  110.0 1.4 %copy-done.12 = bf16[512,1536]{1,0:T(8,128)(2,1)S(1)} copy-done((bf16[512,1536]{1,0:T(8,128)(2,1)S(1)}, bf16[512,1536]{1,0:T(8,128)(2,1)}, u32[]{:S(2)}) %copy-start.12) | copy-done | bytes 1572888
  111.4 4.1 %shard_map.90 = bf16[512,1536]{1,0:T(8,128)(2,1)} custom-call(bf16[512,512]{1,0:T(8,128)(2,1)} %bitcast.4.top_ref, bf16[512,1536]{1,0:T(8,128)(2,1)S(1)} %copy-done.12, f32[512,1536]{1,0:T(8,128)S(1)} %get-tuple-element.28.a_ref), custom_call_target="tpu_custom_call" | custom-call | flops 805306368 | bytes 6291456 | tf_op jit(solution)/shard_map/pallas_call | solution.py:251
  (40 shorter events, 0.1 us)
Async XLA Ops:
  0.0 1.4 %copy-start = (bf16[1,1,1,512,1536]{4,3,2,1,0:T(8,128)(2,1)S(1)}, bf16[1,1,1,512,1536]{4,3,2,1,0:T(8,128)(2,1)}, u32[]{:S(2)}) copy-start(bf16[1,1,1,512,1536]{4,3,2,1,0:T(8,128)(2,1)} %param.8) | copy-start | bytes 4718596
  1.4 1.0 copy-start.9
  2.4 0.7 copy-start.29
  3.1 15.1 %copy-start.14 = (f32[1,1,512,512]{3,2,1,0:T(8,128)S(1)}, f32[1,1,512,512]{3,2,1,0:T(8,128)}, u32[]{:S(2)}) copy-start(f32[1,1,512,512]{3,2,1,0:T(8,128)} %param.13) | copy-start | bytes 3145732
  15.5 1.2 %copy-start.3 = (f32[1,1,512,512]{3,2,1,0:T(8,128)S(1)}, f32[1,1,512,512]{3,2,1,0:T(8,128)}, u32[]{:S(2)}) copy-start(f32[1,1,512,512]{3,2,1,0:T(8,128)} %param.14) | copy-start | bytes 3145732
  17.5 0.6 copy-start.27
  19.5 12.5 %all-to-all-start.4 = ((bf16[8,64,128]{2,1,0:T(8,128)(2,1)}), bf16[8,64,128]{2,1,0:T(8,128)(2,1)}, u32[]{:S(2)}, u32[]{:S(2)}) async-start(bf16[8,64,128]{2,1,0:T(8,128)(2,1)} %shard_map.86), calls=%async_computation.4 | async-start | bytes 262144 | tf_op jit(solution)/shard_map/all_to_all | solution.py:290
  24.3 1.4 %copy-start.1 = (bf16[1,1,1,512,1536]{4,3,2,1,0:T(8,128)(2,1)S(1)}, bf16[1,1,1,512,1536]{4,3,2,1,0:T(8,128)(2,1)}, u32[]{:S(2)}) copy-start(bf16[1,1,1,512,1536]{4,3,2,1,0:T(8,128)(2,1)} %param.8) | copy-start | bytes 4718596
  25.7 2.3 %copy-start.2 = (bf16[1,1,1,1536,1536]{4,3,2,1,0:T(8,128)(2,1)S(1)}, bf16[1,1,1,1536,1536]{4,3,2,1,0:T(8,128)(2,1)}, u32[]{:S(2)}) copy-start(bf16[1,1,1,1536,1536]{4,3,2,1,0:T(8,128)(2,1)} %param.9) | copy-start | bytes 14155780
  28.0 4.0 %copy-start.10 = (bf16[1,1,1,128,1536]{4,3,2,1,0:T(8,128)(2,1)S(1)}, bf16[1,1,1,128,1536]{4,3,2,1,0:T(8,128)(2,1)}, u32[]{:S(2)}) copy-start(bf16[1,1,1,128,1536]{4,3,2,1,0:T(8,128)(2,1)} %param.10) | copy-start | bytes 1179652
  28.0 4.0 %copy-start.30 = (s32[1,1,1,128]{3,2,1,0:T(1,128)S(1)}, s32[1,1,1,128]{3,2,1,0:T(1,128)}, u32[]{:S(2)}) copy-start(s32[1,1,1,128]{3,2,1,0:T(1,128)} %param.11) | copy-start | bytes 1540
  28.0 4.0 %copy-start.31 = (s32[1,1,1,12]{3,2,1,0:T(1,128)S(1)}, s32[1,1,1,12]{3,2,1,0:T(1,128)}, u32[]{:S(2)}) copy-start(s32[1,1,1,12]{3,2,1,0:T(1,128)} %param.12) | copy-start | bytes 148
  32.1 1.2 %copy-start.4 = (f32[1,1,512,512]{3,2,1,0:T(8,128)S(1)}, f32[1,1,512,512]{3,2,1,0:T(8,128)}, u32[]{:S(2)}) copy-start(f32[1,1,512,512]{3,2,1,0:T(8,128)} %param.14) | copy-start | bytes 3145732
  33.3 12.2 %copy-start.28 = (bf16[4,16,512]{2,1,0:T(8,128)(2,1)S(1)}, bf16[4,16,512]{2,1,0:T(8,128)(2,1)}, u32[]{:S(2)}) copy-start(bf16[4,16,512]{2,1,0:T(8,128)(2,1)} %copy-done.27) | copy-start | bytes 196612
  36.4 1.6 %copy-start.5 = (f32[512,1536]{1,0:T(8,128)}, f32[512,1536]{1,0:T(8,128)S(1)}, u32[]{:S(2)}) copy-start(f32[512,1536]{1,0:T(8,128)S(1)} %get-tuple-element.19.a_ref) | copy-start | bytes 9437188
  38.0 1.1 copy-start.7
  39.2 0.8 copy-start.33
  40.0 0.8 copy-start.34
  40.8 0.8 copy-start.35
  41.6 0.8 copy-start.36
  42.4 18.1 %copy-start.32 = (bf16[1024,256]{1,0:T(8,128)(2,1)}, bf16[1024,256]{1,0:T(8,128)(2,1)S(1)}, u32[]{:S(2)}) copy-start(bf16[1024,256]{1,0:T(8,128)(2,1)S(1)} %get-tuple-element.26) | copy-start | bytes 1572868
  42.4 38.2 %collective-permute-start = (bf16[1024,256]{1,0:T(8,128)(2,1)}, bf16[1024,256]{1,0:T(8,128)(2,1)S(1)}, u32[]{:S(2)}, u32[]{:S(2)}) collective-permute-start(bf16[1024,256]{1,0:T(8,128)(2,1)} %get-tuple-element.21), channel_id=1, source_target_pairs={{0,64},{64,128},{128,192},{1,65},{65,129},{129,193},{2,66},{66,130... | collective-permute-start | bytes 1572872 | tf_op jit(solution)/shard_map/ppermute | solution.py:300
  61.1 21.4 %all-to-all-start.2 = ((bf16[8,16,512]{2,1,0:T(8,128)(2,1)}), bf16[8,16,512]{2,1,0:T(8,128)(2,1)S(1)}, u32[]{:S(2)}, u32[]{:S(2)}) async-start(bf16[8,16,512]{2,1,0:T(8,128)(2,1)} %shard_map.84), calls=%async_computation.2 | async-start | bytes 262144 | tf_op jit(solution)/shard_map/all_to_all | solution.py:291
  69.3 21.4 %collective-permute-start.1 = (bf16[1024,256]{1,0:T(8,128)(2,1)}, bf16[1024,256]{1,0:T(8,128)(2,1)S(1)}, u32[]{:S(2)}, u32[]{:S(2)}) collective-permute-start(bf16[1024,256]{1,0:T(8,128)(2,1)} %copy-done.36), channel_id=1, source_target_pairs={{64,0},{128,64},{192,128},{65,1},{129,65},{193,129},{66,2},{130,66... | collective-permute-start | bytes 1572872 | tf_op jit(solution)/shard_map/ppermute | solution.py:301
  70.6 20.9 %collective-permute-start.2 = (bf16[1024,256]{1,0:T(8,128)(2,1)}, bf16[1024,256]{1,0:T(8,128)(2,1)S(1)}, u32[]{:S(2)}, u32[]{:S(2)}) collective-permute-start(bf16[1024,256]{1,0:T(8,128)(2,1)} %copy-done.35), channel_id=1, source_target_pairs={{0,8},{8,16},{16,24},{24,32},{32,40},{40,48},{48,56},{1,9},{9,17},... | collective-permute-start | bytes 1572872 | tf_op jit(solution)/shard_map/ppermute | solution.py:300
  74.0 18.3 %collective-permute-start.3 = (bf16[1024,256]{1,0:T(8,128)(2,1)}, bf16[1024,256]{1,0:T(8,128)(2,1)S(1)}, u32[]{:S(2)}, u32[]{:S(2)}) collective-permute-start(bf16[1024,256]{1,0:T(8,128)(2,1)} %copy-done.34), channel_id=1, source_target_pairs={{8,0},{16,8},{24,16},{32,24},{40,32},{48,40},{56,48},{9,1},{17,9},... | collective-permute-start | bytes 1572872 | tf_op jit(solution)/shard_map/ppermute | solution.py:301
  75.3 17.8 %collective-permute-start.4 = (bf16[1024,256]{1,0:T(8,128)(2,1)}, bf16[1024,256]{1,0:T(8,128)(2,1)S(1)}, u32[]{:S(2)}, u32[]{:S(2)}) collective-permute-start(bf16[1024,256]{1,0:T(8,128)(2,1)} %copy-done.33), channel_id=1, source_target_pairs={{0,1},{1,2},{2,3},{3,4},{4,5},{5,6},{6,7},{8,9},{9,10},{10,11},{11... | collective-permute-start | bytes 1572872 | tf_op jit(solution)/shard_map/ppermute | solution.py:300
  80.6 14.2 %copy-start.15 = (bf16[1024,256]{1,0:T(8,128)(2,1)}, bf16[1024,256]{1,0:T(8,128)(2,1)S(1)}, u32[]{:S(2)}) copy-start(bf16[1024,256]{1,0:T(8,128)(2,1)S(1)} %collective-permute-done.rest_0_) | copy-start | bytes 1572868
  80.6 13.3 %collective-permute-start.5 = (bf16[1024,256]{1,0:T(8,128)(2,1)}, bf16[1024,256]{1,0:T(8,128)(2,1)S(1)}, u32[]{:S(2)}, u32[]{:S(2)}) collective-permute-start(bf16[1024,256]{1,0:T(8,128)(2,1)} %copy-done.32), channel_id=1, source_target_pairs={{1,0},{2,1},{3,2},{4,3},{5,4},{6,5},{7,6},{9,8},{10,9},{11,10},{12... | collective-permute-start | bytes 1572872 | tf_op jit(solution)/shard_map/ppermute | solution.py:301
  83.4 26.6 %all-to-all-start.3 = ((bf16[32,16,512]{2,1,0:T(8,128)(2,1)}), bf16[32,16,512]{2,1,0:T(8,128)(2,1)}, u32[]{:S(2)}, u32[]{:S(2)}) async-start(bf16[32,16,512]{2,1,0:T(8,128)(2,1)} %shard_map.85), calls=%async_computation.3 | async-start | bytes 1048576 | tf_op jit(solution)/shard_map/all_to_all | solution.py:293
  90.7 0.8 copy-start.17
  91.5 0.8 copy-start.19
  92.3 0.8 copy-start.21
  93.1 0.8 copy-start.23
  94.0 0.8 copy-start.25
  94.8 1.9 %copy-start.6 = (f32[512,1536]{1,0:T(8,128)S(1)}, f32[512,1536]{1,0:T(8,128)}, u32[]{:S(2)}) copy-start(f32[512,1536]{1,0:T(8,128)} %copy-done.5) | copy-start | bytes 9437188
  96.7 1.4 %copy-start.8 = (bf16[512,1536]{1,0:T(8,128)(2,1)S(1)}, bf16[512,1536]{1,0:T(8,128)(2,1)}, u32[]{:S(2)}) copy-start(bf16[512,1536]{1,0:T(8,128)(2,1)} %copy-done.7) | copy-start | bytes 4718596
  98.1 1.2 %copy-start.13 = (f32[512,512]{1,0:T(8,128)S(1)}, f32[512,512]{1,0:T(8,128)}, u32[]{:S(2)}) copy-start(f32[512,512]{1,0:T(8,128)} %inv_ref.1) | copy-start | bytes 3145732
  99.3 1.0 copy-start.16
  100.4 1.0 copy-start.18
  101.4 1.0 copy-start.20
  102.4 1.0 copy-start.22
  103.5 1.0 copy-start.24
  104.5 1.0 copy-start.26
  108.9 1.1 copy-start.11
  110.0 1.4 %copy-start.12 = (bf16[512,1536]{1,0:T(8,128)(2,1)S(1)}, bf16[512,1536]{1,0:T(8,128)(2,1)}, u32[]{:S(2)}) copy-start(bf16[512,1536]{1,0:T(8,128)(2,1)} %copy-done.11) | copy-start | bytes 4718596

commit v2 on v1

v2 whole, which is shorter than its diff:
```python
import functools

import jax
import jax.numpy as jnp
from jax import lax
from jax.experimental import pallas as pl
from jax.experimental.pallas import tpu as pltpu
from jax.sharding import PartitionSpec as P

BW = 128
FACE = 256
FACES = 6
NI = 1536
NC = 128
C2 = 512
R = 512
SX, SY, SZ = 4, 8, 8
RX = R // (SX * SZ)
RZ = R // SZ
TAIL = 16
PACK = RZ + TAIL
BASE = 16
COST = 1024
BIG = 58
SMALL = 6
CHIPS = SZ // 2

LAST = (((1,), (1,)), ((), ()))
FIRST = (((0,), (0,)), ((), ()))
f32 = jnp.float32
bf16 = jnp.bfloat16


def mm(a, b):
    return jnp.dot(a, b, preferred_element_type=f32)


def split(x):
    hi = x.astype(bf16)
    return hi, (x - hi.astype(f32)).astype(bf16)


def mm3(a, b):
    a_hi, a_lo = split(a)
    b_hi, b_lo = split(b)
    return mm(a_hi, b_hi) + (mm(a_hi, b_lo) + mm(a_lo, b_hi))


def swap_halves(x, swap):
    return jnp.where(swap, jnp.concatenate([x[:, BW:], x[:, :BW]], axis=1), x)


def call(body, out_shape, flops, size, vmem, **kw):
    return pl.pallas_call(
        body,
        out_shape=out_shape,
        cost_estimate=pl.CostEstimate(flops=COST, bytes_accessed=COST, transcendentals=0),
        compiler_params=pltpu.CompilerParams(vmem_limit_bytes=vmem << 20),
        **kw,
    )


SMEM = pl.BlockSpec(memory_space=pltpu.SMEM)
VMEM = pl.BlockSpec(memory_space=pltpu.VMEM)
HBM = pl.BlockSpec(memory_space=pltpu.HBM)
DMA = pltpu.SemaphoreType.DMA


def started(pairs, sems):
    copies = []
    for i, (src, dst) in enumerate(pairs):
        copies.append(pltpu.make_async_copy(src, dst, sems.at[i]))
        copies[-1].start()
    return copies


def face_cols(f):
    return slice(f * FACE, (f + 1) * FACE)


def coarse_body(idx_hbm, res_hbm, basis_hbm, out_ref, res_ref, idx_ref, basis_ref, sems):
    rows = R // SX
    pairs = [(basis_hbm, basis_ref)]
    for a in range(SX):
        part = pl.ds(a * rows, rows)
        pairs.append((res_hbm.at[part], res_ref.at[part]))
    pairs.append((idx_hbm, idx_ref))
    copies = started(pairs, sems)
    copies[0].wait()
    for a in range(SX):
        copies[1 + a].wait()
        part = lax.dot_general(
            res_ref[a * rows : (a + 1) * rows, :], basis_ref[...], LAST, preferred_element_type=f32
        )
        out_ref[:, a * RX : (a + 1) * RX, :] = part.astype(bf16).reshape(SZ, RX, NC)
    copies[1 + SX].wait()
    idx = idx_ref[...]
    row = lax.broadcasted_iota(jnp.int32, (TAIL, NC), 0)
    digits = jnp.where(row == 0, idx >> 4, jnp.where(row == 1, idx & (BASE - 1), 0))
    digits = digits.astype(f32).astype(bf16)
    out_ref[:, RZ:, :] = jnp.broadcast_to(digits[None], (SZ, TAIL, NC))


def coarse_kernel(idx, res, basis):
    return call(
        coarse_body,
        (jax.ShapeDtypeStruct((SZ, PACK, NC), bf16), jax.ShapeDtypeStruct((R, NI), bf16)),
        0,
        0,
        vmem=BIG,
        in_specs=[HBM] * 3,
        out_specs=(VMEM, VMEM),
        scratch_shapes=[
            pltpu.VMEM((1, NC), jnp.int32),
            pltpu.VMEM((NC, NI), bf16),
            DMA((2 + SX,)),
        ],
    )(idx, res, basis)


def local_body(res_ref, schur_ref, out_ref):
    for f in range(FACES):
        out_ref[f] = mm(res_ref[...], schur_ref[:, face_cols(f)])


def local_kernel(res, schur):
    return call(
        local_body,
        jax.ShapeDtypeStruct((FACES, R, FACE), f32),
        0,
        0,
        vmem=SMALL,
        in_specs=[VMEM] * 2,
        out_specs=VMEM,
    )(res, schur)


def member_onehot(pack_ref):
    digits = pack_ref[:, RZ:, :].astype(f32)
    column = lax.broadcasted_iota(jnp.int32, (C2, NC), 0).astype(f32)
    parts = []
    for c in range(SZ):
        idx = digits[c, 0:1, :] * float(BASE) + digits[c, 1:2, :]
        parts.append((column == idx).astype(bf16))
    return jnp.concatenate(parts, axis=1)


def group_body(pack_ref, restrict_ref, res_ref, top_ref):
    onehot = member_onehot(pack_ref)
    rows = jnp.concatenate([pack_ref[c, :RZ, :] for c in range(SZ)], axis=1)
    group_res = lax.dot_general(rows, onehot, LAST, preferred_element_type=f32)
    res_ref[...] = group_res
    top_ref[...] = mm3(group_res, restrict_ref[...]).astype(bf16)


def group_kernel(pack, restrict):
    return call(
        group_body,
        (jax.ShapeDtypeStruct((RZ, C2), f32), jax.ShapeDtypeStruct((RZ, C2), bf16)),
        0,
        0,
        vmem=8,
        in_specs=[VMEM] * 2,
        out_specs=(VMEM, VMEM),
    )(pack, restrict)


def map_body(top_inv_ref, restrict_ref, hi_ref, lo_ref):
    t_hi, t_lo = split(top_inv_ref[...])
    r_hi, r_lo = split(restrict_ref[...])
    back = functools.partial(lax.dot_general, dimension_numbers=LAST, preferred_element_type=f32)
    both = back(t_hi, r_hi) + (back(t_hi, r_lo) + back(t_lo, r_hi))
    hi_ref[...], lo_ref[...] = split(both)


def map_kernel(top_inv, restrict):
    return call(
        map_body,
        (jax.ShapeDtypeStruct((C2, C2), bf16),) * 2,
        0,
        0,
        vmem=SMALL,
        in_specs=[VMEM] * 2,
        out_specs=(VMEM,) * 2,
    )(top_inv, restrict)


def own_body(res_ref, group_inv_ref, own_ref):
    own_ref[...] = mm3(res_ref[...], group_inv_ref[...])


def own_kernel(group_res, group_inv):
    return call(
        own_body,
        jax.ShapeDtypeStruct((RZ, C2), f32),
        0,
        0,
        vmem=SMALL,
        in_specs=[VMEM] * 2,
        out_specs=VMEM,
    )(group_res, group_inv)


def solve_body(pack_ref, own_ref, hi_ref, lo_ref, *refs):
    parts, out_ref = refs[:-1], refs[-1]
    onehot = member_onehot(pack_ref)
    top_res = sum(p[...].astype(f32) for p in parts)
    t_hi, t_lo = split(top_res)
    sol = own_ref[...] + mm(t_hi, hi_ref[...]) + (mm(t_hi, lo_ref[...]) + mm(t_lo, hi_ref[...]))
    picked = mm(sol.astype(bf16), onehot).astype(bf16)
    for c in range(SZ):
        out_ref[c] = picked[:, c * NC : (c + 1) * NC]


def solve_kernel(pack, own, map_hi, map_lo, parts):
    return call(
        solve_body,
        jax.ShapeDtypeStruct((SZ, RZ, NC), bf16),
        0,
        0,
        vmem=8,
        in_specs=[VMEM] * (4 + len(parts)),
        out_specs=VMEM,
    )(pack, own, map_hi, map_lo, *parts)


def sum_body(*refs):
    refs[-1][...] = sum(r[...].astype(f32) for r in refs[:-1]).astype(bf16)


def sum_kernel(parts):
    return call(
        sum_body,
        jax.ShapeDtypeStruct((RZ, C2), bf16),
        0,
        0,
        vmem=4,
        in_specs=[VMEM] * len(parts),
        out_specs=VMEM,
    )(*parts)


def send_face(meta_ref, e):
    odd = meta_ref[0, 18 + e // 2]
    return e // 2 * 2 + (odd if e % 2 else 1 - odd)


def update_body(meta_ref, back_ref, basis_ref, local_ref, *refs):
    sends, rows_ref = refs[:FACES], refs[FACES]
    for c in range(SZ):
        for a in range(SX):
            start = (a * SZ + c) * RX
            rows_ref[start : start + RX, :] = back_ref[c, a * RX : (a + 1) * RX, :]
    rows = rows_ref[...]
    for e in range(FACES):
        f = send_face(meta_ref, e)
        cols = pl.ds(pl.multiple_of(f * FACE, FACE), FACE)
        update = local_ref[f] + mm(rows, basis_ref[:, cols])
        sends[e][...] = swap_halves(update, meta_ref[0, 2 * f] == 1).astype(bf16)


def update_kernel(meta, back, basis, local):
    return call(
        update_body,
        (jax.ShapeDtypeStruct((R, FACE), bf16),) * FACES,
        0,
        0,
        vmem=SMALL,
        in_specs=[SMEM] + [VMEM] * 3,
        out_specs=(VMEM,) * FACES,
        scratch_shapes=[pltpu.VMEM((R, NC), bf16)],
    )(meta, back, basis, local)


def last_body(meta_ref, *refs):
    sends, gots = refs[:FACES], refs[FACES : 2 * FACES]
    out_hbm, out_ref, out_sems = refs[2 * FACES :]
    outs = []
    for e in range(FACES):
        f = send_face(meta_ref, e)
        cols = pl.ds(pl.multiple_of(f * FACE, FACE), FACE)
        weight = jnp.where(meta_ref[0, 12 + f] == 1, 0.5, 1.0).astype(f32)
        both = weight * (sends[e][...].astype(f32) + gots[e][...].astype(f32))
        out_ref[e] = swap_halves(both, meta_ref[0, 2 * f] == 1).astype(bf16)
        outs += started([(out_ref.at[e], out_hbm.at[:, cols])], out_sems.at[pl.ds(e, 1)])
    for c in outs:
        c.wait()


def last_kernel(meta, sends, gots):
    return call(
        last_body,
        jax.ShapeDtypeStruct((R, NI), bf16),
        0,
        0,
        vmem=SMALL,
        in_specs=[SMEM] + [VMEM] * (2 * FACES),
        out_specs=HBM,
        scratch_shapes=[pltpu.VMEM((FACES, R, FACE), bf16), DMA((FACES,))],
    )(meta, *sends, *gots)


def ring(count, d):
    return [(i, (i + d) % count) for i in range(count)]


def after(x, *others):
    return lax.optimization_barrier((x,) + others)[0]


def per_device(
    residual,
    schur_inverse,
    coarse_basis,
    coarse_index,
    block_slot,
    group_inverse,
    group_restrict,
    top_inverse,
):
    res = residual[0, 0, 0]
    schur = schur_inverse[0, 0, 0]
    basis = coarse_basis[0, 0, 0]
    idx = coarse_index.reshape(1, NC)
    group_inv = group_inverse[0, 0]
    restrict = group_restrict[0, 0]
    place = [lax.axis_index(axis) for axis in ("gx", "gy", "gz")]
    facts = []
    for at, count in zip(place, (SX, SY, SZ)):
        facts += [at > 0, at < count - 1]
    facts += [at % 2 for at in place]
    facts = jnp.stack([jnp.asarray(v, jnp.int32) for v in facts])
    meta = jnp.concatenate([block_slot.reshape(2 * FACES), facts]).reshape(1, -1)

    pack, res = coarse_kernel(idx, res, basis)
    local = local_kernel(res, schur)
    pack = after(lax.all_to_all(pack, "gz", 0, 0), local)
    group_res, part = group_kernel(pack, restrict)
    top_map = map_kernel(top_inverse, after(restrict, part))
    own = own_kernel(group_res, group_inv)
    gots = [part] + [lax.ppermute(part, "gx", [(i, i ^ d) for i in range(SX)]) for d in (1, 3, 2)]
    part = sum_kernel(lax.optimization_barrier((*gots, *top_map))[:SX])
    got = after(lax.ppermute(part, "gy", [(i, i ^ 1) for i in range(SY)]), own)
    part = sum_kernel([part, got])
    part = sum_kernel([part, lax.ppermute(part, "gy", [(i, i ^ 2) for i in range(SY)])])
    parts = [part, lax.ppermute(part, "gy", [(i, SY - 1 - i) for i in range(SY)])]
    back = solve_kernel(pack, own, *top_map, parts)
    back = lax.all_to_all(back, "gz", 0, 0)
    sends = update_kernel(meta, back, basis, local)
    gots = []
    for axis, count, e in (("gx", SX, 0), ("gy", SY, 2), ("gz", SZ, 4)):
        near = [(i, i + 1) for i in range(0, count, 2)]
        far = [(i, i + 1) for i in range(1, count - 1, 2)]
        for f, pairs in ((e, near), (e + 1, far)):
            gots.append(lax.ppermute(sends[f], axis, pairs + [(j, i) for i, j in pairs]))
    return last_kernel(meta, sends, gots).reshape(1, 1, 1, R, NI)


def solution(mesh):
    return jax.shard_map(
        per_device,
        mesh=mesh,
        in_specs=(
            P("gx", "gy", "gz", None, None),
            P("gx", "gy", "gz", None, None),
            P("gx", "gy", "gz", None, None),
            P("gx", "gy", "gz", None),
            P("gx", "gy", "gz", None),
            P("gx", "gy", None, None),
            P("gx", "gy", None, None),
            P(),
        ),
        out_specs=P("gx", "gy", "gz", None, None),
        check_vma=False,
    )
```

time: 117 us -> 76.9 us (0.66)
  the two profiles are of different devices: /device:TPU:1 before, /device:TPU:131 now
where the time goes in v2:
time: 76.9 us; the launch traced here: 76.4 us
  starting transfers between devices  31 us (40%)
  waiting for transfers between devices  25.6 us (33%)
  Pallas kernels  12.6 us (16%)
  local copies, waits for them, and re-layouts  7.01 us (9%)
    ppermute x6, starting transfers between devices, per_device(): lax.ppermute(sends[f], axis, pairs + [(j, i) for i, j in pairs])  10.4 us
    all_to_all x1, starting transfers between devices, per_device(): back = lax.all_to_all(back, 'gz', 0, 0)  9.96 us
    ppermute x6, waiting for transfers between devices, per_device(): lax.ppermute(sends[f], axis, pairs + [(j, i) for i, j in pairs])  9.29 us
    unnamed x22, local copies, waits for them, and re-layouts  6.93 us
    all_to_all x1, waiting for transfers between devices, per_device(): back = lax.all_to_all(back, 'gz', 0, 0)  5.29 us
    all_to_all x1, starting transfers between devices, per_device(): pack = after(lax.all_to_all(pack, 'gz', 0, 0), local)  5.15 us
    ppermute x1, waiting for transfers between devices, per_device(): lax.ppermute(part, 'gy', [(i, SY - 1 - i) for i in range(SY)])  4.31 us
    pallas_call x1, Pallas kernels, coarse_kernel(): call(coarse_body, (jax.ShapeDtypeStruct((SZ, PACK, NC), bf16), jax.ShapeD...  3.76 us
  transfers between devices with their start and end apart: 14, of which 9 were waited for; matrix products, arithmetic and copies ran while one was open for 0% of the time, Pallas kernels for 5%

profile of v2, /device:TPU:131, one launch (start us, length us, event | category | flops | bytes accessed | tf_op | source)
XLA Modules:
  0.0 76.4 jit_solution(11360229493264296461)
XLA Ops:
  0.0 3.8 %shard_map.82 = (bf16[8,80,128]{2,1,0:T(8,128)(2,1)}, bf16[512,1536]{1,0:T(8,128)(2,1)}) custom-call(s32[1,128]{1,0:T(1,128)} %bitcast.27, bf16[512,1536]{1,0:T(8,128)(2,1)} %bitcast.26, bf16[128,1536]{1,0:T(8,128)(2,1)} %bitcast.21), custom_call_target="tpu_custom_call" | custom-call | flops 1024 | bytes 1024 | tf_op jit(solution)/shard_map/pallas_call | solution.py:105
  3.8 5.2 %all-to-all-start = ((bf16[8,80,128]{2,1,0:T(8,128)(2,1)}), bf16[8,80,128]{2,1,0:T(8,128)(2,1)S(1)}, u32[]{:S(2)}, u32[]{:S(2)}) async-start(bf16[8,80,128]{2,1,0:T(8,128)(2,1)} %get-tuple-element.24), calls=%async_computation | async-start | bytes 327680 | tf_op jit(solution)/shard_map/all_to_all | solution.py:337
  8.9 0.0 copy-start
  8.9 2.3 %copy-done = bf16[1,1,1,1536,1536]{4,3,2,1,0:T(8,128)(2,1)S(1)} copy-done((bf16[1,1,1,1536,1536]{4,3,2,1,0:T(8,128)(2,1)S(1)}, bf16[1,1,1,1536,1536]{4,3,2,1,0:T(8,128)(2,1)}, u32[]{:S(2)}) %copy-start) | copy-done | bytes 4718616
  11.3 0.0 copy-start.3
  11.3 1.4 %copy-done.3 = bf16[512,1536]{1,0:T(8,128)(2,1)S(1)} copy-done((bf16[512,1536]{1,0:T(8,128)(2,1)S(1)}, bf16[512,1536]{1,0:T(8,128)(2,1)}, u32[]{:S(2)}) %copy-start.3) | copy-done | bytes 1572888
  12.7 2.6 %shard_map.83.local_ref = f32[6,512,256]{2,1,0:T(8,128)S(1)} custom-call(bf16[512,1536]{1,0:T(8,128)(2,1)S(1)} %copy-done.3, bf16[1536,1536]{1,0:T(8,128)(2,1)S(1)} %bitcast.18), custom_call_target="tpu_custom_call" | custom-call | flops 1024 | bytes 1024 | tf_op jit(solution)/shard_map/pallas_call | solution.py:127
  15.3 0.0 all-to-all-done.pack_ref
  15.3 0.0 copy-start.5
  15.3 0.0 copy-start.1
  15.3 1.3 %copy-done.1 = f32[1,1,512,512]{3,2,1,0:T(8,128)S(1)} copy-done((f32[1,1,512,512]{3,2,1,0:T(8,128)S(1)}, f32[1,1,512,512]{3,2,1,0:T(8,128)}, u32[]{:S(2)}) %copy-start.1) | copy-done | bytes 1048600
  16.6 0.0 copy-start.2
  16.6 0.0 copy-start.7
  16.6 0.8 %shard_map.84 = (f32[64,512]{1,0:T(8,128)S(1)}, bf16[64,512]{1,0:T(8,128)(2,1)S(1)}) custom-call(bf16[8,80,128]{2,1,0:T(8,128)(2,1)S(1)} %all-to-all-done.pack_ref, f32[512,512]{1,0:T(8,128)S(1)} %bitcast.19), custom_call_target="tpu_custom_call" | custom-call | flops 1024 | bytes 1024 | tf_op jit(solution)/shard_map/pallas_call | solution.py:157
  17.4 0.3 collective-permute-start
  17.7 1.9 %collective-permute-start.1 = (bf16[64,512]{1,0:T(8,128)(2,1)S(1)}, bf16[64,512]{1,0:T(8,128)(2,1)S(1)}, u32[]{:S(2)}, u32[]{:S(2)}) collective-permute-start(bf16[64,512]{1,0:T(8,128)(2,1)S(1)} %get-tuple-element.32.refs_0_), channel_id=1, source_target_pairs={{0,192},{64,128},{128,64},{192,0},{1,193},{65,129},{129,65},{193,1... | collective-permute-start | bytes 196616 | tf_op jit(solution)/shard_map/ppermute | solution.py:341
  19.6 1.1 %collective-permute-start.2 = (bf16[64,512]{1,0:T(8,128)(2,1)S(1)}, bf16[64,512]{1,0:T(8,128)(2,1)S(1)}, u32[]{:S(2)}, u32[]{:S(2)}) collective-permute-start(bf16[64,512]{1,0:T(8,128)(2,1)S(1)} %get-tuple-element.32.refs_0_), channel_id=1, source_target_pairs={{0,128},{64,192},{128,0},{192,64},{1,129},{65,193},{129,1},{193,65... | collective-permute-start | bytes 196616 | tf_op jit(solution)/shard_map/ppermute | solution.py:341
  20.7 0.0 copy-done.2
  20.7 0.0 copy-start.8
  20.7 1.2 %copy-done.8 = f32[512,512]{1,0:T(8,128)S(1)} copy-done((f32[512,512]{1,0:T(8,128)S(1)}, f32[512,512]{1,0:T(8,128)}, u32[]{:S(2)}) %copy-start.8) | copy-done | bytes 1048600
  22.0 1.0 %shard_map.86 = (bf16[512,512]{1,0:T(8,128)(2,1)S(1)}, bf16[512,512]{1,0:T(8,128)(2,1)S(1)}) custom-call(f32[512,512]{1,0:T(8,128)S(1)} %copy-done.8, f32[512,512]{1,0:T(8,128)S(1)} %bitcast.20), custom_call_target="tpu_custom_call" | custom-call | flops 1024 | bytes 1024 | tf_op jit(solution)/shard_map/pallas_call | solution.py:177
  23.0 0.0 copy-done.5
  23.0 0.0 collective-permute-done.refs_1_
  23.0 0.0 copy-start.6
  23.0 0.0 collective-permute-done.1.refs_2_
  23.0 1.2 %collective-permute-done.2.refs_3_ = bf16[64,512]{1,0:T(8,128)(2,1)S(1)} collective-permute-done((bf16[64,512]{1,0:T(8,128)(2,1)S(1)}, bf16[64,512]{1,0:T(8,128)(2,1)S(1)}, u32[]{:S(2)}, u32[]{:S(2)}) %collective-permute-start.2) | collective-permute-done | bytes 65568 | tf_op jit(solution)/shard_map/ppermute | solution.py:341
  24.3 0.8 %collective-permute-start.3 = (bf16[64,512]{1,0:T(8,128)(2,1)S(1)}, bf16[64,512]{1,0:T(8,128)(2,1)S(1)}, u32[]{:S(2)}, u32[]{:S(2)}) collective-permute-start(bf16[64,512]{1,0:T(8,128)(2,1)S(1)} %shard_map.87.refs_0_), channel_id=1, source_target_pairs={{0,8},{8,0},{16,24},{24,16},{32,40},{40,32},{48,56},{56,48},{1,9},... | collective-permute-start | bytes 196616 | tf_op jit(solution)/shard_map/ppermute | solution.py:343
  25.1 0.0 copy-done.7
  25.1 0.0 copy-start.10
  25.1 0.0 copy-start.4
  25.1 0.4 shard_map.85.own_ref
  25.5 2.0 %collective-permute-done.3.refs_1_ = bf16[64,512]{1,0:T(8,128)(2,1)S(1)} collective-permute-done((bf16[64,512]{1,0:T(8,128)(2,1)S(1)}, bf16[64,512]{1,0:T(8,128)(2,1)S(1)}, u32[]{:S(2)}, u32[]{:S(2)}) %collective-permute-start.3) | collective-permute-done | bytes 65568 | tf_op jit(solution)/shard_map/ppermute | solution.py:343
  27.5 1.3 %collective-permute-start.4 = (bf16[64,512]{1,0:T(8,128)(2,1)S(1)}, bf16[64,512]{1,0:T(8,128)(2,1)S(1)}, u32[]{:S(2)}, u32[]{:S(2)}) collective-permute-start(bf16[64,512]{1,0:T(8,128)(2,1)S(1)} %shard_map.88.refs_0_), channel_id=1, source_target_pairs={{0,16},{8,24},{16,0},{24,8},{32,48},{40,56},{48,32},{56,40},{1,17}... | collective-permute-start | bytes 196616 | tf_op jit(solution)/shard_map/ppermute | solution.py:345
  28.8 3.5 %collective-permute-done.4.refs_1_ = bf16[64,512]{1,0:T(8,128)(2,1)S(1)} collective-permute-done((bf16[64,512]{1,0:T(8,128)(2,1)S(1)}, bf16[64,512]{1,0:T(8,128)(2,1)S(1)}, u32[]{:S(2)}, u32[]{:S(2)}) %collective-permute-start.4) | collective-permute-done | bytes 65568 | tf_op jit(solution)/shard_map/ppermute | solution.py:345
  32.3 0.1 collective-permute-start.5
  32.4 4.3 %collective-permute-done.5.refs_1_ = bf16[64,512]{1,0:T(8,128)(2,1)S(1)} collective-permute-done((bf16[64,512]{1,0:T(8,128)(2,1)S(1)}, bf16[64,512]{1,0:T(8,128)(2,1)S(1)}, u32[]{:S(2)}, u32[]{:S(2)}) %collective-permute-start.5) | collective-permute-done | bytes 65568 | tf_op jit(solution)/shard_map/ppermute | solution.py:346
  36.7 0.0 copy-done.6
  36.7 0.6 shard_map.90
  37.4 0.0 copy-start.9
  37.4 0.6 copy-done.9
  38.0 10.0 %all-to-all-start.1 = ((bf16[8,64,128]{2,1,0:T(8,128)(2,1)}), bf16[8,64,128]{2,1,0:T(8,128)(2,1)}, u32[]{:S(2)}, u32[]{:S(2)}) async-start(bf16[8,64,128]{2,1,0:T(8,128)(2,1)} %copy-done.9), calls=%async_computation.1 | async-start | bytes 262144 | tf_op jit(solution)/shard_map/all_to_all | solution.py:348
  48.0 0.0 copy-done.10
  48.0 0.1 concatenate.3
  48.1 5.3 %all-to-all-done.1.back_ref = bf16[8,64,128]{2,1,0:T(8,128)(2,1)} async-done(((bf16[8,64,128]{2,1,0:T(8,128)(2,1)}), bf16[8,64,128]{2,1,0:T(8,128)(2,1)}, u32[]{:S(2)}, u32[]{:S(2)}) %all-to-all-start.1) | async-done | bytes 131104 | tf_op jit(solution)/shard_map/all_to_all | solution.py:348
  53.4 0.0 copy-done.4
  53.4 1.5 %shard_map.91 = (bf16[512,256]{1,0:T(8,128)(2,1)S(1)}, bf16[512,256]{1,0:T(8,128)(2,1)S(1)}, bf16[512,256]{1,0:T(8,128)(2,1)S(1)}, bf16[512,256]{1,0:T(8,128)(2,...) custom-call(s32[1,21]{1,0:T(1,128)S(1)} %bitcast.24, bf16[8,64,128]{2,1,0:T(8,128)(2,1)} %all-to-all-done.1.back_ref, ...), custom_call_target="tpu_custom_call" | custom-call | flops 1024 | bytes 1024 | tf_op jit(solution)/shard_map/pallas_call | solution.py:263
  54.9 0.9 %collective-permute-start.10 = (bf16[512,256]{1,0:T(8,128)(2,1)S(1)}, bf16[512,256]{1,0:T(8,128)(2,1)S(1)}, u32[]{:S(2)}, u32[]{:S(2)}) collective-permute-start(bf16[512,256]{1,0:T(8,128)(2,1)S(1)} %get-tuple-element.41.refs_4_), channel_id=1, source_target_pairs={{0,1},{2,3},{4,5},{6,7},{1,0},{3,2},{5,4},{7,6},{8,9},{10,11},{12,... | collective-permute-start | bytes 786440 | tf_op jit(solution)/shard_map/ppermute | solution.py:355
  55.8 2.1 %collective-permute-start.11 = (bf16[512,256]{1,0:T(8,128)(2,1)S(1)}, bf16[512,256]{1,0:T(8,128)(2,1)S(1)}, u32[]{:S(2)}, u32[]{:S(2)}) collective-permute-start(bf16[512,256]{1,0:T(8,128)(2,1)S(1)} %get-tuple-element.42.refs_5_), channel_id=1, source_target_pairs={{1,2},{3,4},{5,6},{2,1},{4,3},{6,5},{9,10},{11,12},{13,14},{10,9},... | collective-permute-start | bytes 786440 | tf_op jit(solution)/shard_map/ppermute | solution.py:355
  57.9 1.2 %collective-permute-start.6 = (bf16[512,256]{1,0:T(8,128)(2,1)S(1)}, bf16[512,256]{1,0:T(8,128)(2,1)S(1)}, u32[]{:S(2)}, u32[]{:S(2)}) collective-permute-start(bf16[512,256]{1,0:T(8,128)(2,1)S(1)} %get-tuple-element.37.refs_0_), channel_id=1, source_target_pairs={{0,64},{128,192},{64,0},{192,128},{1,65},{129,193},{65,1},{193,129... | collective-permute-start | bytes 786440 | tf_op jit(solution)/shard_map/ppermute | solution.py:355
  59.2 2.2 %collective-permute-start.7 = (bf16[512,256]{1,0:T(8,128)(2,1)S(1)}, bf16[512,256]{1,0:T(8,128)(2,1)S(1)}, u32[]{:S(2)}, u32[]{:S(2)}) collective-permute-start(bf16[512,256]{1,0:T(8,128)(2,1)S(1)} %get-tuple-element.38.refs_1_), channel_id=1, source_target_pairs={{64,128},{128,64},{65,129},{129,65},{66,130},{130,66},{67,131},{13... | collective-permute-start | bytes 786440 | tf_op jit(solution)/shard_map/ppermute | solution.py:355
  61.3 2.0 %collective-permute-start.8 = (bf16[512,256]{1,0:T(8,128)(2,1)S(1)}, bf16[512,256]{1,0:T(8,128)(2,1)S(1)}, u32[]{:S(2)}, u32[]{:S(2)}) collective-permute-start(bf16[512,256]{1,0:T(8,128)(2,1)S(1)} %get-tuple-element.39.refs_2_), channel_id=1, source_target_pairs={{0,8},{16,24},{32,40},{48,56},{8,0},{24,16},{40,32},{56,48},{1,9},... | collective-permute-start | bytes 786440 | tf_op jit(solution)/shard_map/ppermute | solution.py:355
  63.4 0.0 collective-permute-done.10.refs_10_
  63.4 1.9 %collective-permute-start.9 = (bf16[512,256]{1,0:T(8,128)(2,1)S(1)}, bf16[512,256]{1,0:T(8,128)(2,1)S(1)}, u32[]{:S(2)}, u32[]{:S(2)}) collective-permute-start(bf16[512,256]{1,0:T(8,128)(2,1)S(1)} %get-tuple-element.40.refs_3_), channel_id=1, source_target_pairs={{8,16},{24,32},{40,48},{16,8},{32,24},{48,40},{9,17},{25,33},{41,4... | collective-permute-start | bytes 786440 | tf_op jit(solution)/shard_map/ppermute | solution.py:355
  65.3 0.0 collective-permute-done.11.refs_11_
  65.3 0.1 collective-permute-done.6.refs_6_
  65.4 3.3 %collective-permute-done.7.refs_7_ = bf16[512,256]{1,0:T(8,128)(2,1)S(1)} collective-permute-done((bf16[512,256]{1,0:T(8,128)(2,1)S(1)}, bf16[512,256]{1,0:T(8,128)(2,1)S(1)}, u32[]{:S(2)}, u32[]{:S(2)}) %collective-permute-start.7) | collective-permute-done | bytes 262176 | tf_op jit(solution)/shard_map/ppermute | solution.py:355
  68.7 0.8 %collective-permute-done.8.refs_8_ = bf16[512,256]{1,0:T(8,128)(2,1)S(1)} collective-permute-done((bf16[512,256]{1,0:T(8,128)(2,1)S(1)}, bf16[512,256]{1,0:T(8,128)(2,1)S(1)}, u32[]{:S(2)}, u32[]{:S(2)}) %collective-permute-start.8) | collective-permute-done | bytes 262176 | tf_op jit(solution)/shard_map/ppermute | solution.py:355
  69.6 5.0 %collective-permute-done.9.refs_9_ = bf16[512,256]{1,0:T(8,128)(2,1)S(1)} collective-permute-done((bf16[512,256]{1,0:T(8,128)(2,1)S(1)}, bf16[512,256]{1,0:T(8,128)(2,1)S(1)}, u32[]{:S(2)}, u32[]{:S(2)}) %collective-permute-start.9) | collective-permute-done | bytes 262176 | tf_op jit(solution)/shard_map/ppermute | solution.py:355
  74.6 1.9 %shard_map.92 = bf16[512,1536]{1,0:T(8,128)(2,1)} custom-call(s32[1,21]{1,0:T(1,128)S(1)} %bitcast.25, bf16[512,256]{1,0:T(8,128)(2,1)S(1)} %get-tuple-element.37.refs_0_, bf16[512,256]{1,0:T(8,128)(2,1)S(1)} %get-tuple-element.38.refs_1_, bf16[512,256]{1,0:T(8,128)(2,1)S(1)} %get-tuple-element.39.refs_2_, bf16[512,256]{1,0:T(8,128)(2,1)S(1)} %get-tuple-element.40.refs_3_, ...), custom_call_target="tpu_custom_call" | custom-call | flops 1024 | bytes 1024 | tf_op jit(solution)/shard_map/pallas_call | solution.py:291
  (3 shorter events, 0.1 us)
Async XLA Ops:
  3.8 11.5 %all-to-all-start = ((bf16[8,80,128]{2,1,0:T(8,128)(2,1)}), bf16[8,80,128]{2,1,0:T(8,128)(2,1)S(1)}, u32[]{:S(2)}, u32[]{:S(2)}) async-start(bf16[8,80,128]{2,1,0:T(8,128)(2,1)} %get-tuple-element.24), calls=%async_computation | async-start | bytes 327680 | tf_op jit(solution)/shard_map/all_to_all | solution.py:337
  8.9 2.3 %copy-start = (bf16[1,1,1,1536,1536]{4,3,2,1,0:T(8,128)(2,1)S(1)}, bf16[1,1,1,1536,1536]{4,3,2,1,0:T(8,128)(2,1)}, u32[]{:S(2)}) copy-start(bf16[1,1,1,1536,1536]{4,3,2,1,0:T(8,128)(2,1)} %param.9) | copy-start | bytes 14155780
  11.3 1.4 %copy-start.3 = (bf16[512,1536]{1,0:T(8,128)(2,1)S(1)}, bf16[512,1536]{1,0:T(8,128)(2,1)}, u32[]{:S(2)}) copy-start(bf16[512,1536]{1,0:T(8,128)(2,1)} %get-tuple-element.25.res_ref) | copy-start | bytes 4718596
  15.3 7.7 %copy-start.5 = (bf16[8,80,128]{2,1,0:T(8,128)(2,1)}, bf16[8,80,128]{2,1,0:T(8,128)(2,1)S(1)}, u32[]{:S(2)}) copy-start(bf16[8,80,128]{2,1,0:T(8,128)(2,1)S(1)} %all-to-all-done.pack_ref) | copy-start | bytes 491524
  15.3 1.3 %copy-start.1 = (f32[1,1,512,512]{3,2,1,0:T(8,128)S(1)}, f32[1,1,512,512]{3,2,1,0:T(8,128)}, u32[]{:S(2)}) copy-start(f32[1,1,512,512]{3,2,1,0:T(8,128)} %param.14) | copy-start | bytes 3145732
  16.6 4.2 %copy-start.2 = (f32[1,1,512,512]{3,2,1,0:T(8,128)S(1)}, f32[1,1,512,512]{3,2,1,0:T(8,128)}, u32[]{:S(2)}) copy-start(f32[1,1,512,512]{3,2,1,0:T(8,128)} %param.14) | copy-start | bytes 3145732
  16.6 8.5 %copy-start.7 = (f32[1,1,512,512]{3,2,1,0:T(8,128)S(1)}, f32[1,1,512,512]{3,2,1,0:T(8,128)}, u32[]{:S(2)}) copy-start(f32[1,1,512,512]{3,2,1,0:T(8,128)} %param.13) | copy-start | bytes 3145732
  17.4 5.6 %collective-permute-start = (bf16[64,512]{1,0:T(8,128)(2,1)S(1)}, bf16[64,512]{1,0:T(8,128)(2,1)S(1)}, u32[]{:S(2)}, u32[]{:S(2)}) collective-permute-start(bf16[64,512]{1,0:T(8,128)(2,1)S(1)} %get-tuple-element.32.refs_0_), channel_id=1, source_target_pairs={{0,64},{64,0},{128,192},{192,128},{1,65},{65,1},{129,193},{193,129... | collective-permute-start | bytes 196616 | tf_op jit(solution)/shard_map/ppermute | solution.py:341
  17.7 5.3 %collective-permute-start.1 = (bf16[64,512]{1,0:T(8,128)(2,1)S(1)}, bf16[64,512]{1,0:T(8,128)(2,1)S(1)}, u32[]{:S(2)}, u32[]{:S(2)}) collective-permute-start(bf16[64,512]{1,0:T(8,128)(2,1)S(1)} %get-tuple-element.32.refs_0_), channel_id=1, source_target_pairs={{0,192},{64,128},{128,64},{192,0},{1,193},{65,129},{129,65},{193,1... | collective-permute-start | bytes 196616 | tf_op jit(solution)/shard_map/ppermute | solution.py:341
  19.6 4.6 %collective-permute-start.2 = (bf16[64,512]{1,0:T(8,128)(2,1)S(1)}, bf16[64,512]{1,0:T(8,128)(2,1)S(1)}, u32[]{:S(2)}, u32[]{:S(2)}) collective-permute-start(bf16[64,512]{1,0:T(8,128)(2,1)S(1)} %get-tuple-element.32.refs_0_), channel_id=1, source_target_pairs={{0,128},{64,192},{128,0},{192,64},{1,129},{65,193},{129,1},{193,65... | collective-permute-start | bytes 196616 | tf_op jit(solution)/shard_map/ppermute | solution.py:341
  20.7 1.2 %copy-start.8 = (f32[512,512]{1,0:T(8,128)S(1)}, f32[512,512]{1,0:T(8,128)}, u32[]{:S(2)}) copy-start(f32[512,512]{1,0:T(8,128)} %top_inv_ref.1) | copy-start | bytes 3145732
  23.0 13.7 %copy-start.6 = (bf16[8,80,128]{2,1,0:T(8,128)(2,1)S(1)}, bf16[8,80,128]{2,1,0:T(8,128)(2,1)}, u32[]{:S(2)}) copy-start(bf16[8,80,128]{2,1,0:T(8,128)(2,1)} %copy-done.5) | copy-start | bytes 491524
  24.3 3.2 %collective-permute-start.3 = (bf16[64,512]{1,0:T(8,128)(2,1)S(1)}, bf16[64,512]{1,0:T(8,128)(2,1)S(1)}, u32[]{:S(2)}, u32[]{:S(2)}) collective-permute-start(bf16[64,512]{1,0:T(8,128)(2,1)S(1)} %shard_map.87.refs_0_), channel_id=1, source_target_pairs={{0,8},{8,0},{16,24},{24,16},{32,40},{40,32},{48,56},{56,48},{1,9},... | collective-permute-start | bytes 196616 | tf_op jit(solution)/shard_map/ppermute | solution.py:343
  25.1 22.9 %copy-start.10 = (s32[1,1,1,12]{3,2,1,0:T(1,128)S(1)}, s32[1,1,1,12]{3,2,1,0:T(1,128)}, u32[]{:S(2)}) copy-start(s32[1,1,1,12]{3,2,1,0:T(1,128)} %param.12) | copy-start | bytes 148
  25.1 28.3 %copy-start.4 = (bf16[1,1,1,128,1536]{4,3,2,1,0:T(8,128)(2,1)S(1)}, bf16[1,1,1,128,1536]{4,3,2,1,0:T(8,128)(2,1)}, u32[]{:S(2)}) copy-start(bf16[1,1,1,128,1536]{4,3,2,1,0:T(8,128)(2,1)} %param.10) | copy-start | bytes 1179652
  27.5 4.8 %collective-permute-start.4 = (bf16[64,512]{1,0:T(8,128)(2,1)S(1)}, bf16[64,512]{1,0:T(8,128)(2,1)S(1)}, u32[]{:S(2)}, u32[]{:S(2)}) collective-permute-start(bf16[64,512]{1,0:T(8,128)(2,1)S(1)} %shard_map.88.refs_0_), channel_id=1, source_target_pairs={{0,16},{8,24},{16,0},{24,8},{32,48},{40,56},{48,32},{56,40},{1,17}... | collective-permute-start | bytes 196616 | tf_op jit(solution)/shard_map/ppermute | solution.py:345
  32.3 4.4 %collective-permute-start.5 = (bf16[64,512]{1,0:T(8,128)(2,1)S(1)}, bf16[64,512]{1,0:T(8,128)(2,1)S(1)}, u32[]{:S(2)}, u32[]{:S(2)}) collective-permute-start(bf16[64,512]{1,0:T(8,128)(2,1)S(1)} %shard_map.89.refs_0_), channel_id=1, source_target_pairs={{0,56},{8,48},{16,40},{24,32},{32,24},{40,16},{48,8},{56,0},{1,57}... | collective-permute-start | bytes 196616 | tf_op jit(solution)/shard_map/ppermute | solution.py:346
  37.4 0.7 copy-start.9
  38.0 15.3 %all-to-all-start.1 = ((bf16[8,64,128]{2,1,0:T(8,128)(2,1)}), bf16[8,64,128]{2,1,0:T(8,128)(2,1)}, u32[]{:S(2)}, u32[]{:S(2)}) async-start(bf16[8,64,128]{2,1,0:T(8,128)(2,1)} %copy-done.9), calls=%async_computation.1 | async-start | bytes 262144 | tf_op jit(solution)/shard_map/all_to_all | solution.py:348
  54.9 8.5 %collective-permute-start.10 = (bf16[512,256]{1,0:T(8,128)(2,1)S(1)}, bf16[512,256]{1,0:T(8,128)(2,1)S(1)}, u32[]{:S(2)}, u32[]{:S(2)}) collective-permute-start(bf16[512,256]{1,0:T(8,128)(2,1)S(1)} %get-tuple-element.41.refs_4_), channel_id=1, source_target_pairs={{0,1},{2,3},{4,5},{6,7},{1,0},{3,2},{5,4},{7,6},{8,9},{10,11},{12,... | collective-permute-start | bytes 786440 | tf_op jit(solution)/shard_map/ppermute | solution.py:355
  55.8 9.4 %collective-permute-start.11 = (bf16[512,256]{1,0:T(8,128)(2,1)S(1)}, bf16[512,256]{1,0:T(8,128)(2,1)S(1)}, u32[]{:S(2)}, u32[]{:S(2)}) collective-permute-start(bf16[512,256]{1,0:T(8,128)(2,1)S(1)} %get-tuple-element.42.refs_5_), channel_id=1, source_target_pairs={{1,2},{3,4},{5,6},{2,1},{4,3},{6,5},{9,10},{11,12},{13,14},{10,9},... | collective-permute-start | bytes 786440 | tf_op jit(solution)/shard_map/ppermute | solution.py:355
  57.9 7.5 %collective-permute-start.6 = (bf16[512,256]{1,0:T(8,128)(2,1)S(1)}, bf16[512,256]{1,0:T(8,128)(2,1)S(1)}, u32[]{:S(2)}, u32[]{:S(2)}) collective-permute-start(bf16[512,256]{1,0:T(8,128)(2,1)S(1)} %get-tuple-element.37.refs_0_), channel_id=1, source_target_pairs={{0,64},{128,192},{64,0},{192,128},{1,65},{129,193},{65,1},{193,129... | collective-permute-start | bytes 786440 | tf_op jit(solution)/shard_map/ppermute | solution.py:355
  59.2 9.5 %collective-permute-start.7 = (bf16[512,256]{1,0:T(8,128)(2,1)S(1)}, bf16[512,256]{1,0:T(8,128)(2,1)S(1)}, u32[]{:S(2)}, u32[]{:S(2)}) collective-permute-start(bf16[512,256]{1,0:T(8,128)(2,1)S(1)} %get-tuple-element.38.refs_1_), channel_id=1, source_target_pairs={{64,128},{128,64},{65,129},{129,65},{66,130},{130,66},{67,131},{13... | collective-permute-start | bytes 786440 | tf_op jit(solution)/shard_map/ppermute | solution.py:355
  61.3 8.2 %collective-permute-start.8 = (bf16[512,256]{1,0:T(8,128)(2,1)S(1)}, bf16[512,256]{1,0:T(8,128)(2,1)S(1)}, u32[]{:S(2)}, u32[]{:S(2)}) collective-permute-start(bf16[512,256]{1,0:T(8,128)(2,1)S(1)} %get-tuple-element.39.refs_2_), channel_id=1, source_target_pairs={{0,8},{16,24},{32,40},{48,56},{8,0},{24,16},{40,32},{56,48},{1,9},... | collective-permute-start | bytes 786440 | tf_op jit(solution)/shard_map/ppermute | solution.py:355
  63.4 11.2 %collective-permute-start.9 = (bf16[512,256]{1,0:T(8,128)(2,1)S(1)}, bf16[512,256]{1,0:T(8,128)(2,1)S(1)}, u32[]{:S(2)}, u32[]{:S(2)}) collective-permute-start(bf16[512,256]{1,0:T(8,128)(2,1)S(1)} %get-tuple-element.40.refs_3_), channel_id=1, source_target_pairs={{8,16},{24,32},{40,48},{16,8},{32,24},{48,40},{9,17},{25,33},{41,4... | collective-permute-start | bytes 786440 | tf_op jit(solution)/shard_map/ppermute | solution.py:355

commit v3 on v2

--- a/solution.py
+++ b/solution.py
@@ -23,6 +23,7 @@
 COST = 1024
 BIG = 58
 SMALL = 6
+ORDER = (0, 2, 1, 3, 5, 4)
 CHIPS = SZ // 2
 
 LAST = (((1,), (1,)), ((), ()))
@@ -62,6 +63,7 @@
 
 SMEM = pl.BlockSpec(memory_space=pltpu.SMEM)
 VMEM = pl.BlockSpec(memory_space=pltpu.VMEM)
+ANY = pl.BlockSpec(memory_space=pl.ANY)
 HBM = pl.BlockSpec(memory_space=pltpu.HBM)
 DMA = pltpu.SemaphoreType.DMA
 
@@ -78,7 +80,7 @@
     return slice(f * FACE, (f + 1) * FACE)
 
 
-def coarse_body(idx_hbm, res_hbm, basis_hbm, out_ref, res_ref, idx_ref, basis_ref, sems):
+def coarse_body(idx_hbm, res_hbm, basis_hbm, out_ref, idx_ref, res_ref, basis_ref, sems):
     rows = R // SX
     pairs = [(basis_hbm, basis_ref)]
     for a in range(SX):
@@ -104,35 +106,36 @@
 def coarse_kernel(idx, res, basis):
     return call(
         coarse_body,
-        (jax.ShapeDtypeStruct((SZ, PACK, NC), bf16), jax.ShapeDtypeStruct((R, NI), bf16)),
+        jax.ShapeDtypeStruct((SZ, PACK, NC), bf16),
         0,
         0,
         vmem=BIG,
         in_specs=[HBM] * 3,
-        out_specs=(VMEM, VMEM),
+        out_specs=VMEM,
         scratch_shapes=[
             pltpu.VMEM((1, NC), jnp.int32),
+            pltpu.VMEM((R, NI), bf16),
             pltpu.VMEM((NC, NI), bf16),
             DMA((2 + SX,)),
         ],
     )(idx, res, basis)
 
 
-def local_body(res_ref, schur_ref, out_ref):
+def local_body(res_ref, schur_ref, _, out_ref):
     for f in range(FACES):
         out_ref[f] = mm(res_ref[...], schur_ref[:, face_cols(f)])
 
 
-def local_kernel(res, schur):
+def local_kernel(res, schur, earlier):
     return call(
         local_body,
         jax.ShapeDtypeStruct((FACES, R, FACE), f32),
         0,
         0,
         vmem=SMALL,
-        in_specs=[VMEM] * 2,
-        out_specs=VMEM,
-    )(res, schur)
+        in_specs=[VMEM, VMEM, ANY],
+        out_specs=VMEM,
+    )(res, schur, earlier)
 
 
 def member_onehot(pack_ref):
@@ -165,24 +168,35 @@
     )(pack, restrict)
 
 
-def map_body(top_inv_ref, restrict_ref, hi_ref, lo_ref):
-    t_hi, t_lo = split(top_inv_ref[...])
+def map_body(top_hbm, restrict_hbm, _, hi_hbm, lo_hbm, top_ref, restrict_ref, hi_ref, lo_ref, sems):
+    for c in started([(top_hbm, top_ref), (restrict_hbm, restrict_ref)], sems.at[pl.ds(0, 2)]):
+        c.wait()
+    t_hi, t_lo = split(top_ref[...])
     r_hi, r_lo = split(restrict_ref[...])
     back = functools.partial(lax.dot_general, dimension_numbers=LAST, preferred_element_type=f32)
     both = back(t_hi, r_hi) + (back(t_hi, r_lo) + back(t_lo, r_hi))
     hi_ref[...], lo_ref[...] = split(both)
-
-
-def map_kernel(top_inv, restrict):
+    for c in started([(hi_ref, hi_hbm), (lo_ref, lo_hbm)], sems.at[pl.ds(2, 2)]):
+        c.wait()
+
+
+def map_kernel(top_inv, restrict, earlier):
     return call(
         map_body,
         (jax.ShapeDtypeStruct((C2, C2), bf16),) * 2,
         0,
         0,
-        vmem=SMALL,
-        in_specs=[VMEM] * 2,
-        out_specs=(VMEM,) * 2,
-    )(top_inv, restrict)
+        vmem=BIG,
+        in_specs=[HBM, HBM, ANY],
+        out_specs=(HBM, HBM),
+        scratch_shapes=[
+            pltpu.VMEM((C2, C2), f32),
+            pltpu.VMEM((C2, C2), f32),
+            pltpu.VMEM((C2, C2), bf16),
+            pltpu.VMEM((C2, C2), bf16),
+            DMA((4,)),
+        ],
+    )(top_inv, restrict, earlier)
 
 
 def own_body(res_ref, group_inv_ref, own_ref):
@@ -224,20 +238,20 @@
     )(pack, own, map_hi, map_lo, *parts)
 
 
-def sum_body(*refs):
-    refs[-1][...] = sum(r[...].astype(f32) for r in refs[:-1]).astype(bf16)
-
-
-def sum_kernel(parts):
-    return call(
-        sum_body,
+def sum_body(count, *refs):
+    refs[-1][...] = sum(r[...].astype(f32) for r in refs[:count]).astype(bf16)
+
+
+def sum_kernel(parts, *earlier):
+    return call(
+        functools.partial(sum_body, len(parts)),
         jax.ShapeDtypeStruct((RZ, C2), bf16),
         0,
         0,
         vmem=4,
-        in_specs=[VMEM] * len(parts),
-        out_specs=VMEM,
-    )(*parts)
+        in_specs=[VMEM] * len(parts) + [ANY] * len(earlier),
+        out_specs=VMEM,
+    )(*parts, *earlier)
 
 
 def send_face(meta_ref, e):
@@ -245,18 +259,25 @@
     return e // 2 * 2 + (odd if e % 2 else 1 - odd)
 
 
+def face_update(meta_ref, e, rows, basis_ref, local_ref, send_ref):
+    f = send_face(meta_ref, e)
+    cols = pl.ds(pl.multiple_of(f * FACE, FACE), FACE)
+    update = local_ref[f] + mm(rows, basis_ref[:, cols])
+    send_ref[...] = swap_halves(update, meta_ref[0, 2 * f] == 1).astype(bf16)
+
+
 def update_body(meta_ref, back_ref, basis_ref, local_ref, *refs):
-    sends, rows_ref = refs[:FACES], refs[FACES]
+    rows_ref = refs[FACES]
     for c in range(SZ):
         for a in range(SX):
             start = (a * SZ + c) * RX
             rows_ref[start : start + RX, :] = back_ref[c, a * RX : (a + 1) * RX, :]
     rows = rows_ref[...]
-    for e in range(FACES):
+    for e, send_ref in zip(ORDER, refs):
         f = send_face(meta_ref, e)
         cols = pl.ds(pl.multiple_of(f * FACE, FACE), FACE)
         update = local_ref[f] + mm(rows, basis_ref[:, cols])
-        sends[e][...] = swap_halves(update, meta_ref[0, 2 * f] == 1).astype(bf16)
+        send_ref[...] = swap_halves(update, meta_ref[0, 2 * f] == 1).astype(bf16)
 
 
 def update_kernel(meta, back, basis, local):
@@ -273,16 +294,16 @@
 
 
 def last_body(meta_ref, *refs):
-    sends, gots = refs[:FACES], refs[FACES : 2 * FACES]
-    out_hbm, out_ref, out_sems = refs[2 * FACES :]
+    out_hbm, out_ref, out_sems = refs[-3:]
     outs = []
-    for e in range(FACES):
+    for i, e in enumerate(ORDER):
         f = send_face(meta_ref, e)
         cols = pl.ds(pl.multiple_of(f * FACE, FACE), FACE)
-        weight = jnp.where(meta_ref[0, 12 + f] == 1, 0.5, 1.0).astype(f32)
-        both = weight * (sends[e][...].astype(f32) + gots[e][...].astype(f32))
-        out_ref[e] = swap_halves(both, meta_ref[0, 2 * f] == 1).astype(bf16)
-        outs += started([(out_ref.at[e], out_hbm.at[:, cols])], out_sems.at[pl.ds(e, 1)])
+        shared = meta_ref[0, 12 + f] == 1
+        own, got = refs[i][...].astype(f32), refs[FACES + i][...].astype(f32)
+        both = jnp.where(shared, 0.5 * (own + got), own)
+        out_ref[i] = swap_halves(both, meta_ref[0, 2 * f] == 1).astype(bf16)
+        outs += started([(out_ref.at[i], out_hbm.at[:, cols])], out_sems.at[pl.ds(i, 1)])
     for c in outs:
         c.wait()
 
@@ -302,10 +323,6 @@
 
 def ring(count, d):
     return [(i, (i + d) % count) for i in range(count)]
-
-
-def after(x, *others):
-    return lax.optimization_barrier((x,) + others)[0]
 
 
 def per_device(
@@ -332,27 +349,25 @@
     facts = jnp.stack([jnp.asarray(v, jnp.int32) for v in facts])
     meta = jnp.concatenate([block_slot.reshape(2 * FACES), facts]).reshape(1, -1)
 
-    pack, res = coarse_kernel(idx, res, basis)
-    local = local_kernel(res, schur)
-    pack = after(lax.all_to_all(pack, "gz", 0, 0), local)
+    pack = coarse_kernel(idx, res, basis)
+    top_map = map_kernel(top_inverse, restrict, pack)
+    pack = lax.optimization_barrier((lax.all_to_all(pack, "gz", 0, 0), top_map[0]))[0]
     group_res, part = group_kernel(pack, restrict)
-    top_map = map_kernel(top_inverse, after(restrict, part))
     own = own_kernel(group_res, group_inv)
     gots = [part] + [lax.ppermute(part, "gx", [(i, i ^ d) for i in range(SX)]) for d in (1, 3, 2)]
-    part = sum_kernel(lax.optimization_barrier((*gots, *top_map))[:SX])
-    got = after(lax.ppermute(part, "gy", [(i, i ^ 1) for i in range(SY)]), own)
-    part = sum_kernel([part, got])
-    part = sum_kernel([part, lax.ppermute(part, "gy", [(i, i ^ 2) for i in range(SY)])])
+    part = sum_kernel(gots)
+    gots = [part] + [lax.ppermute(part, "gy", [(i, i ^ d) for i in range(SY)]) for d in (1, 3, 2)]
+    part = sum_kernel(gots, own)
     parts = [part, lax.ppermute(part, "gy", [(i, SY - 1 - i) for i in range(SY)])]
     back = solve_kernel(pack, own, *top_map, parts)
+    local = local_kernel(res, schur, back)
     back = lax.all_to_all(back, "gz", 0, 0)
     sends = update_kernel(meta, back, basis, local)
     gots = []
-    for axis, count, e in (("gx", SX, 0), ("gy", SY, 2), ("gz", SZ, 4)):
-        near = [(i, i + 1) for i in range(0, count, 2)]
-        far = [(i, i + 1) for i in range(1, count - 1, 2)]
-        for f, pairs in ((e, near), (e + 1, far)):
-            gots.append(lax.ppermute(sends[f], axis, pairs + [(j, i) for i, j in pairs]))
+    for e, send in zip(ORDER, sends):
+        axis, count = (("gx", SX), ("gy", SY), ("gz", SZ))[e // 2]
+        pairs = [(i, (i + 1) % count) for i in range(e % 2, count, 2)]
+        gots.append(lax.ppermute(send, axis, pairs + [(j, i) for i, j in pairs]))
     return last_kernel(meta, sends, gots).reshape(1, 1, 1, R, NI)
 
 

time: 76.9 us -> 70.9 us (0.922)
  the two profiles are of different devices: /device:TPU:131 before, /device:TPU:1 now
where the time goes in v3:
time: 70.9 us; the launch traced here: 70.5 us
  starting transfers between devices  35.7 us (50%)
  Pallas kernels  15.6 us (22%)
  waiting for transfers between devices  15.2 us (21%)
  local copies, waits for them, and re-layouts  3.86 us (5%)
    ppermute x6, starting transfers between devices, per_device(): gots.append(lax.ppermute(send, axis, pairs + [(j, i) for i, j in pairs]))  8.87 us
    all_to_all x1, starting transfers between devices, per_device(): back = lax.all_to_all(back, 'gz', 0, 0)  8.53 us
    all_to_all x1, starting transfers between devices, per_device(): lax.all_to_all(pack, 'gz', 0, 0)  6.53 us
    ppermute x3, starting transfers between devices, per_device(): lax.ppermute(part, 'gy', [(i, i ^ d) for i in range(SY)])  4.53 us
    ppermute x1, starting transfers between devices, per_device(): lax.ppermute(part, 'gy', [(i, SY - 1 - i) for i in range(SY)])  4.15 us
    ppermute x3, waiting for transfers between devices, per_device(): lax.ppermute(part, 'gy', [(i, i ^ d) for i in range(SY)])  3.81 us
    ppermute x6, waiting for transfers between devices, per_device(): gots.append(lax.ppermute(send, axis, pairs + [(j, i) for i, j in pairs]))  3.8 us
    unnamed x16, local copies, waits for them, and re-layouts  3.78 us
  transfers between devices with their start and end apart: 15, of which 9 were waited for; matrix products, arithmetic and copies ran while one was open for 0% of the time, Pallas kernels for 9%

profile of v3, /device:TPU:1, one launch (start us, length us, event | category | flops | bytes accessed | tf_op | source)
XLA Modules:
  0.0 70.5 jit_solution(14903362084328703985)
XLA Ops:
  0.0 0.0 copy-start.2
  0.0 0.0 copy-start.4
  0.0 3.4 %shard_map.82._ = bf16[8,80,128]{2,1,0:T(8,128)(2,1)} custom-call(s32[1,128]{1,0:T(1,128)} %bitcast.28, bf16[512,1536]{1,0:T(8,128)(2,1)} %bitcast.18, bf16[128,1536]{1,0:T(8,128)(2,1)} %bitcast.23), custom_call_target="tpu_custom_call" | custom-call | flops 1024 | bytes 1024 | tf_op jit(solution)/shard_map/pallas_call | solution.py:107
  3.4 6.5 %all-to-all-start = ((bf16[8,80,128]{2,1,0:T(8,128)(2,1)}), bf16[8,80,128]{2,1,0:T(8,128)(2,1)S(1)}, u32[]{:S(2)}, u32[]{:S(2)}) async-start(bf16[8,80,128]{2,1,0:T(8,128)(2,1)} %shard_map.82._), calls=%async_computation | async-start | bytes 327680 | tf_op jit(solution)/shard_map/all_to_all | solution.py:354
  9.9 3.6 %shard_map.83 = (bf16[512,512]{1,0:T(8,128)(2,1)}, bf16[512,512]{1,0:T(8,128)(2,1)}) custom-call(f32[512,512]{1,0:T(8,128)} %top_hbm.1, f32[512,512]{1,0:T(8,128)} %bitcast.21, bf16[8,80,128]{2,1,0:T(8,128)(2,1)} %shard_map.82._), custom_call_target="tpu_custom_call" | custom-call | flops 1024 | bytes 1024 | tf_op jit(solution)/shard_map/pallas_call | solution.py:184
  13.5 0.0 copy-start.5
  13.5 0.0 copy-start.6
  13.6 0.0 copy-start.7
  13.6 2.0 %all-to-all-done.pack_ref = bf16[8,80,128]{2,1,0:T(8,128)(2,1)S(1)} async-done(((bf16[8,80,128]{2,1,0:T(8,128)(2,1)}), bf16[8,80,128]{2,1,0:T(8,128)(2,1)S(1)}, u32[]{:S(2)}, u32[]{:S(2)}) %all-to-all-start) | async-done | bytes 163872 | tf_op jit(solution)/shard_map/all_to_all | solution.py:354
  15.5 0.0 copy-done.2
  15.6 0.8 %shard_map.84 = (f32[64,512]{1,0:T(8,128)S(1)}, bf16[64,512]{1,0:T(8,128)(2,1)S(1)}) custom-call(bf16[8,80,128]{2,1,0:T(8,128)(2,1)S(1)} %all-to-all-done.pack_ref, f32[512,512]{1,0:T(8,128)S(1)} %bitcast.22), custom_call_target="tpu_custom_call" | custom-call | flops 1024 | bytes 1024 | tf_op jit(solution)/shard_map/pallas_call | solution.py:160
  16.4 2.3 %collective-permute-start.2 = (bf16[64,512]{1,0:T(8,128)(2,1)S(1)}, bf16[64,512]{1,0:T(8,128)(2,1)S(1)}, u32[]{:S(2)}, u32[]{:S(2)}) collective-permute-start(bf16[64,512]{1,0:T(8,128)(2,1)S(1)} %get-tuple-element.20.refs_0_), channel_id=1, source_target_pairs={{0,128},{64,192},{128,0},{192,64},{1,129},{65,193},{129,1},{193,65... | collective-permute-start | bytes 196616 | tf_op jit(solution)/shard_map/ppermute | solution.py:357
  18.6 0.9 %collective-permute-start.1 = (bf16[64,512]{1,0:T(8,128)(2,1)S(1)}, bf16[64,512]{1,0:T(8,128)(2,1)S(1)}, u32[]{:S(2)}, u32[]{:S(2)}) collective-permute-start(bf16[64,512]{1,0:T(8,128)(2,1)S(1)} %get-tuple-element.20.refs_0_), channel_id=1, source_target_pairs={{0,192},{64,128},{128,64},{192,0},{1,193},{65,129},{129,65},{193,1... | collective-permute-start | bytes 196616 | tf_op jit(solution)/shard_map/ppermute | solution.py:357
  19.5 0.0 collective-permute-start
  19.5 1.6 %collective-permute-done.2.refs_3_ = bf16[64,512]{1,0:T(8,128)(2,1)S(1)} collective-permute-done((bf16[64,512]{1,0:T(8,128)(2,1)S(1)}, bf16[64,512]{1,0:T(8,128)(2,1)S(1)}, u32[]{:S(2)}, u32[]{:S(2)}) %collective-permute-start.2) | collective-permute-done | bytes 65568 | tf_op jit(solution)/shard_map/ppermute | solution.py:357
  21.1 2.1 %collective-permute-done.1.refs_2_ = bf16[64,512]{1,0:T(8,128)(2,1)S(1)} collective-permute-done((bf16[64,512]{1,0:T(8,128)(2,1)S(1)}, bf16[64,512]{1,0:T(8,128)(2,1)S(1)}, u32[]{:S(2)}, u32[]{:S(2)}) %collective-permute-start.1) | collective-permute-done | bytes 65568 | tf_op jit(solution)/shard_map/ppermute | solution.py:357
  23.1 0.0 collective-permute-done.refs_1_
  23.2 2.9 %collective-permute-start.5 = (bf16[64,512]{1,0:T(8,128)(2,1)S(1)}, bf16[64,512]{1,0:T(8,128)(2,1)S(1)}, u32[]{:S(2)}, u32[]{:S(2)}) collective-permute-start(bf16[64,512]{1,0:T(8,128)(2,1)S(1)} %shard_map.86.refs_0_), channel_id=1, source_target_pairs={{0,16},{8,24},{16,0},{24,8},{32,48},{40,56},{48,32},{56,40},{1,17}... | collective-permute-start | bytes 196616 | tf_op jit(solution)/shard_map/ppermute | solution.py:359
  26.1 1.5 %collective-permute-start.4 = (bf16[64,512]{1,0:T(8,128)(2,1)S(1)}, bf16[64,512]{1,0:T(8,128)(2,1)S(1)}, u32[]{:S(2)}, u32[]{:S(2)}) collective-permute-start(bf16[64,512]{1,0:T(8,128)(2,1)S(1)} %shard_map.86.refs_0_), channel_id=1, source_target_pairs={{0,24},{8,16},{16,8},{24,0},{32,56},{40,48},{48,40},{56,32},{1,25}... | collective-permute-start | bytes 196616 | tf_op jit(solution)/shard_map/ppermute | solution.py:359
  27.5 0.2 collective-permute-start.3
  27.7 0.0 copy-done.4
  27.7 0.4 shard_map.85.refs_4_.own_ref
  28.1 0.0 collective-permute-done.5.refs_3_
  28.1 3.1 %collective-permute-done.4.refs_2_ = bf16[64,512]{1,0:T(8,128)(2,1)S(1)} collective-permute-done((bf16[64,512]{1,0:T(8,128)(2,1)S(1)}, bf16[64,512]{1,0:T(8,128)(2,1)S(1)}, u32[]{:S(2)}, u32[]{:S(2)}) %collective-permute-start.4) | collective-permute-done | bytes 65568 | tf_op jit(solution)/shard_map/ppermute | solution.py:359
  31.2 0.7 %collective-permute-done.3.refs_1_ = bf16[64,512]{1,0:T(8,128)(2,1)S(1)} collective-permute-done((bf16[64,512]{1,0:T(8,128)(2,1)S(1)}, bf16[64,512]{1,0:T(8,128)(2,1)S(1)}, u32[]{:S(2)}, u32[]{:S(2)}) %collective-permute-start.3) | collective-permute-done | bytes 65568 | tf_op jit(solution)/shard_map/ppermute | solution.py:359
  32.0 4.2 %collective-permute-start.6 = (bf16[64,512]{1,0:T(8,128)(2,1)S(1)}, bf16[64,512]{1,0:T(8,128)(2,1)S(1)}, u32[]{:S(2)}, u32[]{:S(2)}) collective-permute-start(bf16[64,512]{1,0:T(8,128)(2,1)S(1)} %shard_map.87.refs_0_), channel_id=1, source_target_pairs={{0,56},{8,48},{16,40},{24,32},{32,24},{40,16},{48,8},{56,0},{1,57}... | collective-permute-start | bytes 196616 | tf_op jit(solution)/shard_map/ppermute | solution.py:361
  36.1 1.9 %collective-permute-done.6.refs_1_ = bf16[64,512]{1,0:T(8,128)(2,1)S(1)} collective-permute-done((bf16[64,512]{1,0:T(8,128)(2,1)S(1)}, bf16[64,512]{1,0:T(8,128)(2,1)S(1)}, u32[]{:S(2)}, u32[]{:S(2)}) %collective-permute-start.6) | collective-permute-done | bytes 65568 | tf_op jit(solution)/shard_map/ppermute | solution.py:361
  38.0 0.0 copy-done.5
  38.0 0.0 copy-done.6
  38.0 1.3 %shard_map.88._ = bf16[8,64,128]{2,1,0:T(8,128)(2,1)} custom-call(bf16[8,80,128]{2,1,0:T(8,128)(2,1)S(1)} %all-to-all-done.pack_ref, f32[64,512]{1,0:T(8,128)S(1)} %shard_map.85.refs_4_.own_ref, bf16[512,512]{1,0:T(8,128)(2,1)S(1)} %copy-done.5, bf16[512,512]{1,0:T(8,128)(2,1)S(1)} %copy-done.6, bf16[64,512]{1,0:T(8,128)(2,1)S(1)} %shard_map.87.refs_0_, ...), custom_call_target="tpu_custom_call" | custom-call | flops 1024 | bytes 1024 | tf_op jit(solution)/shard_map/pallas_call | solution.py:230
  39.3 8.5 %all-to-all-start.1 = ((bf16[8,64,128]{2,1,0:T(8,128)(2,1)}), bf16[8,64,128]{2,1,0:T(8,128)(2,1)}, u32[]{:S(2)}, u32[]{:S(2)}) async-start(bf16[8,64,128]{2,1,0:T(8,128)(2,1)} %shard_map.88._), calls=%async_computation.1 | async-start | bytes 262144 | tf_op jit(solution)/shard_map/all_to_all | solution.py:364
  47.9 0.0 copy-done.7
  47.9 0.1 concatenate.3
  48.0 0.0 copy-start
  48.0 1.4 %copy-done = bf16[1,1,1,512,1536]{4,3,2,1,0:T(8,128)(2,1)S(1)} copy-done((bf16[1,1,1,512,1536]{4,3,2,1,0:T(8,128)(2,1)S(1)}, bf16[1,1,1,512,1536]{4,3,2,1,0:T(8,128)(2,1)}, u32[]{:S(2)}) %copy-start) | copy-done | bytes 1572888
  49.4 0.0 copy-start.1
  49.4 2.3 %copy-done.1 = bf16[1,1,1,1536,1536]{4,3,2,1,0:T(8,128)(2,1)S(1)} copy-done((bf16[1,1,1,1536,1536]{4,3,2,1,0:T(8,128)(2,1)S(1)}, bf16[1,1,1,1536,1536]{4,3,2,1,0:T(8,128)(2,1)}, u32[]{:S(2)}) %copy-start.1) | copy-done | bytes 4718616
  51.7 0.0 copy-start.3
  51.7 2.6 %shard_map.89.local_ref = f32[6,512,256]{2,1,0:T(8,128)S(1)} custom-call(bf16[512,1536]{1,0:T(8,128)(2,1)S(1)} %bitcast.19, bf16[1536,1536]{1,0:T(8,128)(2,1)S(1)} %bitcast.20, bf16[8,64,128]{2,1,0:T(8,128)(2,1)} %shard_map.88._), custom_call_target="tpu_custom_call" | custom-call | flops 1024 | bytes 1024 | tf_op jit(solution)/shard_map/pallas_call | solution.py:130
  54.3 0.0 all-to-all-done.1.back_ref
  54.3 0.0 copy-done.3
  54.3 1.5 %shard_map.90 = (bf16[512,256]{1,0:T(8,128)(2,1)S(1)}, bf16[512,256]{1,0:T(8,128)(2,1)S(1)}, bf16[512,256]{1,0:T(8,128)(2,1)S(1)}, bf16[512,256]{1,0:T(8,128)(2,...) custom-call(s32[1,21]{1,0:T(1,128)S(1)} %bitcast.26, bf16[8,64,128]{2,1,0:T(8,128)(2,1)} %all-to-all-done.1.back_ref, ...), custom_call_target="tpu_custom_call" | custom-call | flops 1024 | bytes 1024 | tf_op jit(solution)/shard_map/pallas_call | solution.py:284
  55.8 0.1 collective-permute-start.7
  55.9 0.1 collective-permute-start.8
  56.0 1.8 %collective-permute-start.9 = (bf16[512,256]{1,0:T(8,128)(2,1)S(1)}, bf16[512,256]{1,0:T(8,128)(2,1)S(1)}, u32[]{:S(2)}, u32[]{:S(2)}) collective-permute-start(bf16[512,256]{1,0:T(8,128)(2,1)S(1)} %get-tuple-element.23.refs_2_), channel_id=1, source_target_pairs={{64,128},{192,0},{128,64},{0,192},{65,129},{193,1},{129,65},{1,193... | collective-permute-start | bytes 786440 | tf_op jit(solution)/shard_map/ppermute | solution.py:370
  57.9 3.8 %collective-permute-start.10 = (bf16[512,256]{1,0:T(8,128)(2,1)S(1)}, bf16[512,256]{1,0:T(8,128)(2,1)S(1)}, u32[]{:S(2)}, u32[]{:S(2)}) collective-permute-start(bf16[512,256]{1,0:T(8,128)(2,1)S(1)} %get-tuple-element.24.refs_3_), channel_id=1, source_target_pairs={{8,16},{24,32},{40,48},{56,0},{16,8},{32,24},{48,40},{0,56},{9,17}... | collective-permute-start | bytes 786440 | tf_op jit(solution)/shard_map/ppermute | solution.py:370
  61.7 2.5 %collective-permute-start.11 = (bf16[512,256]{1,0:T(8,128)(2,1)S(1)}, bf16[512,256]{1,0:T(8,128)(2,1)S(1)}, u32[]{:S(2)}, u32[]{:S(2)}) collective-permute-start(bf16[512,256]{1,0:T(8,128)(2,1)S(1)} %get-tuple-element.25.refs_4_), channel_id=1, source_target_pairs={{1,2},{3,4},{5,6},{7,0},{2,1},{4,3},{6,5},{0,7},{9,10},{11,12},{13... | collective-permute-start | bytes 786440 | tf_op jit(solution)/shard_map/ppermute | solution.py:370
  64.2 0.0 collective-permute-done.7.refs_6_
  64.2 0.5 collective-permute-start.12
  64.7 0.0 collective-permute-done.8.refs_7_
  64.7 0.1 collective-permute-done.9.refs_8_
  64.9 2.8 %collective-permute-done.10.refs_9_ = bf16[512,256]{1,0:T(8,128)(2,1)S(1)} collective-permute-done((bf16[512,256]{1,0:T(8,128)(2,1)S(1)}, bf16[512,256]{1,0:T(8,128)(2,1)S(1)}, u32[]{:S(2)}, u32[]{:S(2)}) %collective-permute-start.10) | collective-permute-done | bytes 262176 | tf_op jit(solution)/shard_map/ppermute | solution.py:370
  67.6 0.9 %collective-permute-done.11.refs_10_ = bf16[512,256]{1,0:T(8,128)(2,1)S(1)} collective-permute-done((bf16[512,256]{1,0:T(8,128)(2,1)S(1)}, bf16[512,256]{1,0:T(8,128)(2,1)S(1)}, u32[]{:S(2)}, u32[]{:S(2)}) %collective-permute-start.11) | collective-permute-done | bytes 262176 | tf_op jit(solution)/shard_map/ppermute | solution.py:370
  68.5 0.0 collective-permute-done.12.refs_11_
  68.5 2.0 %shard_map.91 = bf16[512,1536]{1,0:T(8,128)(2,1)} custom-call(s32[1,21]{1,0:T(1,128)S(1)} %bitcast.27, bf16[512,256]{1,0:T(8,128)(2,1)S(1)} %get-tuple-element.21.refs_0_, bf16[512,256]{1,0:T(8,128)(2,1)S(1)} %get-tuple-element.22.refs_1_, bf16[512,256]{1,0:T(8,128)(2,1)S(1)} %get-tuple-element.23.refs_2_, bf16[512,256]{1,0:T(8,128)(2,1)S(1)} %get-tuple-element.24.refs_3_, ...), custom_call_target="tpu_custom_call" | custom-call | flops 1024 | bytes 1024 | tf_op jit(solution)/shard_map/pallas_call | solution.py:312
  (2 shorter events, 0.1 us)
Async XLA Ops:
  0.0 15.5 %copy-start.2 = (f32[1,1,512,512]{3,2,1,0:T(8,128)S(1)}, f32[1,1,512,512]{3,2,1,0:T(8,128)}, u32[]{:S(2)}) copy-start(f32[1,1,512,512]{3,2,1,0:T(8,128)} %param.14) | copy-start | bytes 3145732
  0.0 27.7 %copy-start.4 = (f32[1,1,512,512]{3,2,1,0:T(8,128)S(1)}, f32[1,1,512,512]{3,2,1,0:T(8,128)}, u32[]{:S(2)}) copy-start(f32[1,1,512,512]{3,2,1,0:T(8,128)} %param.13) | copy-start | bytes 3145732
  3.4 12.1 %all-to-all-start = ((bf16[8,80,128]{2,1,0:T(8,128)(2,1)}), bf16[8,80,128]{2,1,0:T(8,128)(2,1)S(1)}, u32[]{:S(2)}, u32[]{:S(2)}) async-start(bf16[8,80,128]{2,1,0:T(8,128)(2,1)} %shard_map.82._), calls=%async_computation | async-start | bytes 327680 | tf_op jit(solution)/shard_map/all_to_all | solution.py:354
  13.5 24.5 %copy-start.5 = (bf16[512,512]{1,0:T(8,128)(2,1)S(1)}, bf16[512,512]{1,0:T(8,128)(2,1)}, u32[]{:S(2)}) copy-start(bf16[512,512]{1,0:T(8,128)(2,1)} %get-tuple-element.16.hi_ref) | copy-start | bytes 1572868
  13.5 24.5 %copy-start.6 = (bf16[512,512]{1,0:T(8,128)(2,1)S(1)}, bf16[512,512]{1,0:T(8,128)(2,1)}, u32[]{:S(2)}) copy-start(bf16[512,512]{1,0:T(8,128)(2,1)} %get-tuple-element.19.lo_ref) | copy-start | bytes 1572868
  13.6 34.3 %copy-start.7 = (s32[1,1,1,12]{3,2,1,0:T(1,128)S(1)}, s32[1,1,1,12]{3,2,1,0:T(1,128)}, u32[]{:S(2)}) copy-start(s32[1,1,1,12]{3,2,1,0:T(1,128)} %param.12) | copy-start | bytes 148
  16.4 4.7 %collective-permute-start.2 = (bf16[64,512]{1,0:T(8,128)(2,1)S(1)}, bf16[64,512]{1,0:T(8,128)(2,1)S(1)}, u32[]{:S(2)}, u32[]{:S(2)}) collective-permute-start(bf16[64,512]{1,0:T(8,128)(2,1)S(1)} %get-tuple-element.20.refs_0_), channel_id=1, source_target_pairs={{0,128},{64,192},{128,0},{192,64},{1,129},{65,193},{129,1},{193,65... | collective-permute-start | bytes 196616 | tf_op jit(solution)/shard_map/ppermute | solution.py:357
  18.6 4.5 %collective-permute-start.1 = (bf16[64,512]{1,0:T(8,128)(2,1)S(1)}, bf16[64,512]{1,0:T(8,128)(2,1)S(1)}, u32[]{:S(2)}, u32[]{:S(2)}) collective-permute-start(bf16[64,512]{1,0:T(8,128)(2,1)S(1)} %get-tuple-element.20.refs_0_), channel_id=1, source_target_pairs={{0,192},{64,128},{128,64},{192,0},{1,193},{65,129},{129,65},{193,1... | collective-permute-start | bytes 196616 | tf_op jit(solution)/shard_map/ppermute | solution.py:357
  19.5 3.7 %collective-permute-start = (bf16[64,512]{1,0:T(8,128)(2,1)S(1)}, bf16[64,512]{1,0:T(8,128)(2,1)S(1)}, u32[]{:S(2)}, u32[]{:S(2)}) collective-permute-start(bf16[64,512]{1,0:T(8,128)(2,1)S(1)} %get-tuple-element.20.refs_0_), channel_id=1, source_target_pairs={{0,64},{64,0},{128,192},{192,128},{1,65},{65,1},{129,193},{193,129... | collective-permute-start | bytes 196616 | tf_op jit(solution)/shard_map/ppermute | solution.py:357
  23.2 4.9 %collective-permute-start.5 = (bf16[64,512]{1,0:T(8,128)(2,1)S(1)}, bf16[64,512]{1,0:T(8,128)(2,1)S(1)}, u32[]{:S(2)}, u32[]{:S(2)}) collective-permute-start(bf16[64,512]{1,0:T(8,128)(2,1)S(1)} %shard_map.86.refs_0_), channel_id=1, source_target_pairs={{0,16},{8,24},{16,0},{24,8},{32,48},{40,56},{48,32},{56,40},{1,17}... | collective-permute-start | bytes 196616 | tf_op jit(solution)/shard_map/ppermute | solution.py:359
  26.1 5.2 %collective-permute-start.4 = (bf16[64,512]{1,0:T(8,128)(2,1)S(1)}, bf16[64,512]{1,0:T(8,128)(2,1)S(1)}, u32[]{:S(2)}, u32[]{:S(2)}) collective-permute-start(bf16[64,512]{1,0:T(8,128)(2,1)S(1)} %shard_map.86.refs_0_), channel_id=1, source_target_pairs={{0,24},{8,16},{16,8},{24,0},{32,56},{40,48},{48,40},{56,32},{1,25}... | collective-permute-start | bytes 196616 | tf_op jit(solution)/shard_map/ppermute | solution.py:359
  27.5 4.4 %collective-permute-start.3 = (bf16[64,512]{1,0:T(8,128)(2,1)S(1)}, bf16[64,512]{1,0:T(8,128)(2,1)S(1)}, u32[]{:S(2)}, u32[]{:S(2)}) collective-permute-start(bf16[64,512]{1,0:T(8,128)(2,1)S(1)} %shard_map.86.refs_0_), channel_id=1, source_target_pairs={{0,8},{8,0},{16,24},{24,16},{32,40},{40,32},{48,56},{56,48},{1,9},... | collective-permute-start | bytes 196616 | tf_op jit(solution)/shard_map/ppermute | solution.py:359
  32.0 6.1 %collective-permute-start.6 = (bf16[64,512]{1,0:T(8,128)(2,1)S(1)}, bf16[64,512]{1,0:T(8,128)(2,1)S(1)}, u32[]{:S(2)}, u32[]{:S(2)}) collective-permute-start(bf16[64,512]{1,0:T(8,128)(2,1)S(1)} %shard_map.87.refs_0_), channel_id=1, source_target_pairs={{0,56},{8,48},{16,40},{24,32},{32,24},{40,16},{48,8},{56,0},{1,57}... | collective-permute-start | bytes 196616 | tf_op jit(solution)/shard_map/ppermute | solution.py:361
  39.3 15.0 %all-to-all-start.1 = ((bf16[8,64,128]{2,1,0:T(8,128)(2,1)}), bf16[8,64,128]{2,1,0:T(8,128)(2,1)}, u32[]{:S(2)}, u32[]{:S(2)}) async-start(bf16[8,64,128]{2,1,0:T(8,128)(2,1)} %shard_map.88._), calls=%async_computation.1 | async-start | bytes 262144 | tf_op jit(solution)/shard_map/all_to_all | solution.py:364
  48.0 1.4 %copy-start = (bf16[1,1,1,512,1536]{4,3,2,1,0:T(8,128)(2,1)S(1)}, bf16[1,1,1,512,1536]{4,3,2,1,0:T(8,128)(2,1)}, u32[]{:S(2)}) copy-start(bf16[1,1,1,512,1536]{4,3,2,1,0:T(8,128)(2,1)} %param.8) | copy-start | bytes 4718596
  49.4 2.3 %copy-start.1 = (bf16[1,1,1,1536,1536]{4,3,2,1,0:T(8,128)(2,1)S(1)}, bf16[1,1,1,1536,1536]{4,3,2,1,0:T(8,128)(2,1)}, u32[]{:S(2)}) copy-start(bf16[1,1,1,1536,1536]{4,3,2,1,0:T(8,128)(2,1)} %param.9) | copy-start | bytes 14155780
  51.7 2.6 %copy-start.3 = (bf16[1,1,1,128,1536]{4,3,2,1,0:T(8,128)(2,1)S(1)}, bf16[1,1,1,128,1536]{4,3,2,1,0:T(8,128)(2,1)}, u32[]{:S(2)}) copy-start(bf16[1,1,1,128,1536]{4,3,2,1,0:T(8,128)(2,1)} %param.10) | copy-start | bytes 1179652
  55.8 8.3 %collective-permute-start.7 = (bf16[512,256]{1,0:T(8,128)(2,1)S(1)}, bf16[512,256]{1,0:T(8,128)(2,1)S(1)}, u32[]{:S(2)}, u32[]{:S(2)}) collective-permute-start(bf16[512,256]{1,0:T(8,128)(2,1)S(1)} %get-tuple-element.21.refs_0_), channel_id=1, source_target_pairs={{0,64},{128,192},{64,0},{192,128},{1,65},{129,193},{65,1},{193,129... | collective-permute-start | bytes 786440 | tf_op jit(solution)/shard_map/ppermute | solution.py:370
  55.9 8.8 %collective-permute-start.8 = (bf16[512,256]{1,0:T(8,128)(2,1)S(1)}, bf16[512,256]{1,0:T(8,128)(2,1)S(1)}, u32[]{:S(2)}, u32[]{:S(2)}) collective-permute-start(bf16[512,256]{1,0:T(8,128)(2,1)S(1)} %get-tuple-element.22.refs_1_), channel_id=1, source_target_pairs={{0,8},{16,24},{32,40},{48,56},{8,0},{24,16},{40,32},{56,48},{1,9},... | collective-permute-start | bytes 786440 | tf_op jit(solution)/shard_map/ppermute | solution.py:370
  56.0 8.8 %collective-permute-start.9 = (bf16[512,256]{1,0:T(8,128)(2,1)S(1)}, bf16[512,256]{1,0:T(8,128)(2,1)S(1)}, u32[]{:S(2)}, u32[]{:S(2)}) collective-permute-start(bf16[512,256]{1,0:T(8,128)(2,1)S(1)} %get-tuple-element.23.refs_2_), channel_id=1, source_target_pairs={{64,128},{192,0},{128,64},{0,192},{65,129},{193,1},{129,65},{1,193... | collective-permute-start | bytes 786440 | tf_op jit(solution)/shard_map/ppermute | solution.py:370
  57.9 9.8 %collective-permute-start.10 = (bf16[512,256]{1,0:T(8,128)(2,1)S(1)}, bf16[512,256]{1,0:T(8,128)(2,1)S(1)}, u32[]{:S(2)}, u32[]{:S(2)}) collective-permute-start(bf16[512,256]{1,0:T(8,128)(2,1)S(1)} %get-tuple-element.24.refs_3_), channel_id=1, source_target_pairs={{8,16},{24,32},{40,48},{56,0},{16,8},{32,24},{48,40},{0,56},{9,17}... | collective-permute-start | bytes 786440 | tf_op jit(solution)/shard_map/ppermute | solution.py:370
  61.7 6.8 %collective-permute-start.11 = (bf16[512,256]{1,0:T(8,128)(2,1)S(1)}, bf16[512,256]{1,0:T(8,128)(2,1)S(1)}, u32[]{:S(2)}, u32[]{:S(2)}) collective-permute-start(bf16[512,256]{1,0:T(8,128)(2,1)S(1)} %get-tuple-element.25.refs_4_), channel_id=1, source_target_pairs={{1,2},{3,4},{5,6},{7,0},{2,1},{4,3},{6,5},{0,7},{9,10},{11,12},{13... | collective-permute-start | bytes 786440 | tf_op jit(solution)/shard_map/ppermute | solution.py:370
  64.2 4.3 %collective-permute-start.12 = (bf16[512,256]{1,0:T(8,128)(2,1)S(1)}, bf16[512,256]{1,0:T(8,128)(2,1)S(1)}, u32[]{:S(2)}, u32[]{:S(2)}) collective-permute-start(bf16[512,256]{1,0:T(8,128)(2,1)S(1)} %get-tuple-element.26.refs_5_), channel_id=1, source_target_pairs={{0,1},{2,3},{4,5},{6,7},{1,0},{3,2},{5,4},{7,6},{8,9},{10,11},{12,... | collective-permute-start | bytes 786440 | tf_op jit(solution)/shard_map/ppermute | solution.py:370

commit v4 on v3

--- a/solution.py
+++ b/solution.py
@@ -23,7 +23,7 @@
 COST = 1024
 BIG = 58
 SMALL = 6
-ORDER = (0, 2, 1, 3, 5, 4)
+SLOTS = ((0, True), (1, True), (0, False), (1, False), (2, False), (2, True))
 CHIPS = SZ // 2
 
 LAST = (((1,), (1,)), ((), ()))
@@ -47,8 +47,8 @@
     return mm(a_hi, b_hi) + (mm(a_hi, b_lo) + mm(a_lo, b_hi))
 
 
-def swap_halves(x, swap):
-    return jnp.where(swap, jnp.concatenate([x[:, BW:], x[:, :BW]], axis=1), x)
+def block_cols(block):
+    return pl.ds(pl.multiple_of(block * BW, BW), BW)
 
 
 def call(body, out_shape, flops, size, vmem, **kw):
@@ -81,21 +81,13 @@
 
 
 def coarse_body(idx_hbm, res_hbm, basis_hbm, out_ref, idx_ref, res_ref, basis_ref, sems):
-    rows = R // SX
-    pairs = [(basis_hbm, basis_ref)]
+    copies = started([(idx_hbm, idx_ref), (basis_hbm, basis_ref), (res_hbm, res_ref)], sems)
+    for c in copies:
+        c.wait()
+    part = lax.dot_general(res_ref[...], basis_ref[...], LAST, preferred_element_type=f32)
+    part = part.astype(bf16).reshape(SX, SZ, RX, NC)
     for a in range(SX):
-        part = pl.ds(a * rows, rows)
-        pairs.append((res_hbm.at[part], res_ref.at[part]))
-    pairs.append((idx_hbm, idx_ref))
-    copies = started(pairs, sems)
-    copies[0].wait()
-    for a in range(SX):
-        copies[1 + a].wait()
-        part = lax.dot_general(
-            res_ref[a * rows : (a + 1) * rows, :], basis_ref[...], LAST, preferred_element_type=f32
-        )
-        out_ref[:, a * RX : (a + 1) * RX, :] = part.astype(bf16).reshape(SZ, RX, NC)
-    copies[1 + SX].wait()
+        out_ref[:, a * RX : (a + 1) * RX, :] = part[a]
     idx = idx_ref[...]
     row = lax.broadcasted_iota(jnp.int32, (TAIL, NC), 0)
     digits = jnp.where(row == 0, idx >> 4, jnp.where(row == 1, idx & (BASE - 1), 0))
@@ -116,20 +108,20 @@
             pltpu.VMEM((1, NC), jnp.int32),
             pltpu.VMEM((R, NI), bf16),
             pltpu.VMEM((NC, NI), bf16),
-            DMA((2 + SX,)),
+            DMA((3,)),
         ],
     )(idx, res, basis)
 
 
 def local_body(res_ref, schur_ref, _, out_ref):
     for f in range(FACES):
-        out_ref[f] = mm(res_ref[...], schur_ref[:, face_cols(f)])
+        out_ref[f] = mm(res_ref[...], schur_ref[:, face_cols(f)]).astype(bf16)
 
 
 def local_kernel(res, schur, earlier):
     return call(
         local_body,
-        jax.ShapeDtypeStruct((FACES, R, FACE), f32),
+        jax.ShapeDtypeStruct((FACES, R, FACE), bf16),
         0,
         0,
         vmem=SMALL,
@@ -199,31 +191,37 @@
     )(top_inv, restrict, earlier)
 
 
-def own_body(res_ref, group_inv_ref, own_ref):
+def own_body(res_ref, group_inv_ref, _, own_ref):
     own_ref[...] = mm3(res_ref[...], group_inv_ref[...])
 
 
-def own_kernel(group_res, group_inv):
+def own_kernel(group_res, group_inv, later):
     return call(
         own_body,
         jax.ShapeDtypeStruct((RZ, C2), f32),
         0,
         0,
         vmem=SMALL,
-        in_specs=[VMEM] * 2,
+        in_specs=[VMEM] * 3,
         out_specs=VMEM,
-    )(group_res, group_inv)
+    )(group_res, group_inv, later)
 
 
 def solve_body(pack_ref, own_ref, hi_ref, lo_ref, *refs):
-    parts, out_ref = refs[:-1], refs[-1]
+    parts, (out_hbm, out_ref, sems) = refs[:-3], refs[-3:]
     onehot = member_onehot(pack_ref)
     top_res = sum(p[...].astype(f32) for p in parts)
     t_hi, t_lo = split(top_res)
     sol = own_ref[...] + mm(t_hi, hi_ref[...]) + (mm(t_hi, lo_ref[...]) + mm(t_lo, hi_ref[...]))
-    picked = mm(sol.astype(bf16), onehot).astype(bf16)
-    for c in range(SZ):
-        out_ref[c] = picked[:, c * NC : (c + 1) * NC]
+    sol = sol.astype(bf16)
+    outs = []
+    for i in range(SZ // 2):
+        picked = mm(sol, onehot[:, 2 * i * NC : (2 * i + 2) * NC]).astype(bf16)
+        out_ref[2 * i], out_ref[2 * i + 1] = picked[:, :NC], picked[:, NC:]
+        pair = pl.ds(2 * i, 2)
+        outs += started([(out_ref.at[pair], out_hbm.at[pair])], sems.at[pl.ds(i, 1)])
+    for c in outs:
+        c.wait()
 
 
 def solve_kernel(pack, own, map_hi, map_lo, parts):
@@ -234,7 +232,8 @@
         0,
         vmem=8,
         in_specs=[VMEM] * (4 + len(parts)),
-        out_specs=VMEM,
+        out_specs=HBM,
+        scratch_shapes=[pltpu.VMEM((SZ, RZ, NC), bf16), DMA((SZ // 2,))],
     )(pack, own, map_hi, map_lo, *parts)
 
 
@@ -254,16 +253,12 @@
     )(*parts, *earlier)
 
 
-def send_face(meta_ref, e):
-    odd = meta_ref[0, 18 + e // 2]
-    return e // 2 * 2 + (odd if e % 2 else 1 - odd)
-
-
-def face_update(meta_ref, e, rows, basis_ref, local_ref, send_ref):
-    f = send_face(meta_ref, e)
-    cols = pl.ds(pl.multiple_of(f * FACE, FACE), FACE)
-    update = local_ref[f] + mm(rows, basis_ref[:, cols])
-    send_ref[...] = swap_halves(update, meta_ref[0, 2 * f] == 1).astype(bf16)
+def send_face(meta_ref, slot):
+    axis, near = SLOTS[slot]
+    if axis != 2:
+        axis = axis ^ meta_ref[0, 20]
+    odd = meta_ref[0, 18 + axis]
+    return 2 * axis + (1 - odd if near else odd)
 
 
 def update_body(meta_ref, back_ref, basis_ref, local_ref, *refs):
@@ -273,11 +268,12 @@
             start = (a * SZ + c) * RX
             rows_ref[start : start + RX, :] = back_ref[c, a * RX : (a + 1) * RX, :]
     rows = rows_ref[...]
-    for e, send_ref in zip(ORDER, refs):
+    for e, send_ref in enumerate(refs[:FACES]):
         f = send_face(meta_ref, e)
         cols = pl.ds(pl.multiple_of(f * FACE, FACE), FACE)
-        update = local_ref[f] + mm(rows, basis_ref[:, cols])
-        send_ref[...] = swap_halves(update, meta_ref[0, 2 * f] == 1).astype(bf16)
+        update = local_ref[f].astype(f32) + mm(rows, basis_ref[:, cols])
+        turned = jnp.concatenate([update[:, BW:], update[:, :BW]], axis=1)
+        send_ref[...] = jnp.where(meta_ref[0, 2 * f] == 1, turned, update).astype(bf16)
 
 
 def update_kernel(meta, back, basis, local):
@@ -293,36 +289,64 @@
     )(meta, back, basis, local)
 
 
-def last_body(meta_ref, *refs):
+def last_body(slots, meta_ref, *refs):
+    count = len(slots)
     out_hbm, out_ref, out_sems = refs[-3:]
     outs = []
-    for i, e in enumerate(ORDER):
-        f = send_face(meta_ref, e)
-        cols = pl.ds(pl.multiple_of(f * FACE, FACE), FACE)
-        shared = meta_ref[0, 12 + f] == 1
-        own, got = refs[i][...].astype(f32), refs[FACES + i][...].astype(f32)
-        both = jnp.where(shared, 0.5 * (own + got), own)
-        out_ref[i] = swap_halves(both, meta_ref[0, 2 * f] == 1).astype(bf16)
-        outs += started([(out_ref.at[i], out_hbm.at[:, cols])], out_sems.at[pl.ds(i, 1)])
+    for i, slot in enumerate(slots):
+        f = send_face(meta_ref, slot)
+        own = refs[i][...]
+        both = (own + refs[count + i][...]) * jnp.asarray(0.5, bf16)
+        out_ref[i] = jnp.where(meta_ref[0, 12 + f] == 1, both, own)
+        pairs = []
+        for k in range(2):
+            block = 2 * f + meta_ref[0, 2 * f + k]
+            pairs.append((out_ref.at[i, :, pl.ds(k * BW, BW)], out_hbm.at[:, block_cols(block)]))
+        outs += started(pairs, out_sems.at[pl.ds(2 * i, 2)])
     for c in outs:
         c.wait()
 
 
-def last_kernel(meta, sends, gots):
-    return call(
-        last_body,
+def last_kernel(slots, meta, sends, gots, *partial):
+    count = len(slots)
+    return call(
+        functools.partial(last_body, slots),
         jax.ShapeDtypeStruct((R, NI), bf16),
         0,
         0,
         vmem=SMALL,
-        in_specs=[SMEM] + [VMEM] * (2 * FACES),
+        in_specs=[SMEM] + [VMEM] * (2 * count) + [HBM] * len(partial),
         out_specs=HBM,
-        scratch_shapes=[pltpu.VMEM((FACES, R, FACE), bf16), DMA((FACES,))],
-    )(meta, *sends, *gots)
-
-
-def ring(count, d):
-    return [(i, (i + d) % count) for i in range(count)]
+        input_output_aliases={1 + 2 * count: 0} if partial else {},
+        scratch_shapes=[pltpu.VMEM((count, R, FACE), bf16), DMA((2 * count,))],
+    )(meta, *[sends[i] for i in slots], *[gots[i] for i in slots], *partial)
+
+
+def permute(x, target):
+    pairs = []
+    for a in range(SX):
+        for b in range(SY):
+            for c in range(SZ):
+                ta, tb, tc = target(a, b, c)
+                pairs.append(((a * SY + b) * SZ + c, (ta * SY + tb) * SZ + tc))
+    return lax.ppermute(x, ("gx", "gy", "gz"), pairs)
+
+
+def group_of_four(a, b, c, d, turn):
+    return (a ^ d, b, c) if c % 2 == turn else (a, b ^ d, c)
+
+
+def beside(at, count, near):
+    return at ^ 1 if near else ((at + 1) ^ 1) - 1 if 0 < at < count - 1 else count - 1 - at
+
+
+def face_target(a, b, c, slot):
+    axis, near = SLOTS[slot]
+    if axis == 2:
+        return a, b, beside(c, SZ, near)
+    if axis == c % 2:
+        return beside(a, SX, near), b, c
+    return a, beside(b, SY, near), c
 
 
 def per_device(
@@ -353,22 +377,21 @@
     top_map = map_kernel(top_inverse, restrict, pack)
     pack = lax.optimization_barrier((lax.all_to_all(pack, "gz", 0, 0), top_map[0]))[0]
     group_res, part = group_kernel(pack, restrict)
-    own = own_kernel(group_res, group_inv)
-    gots = [part] + [lax.ppermute(part, "gx", [(i, i ^ d) for i in range(SX)]) for d in (1, 3, 2)]
-    part = sum_kernel(gots)
-    gots = [part] + [lax.ppermute(part, "gy", [(i, i ^ d) for i in range(SY)]) for d in (1, 3, 2)]
-    part = sum_kernel(gots, own)
-    parts = [part, lax.ppermute(part, "gy", [(i, SY - 1 - i) for i in range(SY)])]
+    own = own_kernel(group_res, group_inv, res)
+    for turn, earlier in ((0, ()), (1, (own,))):
+        gots = [part]
+        for d in (1, 3, 2):
+            gots.append(permute(part, functools.partial(group_of_four, d=d, turn=turn)))
+        part = sum_kernel(gots, *earlier)
+    parts = [part, permute(part, lambda a, b, c: (a, SY - 1 - b, c))]
     back = solve_kernel(pack, own, *top_map, parts)
     local = local_kernel(res, schur, back)
     back = lax.all_to_all(back, "gz", 0, 0)
     sends = update_kernel(meta, back, basis, local)
-    gots = []
-    for e, send in zip(ORDER, sends):
-        axis, count = (("gx", SX), ("gy", SY), ("gz", SZ))[e // 2]
-        pairs = [(i, (i + 1) % count) for i in range(e % 2, count, 2)]
-        gots.append(lax.ppermute(send, axis, pairs + [(j, i) for i, j in pairs]))
-    return last_kernel(meta, sends, gots).reshape(1, 1, 1, R, NI)
+    gots = [permute(x, functools.partial(face_target, slot=i)) for i, x in enumerate(sends)]
+    out = last_kernel((0, 1), meta, sends, gots)
+    out = last_kernel((2, 3, 4, 5), meta, sends, gots, out)
+    return out.reshape(1, 1, 1, R, NI)
 
 
 def solution(mesh):

time: 70.9 us -> 69 us (0.973)
  local copies, waits for them, and re-layouts: 3.86 us -> 2.46 us
  waiting for transfers between devices: 15.2 us -> 13.8 us
    ppermute x13, waiting for transfers between devices: 13.2 us -> 11.6 us  [permute(): return lax.ppermute(x, ('gx', 'gy', 'gz'), pairs)]
    unnamed x16, local copies, waits for them, and re-layouts: 3.78 us -> 2.37 us
    pallas_call x2 -> x3, Pallas kernels: 4.55 us -> 5.6 us  [the longest x2 3 us: last_kernel(): call(functools.partial(last_body, slots), jax.ShapeDtypeStruct((R, NI), b...]
  transfers between devices with their start and end apart: 15 -> 15, of which waited for: 9 -> 8; matrix products, arithmetic and copies ran while one was open for 0% -> 0% of each run, Pallas kernels for 9% -> 12%
where the time goes in v4:
time: 69 us; the launch traced here: 68.6 us
  starting transfers between devices  36 us (52%)
  Pallas kernels  16.2 us (23%)
  waiting for transfers between devices  13.8 us (20%)
  local copies, waits for them, and re-layouts  2.46 us (4%)
    ppermute x13, starting transfers between devices, permute(): return lax.ppermute(x, ('gx', 'gy', 'gz'), pairs)  20.7 us
    ppermute x13, waiting for transfers between devices, permute(): return lax.ppermute(x, ('gx', 'gy', 'gz'), pairs)  11.6 us
    all_to_all x1, starting transfers between devices, per_device(): back = lax.all_to_all(back, 'gz', 0, 0)  8.63 us
    all_to_all x1, starting transfers between devices, per_device(): lax.all_to_all(pack, 'gz', 0, 0)  6.67 us
    pallas_call x1, Pallas kernels, map_kernel(): call(map_body, (jax.ShapeDtypeStruct((C2, C2), bf16),) * 2, 0, 0, vmem=BI...  3.7 us
    pallas_call x2, Pallas kernels, last_kernel(): call(functools.partial(last_body, slots), jax.ShapeDtypeStruct((R, NI), b...  3 us
    pallas_call x1, Pallas kernels, coarse_kernel(): call(coarse_body, jax.ShapeDtypeStruct((SZ, PACK, NC), bf16), 0, 0, vmem=...  2.82 us
    pallas_call x1, Pallas kernels, local_kernel(): call(local_body, jax.ShapeDtypeStruct((FACES, R, FACE), bf16), 0, 0, vmem...  2.59 us
  transfers between devices with their start and end apart: 15, of which 8 were waited for; matrix products, arithmetic and copies ran while one was open for 0% of the time, Pallas kernels for 12%

profile of v4, /device:TPU:1, one launch (start us, length us, event | category | flops | bytes accessed | tf_op | source)
XLA Modules:
  0.0 68.6 jit_solution(566411889503381528)
XLA Ops:
  0.0 2.8 %shard_map.82._ = bf16[8,80,128]{2,1,0:T(8,128)(2,1)} custom-call(s32[1,128]{1,0:T(1,128)} %bitcast.30, bf16[512,1536]{1,0:T(8,128)(2,1)} %bitcast.18, bf16[128,1536]{1,0:T(8,128)(2,1)} %bitcast.24), custom_call_target="tpu_custom_call" | custom-call | flops 1024 | bytes 1024 | tf_op jit(solution)/shard_map/pallas_call | solution.py:99
  2.8 0.0 copy-start.2
  2.8 6.7 %all-to-all-start = ((bf16[8,80,128]{2,1,0:T(8,128)(2,1)}), bf16[8,80,128]{2,1,0:T(8,128)(2,1)S(1)}, u32[]{:S(2)}, u32[]{:S(2)}) async-start(bf16[8,80,128]{2,1,0:T(8,128)(2,1)} %shard_map.82._), calls=%async_computation | async-start | bytes 327680 | tf_op jit(solution)/shard_map/all_to_all | solution.py:378
  9.5 0.0 copy-start
  9.5 3.7 %shard_map.83 = (bf16[512,512]{1,0:T(8,128)(2,1)}, bf16[512,512]{1,0:T(8,128)(2,1)}) custom-call(f32[512,512]{1,0:T(8,128)} %top_hbm.1, f32[512,512]{1,0:T(8,128)} %bitcast.22, bf16[8,80,128]{2,1,0:T(8,128)(2,1)} %shard_map.82._), custom_call_target="tpu_custom_call" | custom-call | flops 1024 | bytes 1024 | tf_op jit(solution)/shard_map/pallas_call | solution.py:176
  13.2 1.9 %all-to-all-done.pack_ref = bf16[8,80,128]{2,1,0:T(8,128)(2,1)S(1)} async-done(((bf16[8,80,128]{2,1,0:T(8,128)(2,1)}), bf16[8,80,128]{2,1,0:T(8,128)(2,1)S(1)}, u32[]{:S(2)}, u32[]{:S(2)}) %all-to-all-start) | async-done | bytes 163872 | tf_op jit(solution)/shard_map/all_to_all | solution.py:378
  15.1 0.0 copy-start.4
  15.1 0.0 copy-done.2
  15.1 0.8 %shard_map.84 = (f32[64,512]{1,0:T(8,128)S(1)}, bf16[64,512]{1,0:T(8,128)(2,1)S(1)}) custom-call(bf16[8,80,128]{2,1,0:T(8,128)(2,1)S(1)} %all-to-all-done.pack_ref, f32[512,512]{1,0:T(8,128)S(1)} %bitcast.23), custom_call_target="tpu_custom_call" | custom-call | flops 1024 | bytes 1024 | tf_op jit(solution)/shard_map/pallas_call | solution.py:152
  15.9 2.5 %collective-permute-start.2 = (bf16[64,512]{1,0:T(8,128)(2,1)S(1)}, bf16[64,512]{1,0:T(8,128)(2,1)S(1)}, u32[]{:S(2)}, u32[]{:S(2)}) collective-permute-start(bf16[64,512]{1,0:T(8,128)(2,1)S(1)} %get-tuple-element.20.refs_0_), channel_id=1, source_target_pairs={{0,128},{1,17},{2,130},{3,19},{4,132},{5,21},{6,134},{7,23},{8,136... | collective-permute-start | bytes 196616 | tf_op jit(solution)/shard_map/ppermute | solution.py:332
  18.4 1.4 %collective-permute-start.1 = (bf16[64,512]{1,0:T(8,128)(2,1)S(1)}, bf16[64,512]{1,0:T(8,128)(2,1)S(1)}, u32[]{:S(2)}, u32[]{:S(2)}) collective-permute-start(bf16[64,512]{1,0:T(8,128)(2,1)S(1)} %get-tuple-element.20.refs_0_), channel_id=1, source_target_pairs={{0,192},{1,25},{2,194},{3,27},{4,196},{5,29},{6,198},{7,31},{8,200... | collective-permute-start | bytes 196616 | tf_op jit(solution)/shard_map/ppermute | solution.py:332
  19.9 0.2 collective-permute-start
  20.1 0.0 collective-permute-done.2.refs_3_
  20.1 3.4 %collective-permute-done.1.refs_2_ = bf16[64,512]{1,0:T(8,128)(2,1)S(1)} collective-permute-done((bf16[64,512]{1,0:T(8,128)(2,1)S(1)}, bf16[64,512]{1,0:T(8,128)(2,1)S(1)}, u32[]{:S(2)}, u32[]{:S(2)}) %collective-permute-start.1) | collective-permute-done | bytes 65568 | tf_op jit(solution)/shard_map/ppermute | solution.py:332
  23.5 0.5 collective-permute-done.refs_1_
  24.0 2.5 %collective-permute-start.5 = (bf16[64,512]{1,0:T(8,128)(2,1)S(1)}, bf16[64,512]{1,0:T(8,128)(2,1)S(1)}, u32[]{:S(2)}, u32[]{:S(2)}) collective-permute-start(bf16[64,512]{1,0:T(8,128)(2,1)S(1)} %shard_map.86.refs_0_), channel_id=1, source_target_pairs={{0,16},{1,129},{2,18},{3,131},{4,20},{5,133},{6,22},{7,135},{8,24}... | collective-permute-start | bytes 196616 | tf_op jit(solution)/shard_map/ppermute | solution.py:332
  26.6 0.9 %collective-permute-start.4 = (bf16[64,512]{1,0:T(8,128)(2,1)S(1)}, bf16[64,512]{1,0:T(8,128)(2,1)S(1)}, u32[]{:S(2)}, u32[]{:S(2)}) collective-permute-start(bf16[64,512]{1,0:T(8,128)(2,1)S(1)} %shard_map.86.refs_0_), channel_id=1, source_target_pairs={{0,24},{1,193},{2,26},{3,195},{4,28},{5,197},{6,30},{7,199},{8,16}... | collective-permute-start | bytes 196616 | tf_op jit(solution)/shard_map/ppermute | solution.py:332
  27.4 0.0 collective-permute-start.3
  27.4 0.0 copy-done
  27.4 0.0 copy-done.4
  27.4 0.0 copy-start.5
  27.5 0.0 copy-start.6
  27.5 0.4 shard_map.85.refs_4_.own_ref
  27.9 0.0 copy-start.7
  27.9 0.9 %collective-permute-done.5.refs_3_ = bf16[64,512]{1,0:T(8,128)(2,1)S(1)} collective-permute-done((bf16[64,512]{1,0:T(8,128)(2,1)S(1)}, bf16[64,512]{1,0:T(8,128)(2,1)S(1)}, u32[]{:S(2)}, u32[]{:S(2)}) %collective-permute-start.5) | collective-permute-done | bytes 65568 | tf_op jit(solution)/shard_map/ppermute | solution.py:332
  28.7 2.2 %collective-permute-done.4.refs_2_ = bf16[64,512]{1,0:T(8,128)(2,1)S(1)} collective-permute-done((bf16[64,512]{1,0:T(8,128)(2,1)S(1)}, bf16[64,512]{1,0:T(8,128)(2,1)S(1)}, u32[]{:S(2)}, u32[]{:S(2)}) %collective-permute-start.4) | collective-permute-done | bytes 65568 | tf_op jit(solution)/shard_map/ppermute | solution.py:332
  30.9 0.0 collective-permute-done.3.refs_1_
  30.9 4.5 %collective-permute-start.6 = (bf16[64,512]{1,0:T(8,128)(2,1)S(1)}, bf16[64,512]{1,0:T(8,128)(2,1)S(1)}, u32[]{:S(2)}, u32[]{:S(2)}) collective-permute-start(bf16[64,512]{1,0:T(8,128)(2,1)S(1)} %shard_map.87.refs_0_), channel_id=1, source_target_pairs={{0,56},{1,57},{2,58},{3,59},{4,60},{5,61},{6,62},{7,63},{8,48},{9,... | collective-permute-start | bytes 196616 | tf_op jit(solution)/shard_map/ppermute | solution.py:332
  35.4 1.8 %collective-permute-done.6.refs_1_ = bf16[64,512]{1,0:T(8,128)(2,1)S(1)} collective-permute-done((bf16[64,512]{1,0:T(8,128)(2,1)S(1)}, bf16[64,512]{1,0:T(8,128)(2,1)S(1)}, u32[]{:S(2)}, u32[]{:S(2)}) %collective-permute-start.6) | collective-permute-done | bytes 65568 | tf_op jit(solution)/shard_map/ppermute | solution.py:332
  37.2 0.0 copy-done.5
  37.2 0.0 copy-done.6
  37.2 1.3 %shard_map.88._ = bf16[8,64,128]{2,1,0:T(8,128)(2,1)} custom-call(bf16[8,80,128]{2,1,0:T(8,128)(2,1)S(1)} %all-to-all-done.pack_ref, f32[64,512]{1,0:T(8,128)S(1)} %shard_map.85.refs_4_.own_ref, bf16[512,512]{1,0:T(8,128)(2,1)S(1)} %copy-done.5, bf16[512,512]{1,0:T(8,128)(2,1)S(1)} %copy-done.6, bf16[64,512]{1,0:T(8,128)(2,1)S(1)} %shard_map.87.refs_0_, ...), custom_call_target="tpu_custom_call" | custom-call | flops 1024 | bytes 1024 | tf_op jit(solution)/shard_map/pallas_call | solution.py:228
  38.5 8.6 %all-to-all-start.1 = ((bf16[8,64,128]{2,1,0:T(8,128)(2,1)}), bf16[8,64,128]{2,1,0:T(8,128)(2,1)}, u32[]{:S(2)}, u32[]{:S(2)}) async-start(bf16[8,64,128]{2,1,0:T(8,128)(2,1)} %shard_map.88._), calls=%async_computation.1 | async-start | bytes 262144 | tf_op jit(solution)/shard_map/all_to_all | solution.py:389
  47.1 0.0 copy-done.7
  47.1 0.1 concatenate.3
  47.2 0.0 copy-start.1
  47.2 2.3 %copy-done.1 = bf16[1,1,1,1536,1536]{4,3,2,1,0:T(8,128)(2,1)S(1)} copy-done((bf16[1,1,1,1536,1536]{4,3,2,1,0:T(8,128)(2,1)S(1)}, bf16[1,1,1,1536,1536]{4,3,2,1,0:T(8,128)(2,1)}, u32[]{:S(2)}) %copy-start.1) | copy-done | bytes 4718616
  49.6 0.0 copy-start.3
  49.6 2.6 %shard_map.89.local_ref = bf16[6,512,256]{2,1,0:T(8,128)(2,1)S(1)} custom-call(bf16[512,1536]{1,0:T(8,128)(2,1)S(1)} %bitcast.20, bf16[1536,1536]{1,0:T(8,128)(2,1)S(1)} %bitcast.21, bf16[8,64,128]{2,1,0:T(8,128)(2,1)} %shard_map.88._), custom_call_target="tpu_custom_call" | custom-call | flops 1024 | bytes 1024 | tf_op jit(solution)/shard_map/pallas_call | solution.py:122
  52.2 0.4 all-to-all-done.1.back_ref
  52.5 0.0 copy-done.3
  52.5 1.5 %shard_map.90 = (bf16[512,256]{1,0:T(8,128)(2,1)S(1)}, bf16[512,256]{1,0:T(8,128)(2,1)S(1)}, bf16[512,256]{1,0:T(8,128)(2,1)S(1)}, bf16[512,256]{1,0:T(8,128)(2,...) custom-call(s32[1,21]{1,0:T(1,128)S(1)} %bitcast.27, bf16[8,64,128]{2,1,0:T(8,128)(2,1)} %all-to-all-done.1.back_ref, ...), custom_call_target="tpu_custom_call" | custom-call | flops 1024 | bytes 1024 | tf_op jit(solution)/shard_map/pallas_call | solution.py:280
  54.0 0.4 collective-permute-start.11
  54.5 3.8 %collective-permute-start.7 = (bf16[512,256]{1,0:T(8,128)(2,1)S(1)}, bf16[512,256]{1,0:T(8,128)(2,1)S(1)}, u32[]{:S(2)}, u32[]{:S(2)}) collective-permute-start(bf16[512,256]{1,0:T(8,128)(2,1)S(1)} %get-tuple-element.21.refs_0_), channel_id=1, source_target_pairs={{0,192},{1,57},{2,194},{3,59},{4,196},{5,61},{6,198},{7,63},{8,200... | collective-permute-start | bytes 786440 | tf_op jit(solution)/shard_map/ppermute | solution.py:332
  58.3 1.7 %collective-permute-start.8 = (bf16[512,256]{1,0:T(8,128)(2,1)S(1)}, bf16[512,256]{1,0:T(8,128)(2,1)S(1)}, u32[]{:S(2)}, u32[]{:S(2)}) collective-permute-start(bf16[512,256]{1,0:T(8,128)(2,1)S(1)} %get-tuple-element.22.refs_1_), channel_id=1, source_target_pairs={{0,56},{1,193},{2,58},{3,195},{4,60},{5,197},{6,62},{7,199},{8,16}... | collective-permute-start | bytes 786440 | tf_op jit(solution)/shard_map/ppermute | solution.py:332
  60.0 0.0 collective-permute-start.12
  60.1 1.3 %collective-permute-start.9 = (bf16[512,256]{1,0:T(8,128)(2,1)S(1)}, bf16[512,256]{1,0:T(8,128)(2,1)S(1)}, u32[]{:S(2)}, u32[]{:S(2)}) collective-permute-start(bf16[512,256]{1,0:T(8,128)(2,1)S(1)} %get-tuple-element.23.refs_2_), channel_id=1, source_target_pairs={{0,7},{1,2},{2,1},{3,4},{4,3},{5,6},{6,5},{7,0},{8,15},{9,10},{10,... | collective-permute-start | bytes 786440 | tf_op jit(solution)/shard_map/ppermute | solution.py:332
  61.3 0.0 collective-permute-done.11.refs_2_
  61.3 1.4 %collective-permute-start.10 = (bf16[512,256]{1,0:T(8,128)(2,1)S(1)}, bf16[512,256]{1,0:T(8,128)(2,1)S(1)}, u32[]{:S(2)}, u32[]{:S(2)}) collective-permute-start(bf16[512,256]{1,0:T(8,128)(2,1)S(1)} %get-tuple-element.24.refs_3_), channel_id=1, source_target_pairs={{0,1},{1,0},{2,3},{3,2},{4,5},{5,4},{6,7},{7,6},{8,9},{9,8},{10,11... | collective-permute-start | bytes 786440 | tf_op jit(solution)/shard_map/ppermute | solution.py:332
  62.7 2.8 %collective-permute-done.12.refs_3_ = bf16[512,256]{1,0:T(8,128)(2,1)S(1)} collective-permute-done((bf16[512,256]{1,0:T(8,128)(2,1)S(1)}, bf16[512,256]{1,0:T(8,128)(2,1)S(1)}, u32[]{:S(2)}, u32[]{:S(2)}) %collective-permute-start.12) | collective-permute-done | bytes 262176 | tf_op jit(solution)/shard_map/ppermute | solution.py:332
  65.6 1.4 %shard_map.91.refs_8_ = bf16[512,1536]{1,0:T(8,128)(2,1)} custom-call(s32[1,21]{1,0:T(1,128)S(1)} %bitcast.28, bf16[512,256]{1,0:T(8,128)(2,1)S(1)} %get-tuple-element.25.refs_0_, bf16[512,256]{1,0:T(8,128)(2,1)S(1)} %get-tuple-element.26.refs_1_, bf16[512,256]{1,0:T(8,128)(2,1)S(1)} %collective-permute-done.11.refs_2_, ...), custom_call_target="tpu_custom_call" | custom-call | flops 1024 | bytes 1024 | tf_op jit(solution)/shard_map/pallas_call | solution.py:312
  67.0 0.0 collective-permute-done.7.refs_4_
  67.0 0.0 collective-permute-done.8.refs_5_
  67.0 0.0 collective-permute-done.9.refs_6_
  67.0 0.0 collective-permute-done.10.refs_7_
  67.0 1.6 %shard_map.92 = bf16[512,1536]{1,0:T(8,128)(2,1)} custom-call(s32[1,21]{1,0:T(1,128)S(1)} %bitcast.29, bf16[512,256]{1,0:T(8,128)(2,1)S(1)} %get-tuple-element.21.refs_0_, bf16[512,256]{1,0:T(8,128)(2,1)S(1)} %get-tuple-element.22.refs_1_, bf16[512,256]{1,0:T(8,128)(2,1)S(1)} %get-tuple-element.23.refs_2_, ...), custom_call_target="tpu_custom_call", output_to_operand_aliasing={{}: (9, {})} | custom-call | flops 1024 | bytes 1024 | tf_op jit(solution)/shard_map/pallas_call | solution.py:312
  (2 shorter events, 0.1 us)
Async XLA Ops:
  2.8 12.3 %copy-start.2 = (f32[1,1,512,512]{3,2,1,0:T(8,128)S(1)}, f32[1,1,512,512]{3,2,1,0:T(8,128)}, u32[]{:S(2)}) copy-start(f32[1,1,512,512]{3,2,1,0:T(8,128)} %param.14) | copy-start | bytes 3145732
  2.8 12.3 %all-to-all-start = ((bf16[8,80,128]{2,1,0:T(8,128)(2,1)}), bf16[8,80,128]{2,1,0:T(8,128)(2,1)S(1)}, u32[]{:S(2)}, u32[]{:S(2)}) async-start(bf16[8,80,128]{2,1,0:T(8,128)(2,1)} %shard_map.82._), calls=%async_computation | async-start | bytes 327680 | tf_op jit(solution)/shard_map/all_to_all | solution.py:378
  9.5 17.9 %copy-start = (bf16[1,1,1,512,1536]{4,3,2,1,0:T(8,128)(2,1)S(1)}, bf16[1,1,1,512,1536]{4,3,2,1,0:T(8,128)(2,1)}, u32[]{:S(2)}) copy-start(bf16[1,1,1,512,1536]{4,3,2,1,0:T(8,128)(2,1)} %param.8) | copy-start | bytes 4718596
  15.1 12.3 %copy-start.4 = (f32[1,1,512,512]{3,2,1,0:T(8,128)S(1)}, f32[1,1,512,512]{3,2,1,0:T(8,128)}, u32[]{:S(2)}) copy-start(f32[1,1,512,512]{3,2,1,0:T(8,128)} %param.13) | copy-start | bytes 3145732
  15.9 4.2 %collective-permute-start.2 = (bf16[64,512]{1,0:T(8,128)(2,1)S(1)}, bf16[64,512]{1,0:T(8,128)(2,1)S(1)}, u32[]{:S(2)}, u32[]{:S(2)}) collective-permute-start(bf16[64,512]{1,0:T(8,128)(2,1)S(1)} %get-tuple-element.20.refs_0_), channel_id=1, source_target_pairs={{0,128},{1,17},{2,130},{3,19},{4,132},{5,21},{6,134},{7,23},{8,136... | collective-permute-start | bytes 196616 | tf_op jit(solution)/shard_map/ppermute | solution.py:332
  18.4 5.1 %collective-permute-start.1 = (bf16[64,512]{1,0:T(8,128)(2,1)S(1)}, bf16[64,512]{1,0:T(8,128)(2,1)S(1)}, u32[]{:S(2)}, u32[]{:S(2)}) collective-permute-start(bf16[64,512]{1,0:T(8,128)(2,1)S(1)} %get-tuple-element.20.refs_0_), channel_id=1, source_target_pairs={{0,192},{1,25},{2,194},{3,27},{4,196},{5,29},{6,198},{7,31},{8,200... | collective-permute-start | bytes 196616 | tf_op jit(solution)/shard_map/ppermute | solution.py:332
  19.9 4.1 %collective-permute-start = (bf16[64,512]{1,0:T(8,128)(2,1)S(1)}, bf16[64,512]{1,0:T(8,128)(2,1)S(1)}, u32[]{:S(2)}, u32[]{:S(2)}) collective-permute-start(bf16[64,512]{1,0:T(8,128)(2,1)S(1)} %get-tuple-element.20.refs_0_), channel_id=1, source_target_pairs={{0,64},{1,9},{2,66},{3,11},{4,68},{5,13},{6,70},{7,15},{8,72},{9,1... | collective-permute-start | bytes 196616 | tf_op jit(solution)/shard_map/ppermute | solution.py:332
  24.0 4.7 %collective-permute-start.5 = (bf16[64,512]{1,0:T(8,128)(2,1)S(1)}, bf16[64,512]{1,0:T(8,128)(2,1)S(1)}, u32[]{:S(2)}, u32[]{:S(2)}) collective-permute-start(bf16[64,512]{1,0:T(8,128)(2,1)S(1)} %shard_map.86.refs_0_), channel_id=1, source_target_pairs={{0,16},{1,129},{2,18},{3,131},{4,20},{5,133},{6,22},{7,135},{8,24}... | collective-permute-start | bytes 196616 | tf_op jit(solution)/shard_map/ppermute | solution.py:332
  26.6 4.3 %collective-permute-start.4 = (bf16[64,512]{1,0:T(8,128)(2,1)S(1)}, bf16[64,512]{1,0:T(8,128)(2,1)S(1)}, u32[]{:S(2)}, u32[]{:S(2)}) collective-permute-start(bf16[64,512]{1,0:T(8,128)(2,1)S(1)} %shard_map.86.refs_0_), channel_id=1, source_target_pairs={{0,24},{1,193},{2,26},{3,195},{4,28},{5,197},{6,30},{7,199},{8,16}... | collective-permute-start | bytes 196616 | tf_op jit(solution)/shard_map/ppermute | solution.py:332
  27.4 3.5 %collective-permute-start.3 = (bf16[64,512]{1,0:T(8,128)(2,1)S(1)}, bf16[64,512]{1,0:T(8,128)(2,1)S(1)}, u32[]{:S(2)}, u32[]{:S(2)}) collective-permute-start(bf16[64,512]{1,0:T(8,128)(2,1)S(1)} %shard_map.86.refs_0_), channel_id=1, source_target_pairs={{0,8},{1,65},{2,10},{3,67},{4,12},{5,69},{6,14},{7,71},{8,0},{9,73... | collective-permute-start | bytes 196616 | tf_op jit(solution)/shard_map/ppermute | solution.py:332
  27.4 9.7 %copy-start.5 = (bf16[512,512]{1,0:T(8,128)(2,1)S(1)}, bf16[512,512]{1,0:T(8,128)(2,1)}, u32[]{:S(2)}) copy-start(bf16[512,512]{1,0:T(8,128)(2,1)} %get-tuple-element.16.hi_ref) | copy-start | bytes 1572868
  27.5 9.7 %copy-start.6 = (bf16[512,512]{1,0:T(8,128)(2,1)S(1)}, bf16[512,512]{1,0:T(8,128)(2,1)}, u32[]{:S(2)}) copy-start(bf16[512,512]{1,0:T(8,128)(2,1)} %get-tuple-element.19.lo_ref) | copy-start | bytes 1572868
  27.9 19.3 %copy-start.7 = (s32[1,1,1,12]{3,2,1,0:T(1,128)S(1)}, s32[1,1,1,12]{3,2,1,0:T(1,128)}, u32[]{:S(2)}) copy-start(s32[1,1,1,12]{3,2,1,0:T(1,128)} %param.12) | copy-start | bytes 148
  30.9 6.3 %collective-permute-start.6 = (bf16[64,512]{1,0:T(8,128)(2,1)S(1)}, bf16[64,512]{1,0:T(8,128)(2,1)S(1)}, u32[]{:S(2)}, u32[]{:S(2)}) collective-permute-start(bf16[64,512]{1,0:T(8,128)(2,1)S(1)} %shard_map.87.refs_0_), channel_id=1, source_target_pairs={{0,56},{1,57},{2,58},{3,59},{4,60},{5,61},{6,62},{7,63},{8,48},{9,... | collective-permute-start | bytes 196616 | tf_op jit(solution)/shard_map/ppermute | solution.py:332
  38.5 14.0 %all-to-all-start.1 = ((bf16[8,64,128]{2,1,0:T(8,128)(2,1)}), bf16[8,64,128]{2,1,0:T(8,128)(2,1)}, u32[]{:S(2)}, u32[]{:S(2)}) async-start(bf16[8,64,128]{2,1,0:T(8,128)(2,1)} %shard_map.88._), calls=%async_computation.1 | async-start | bytes 262144 | tf_op jit(solution)/shard_map/all_to_all | solution.py:389
  47.2 2.3 %copy-start.1 = (bf16[1,1,1,1536,1536]{4,3,2,1,0:T(8,128)(2,1)S(1)}, bf16[1,1,1,1536,1536]{4,3,2,1,0:T(8,128)(2,1)}, u32[]{:S(2)}) copy-start(bf16[1,1,1,1536,1536]{4,3,2,1,0:T(8,128)(2,1)} %param.9) | copy-start | bytes 14155780
  49.6 3.0 %copy-start.3 = (bf16[1,1,1,128,1536]{4,3,2,1,0:T(8,128)(2,1)S(1)}, bf16[1,1,1,128,1536]{4,3,2,1,0:T(8,128)(2,1)}, u32[]{:S(2)}) copy-start(bf16[1,1,1,128,1536]{4,3,2,1,0:T(8,128)(2,1)} %param.10) | copy-start | bytes 1179652
  54.0 7.3 %collective-permute-start.11 = (bf16[512,256]{1,0:T(8,128)(2,1)S(1)}, bf16[512,256]{1,0:T(8,128)(2,1)S(1)}, u32[]{:S(2)}, u32[]{:S(2)}) collective-permute-start(bf16[512,256]{1,0:T(8,128)(2,1)S(1)} %get-tuple-element.25.refs_0_), channel_id=1, source_target_pairs={{0,64},{1,9},{2,66},{3,11},{4,68},{5,13},{6,70},{7,15},{8,72},{9,1... | collective-permute-start | bytes 786440 | tf_op jit(solution)/shard_map/ppermute | solution.py:332
  54.5 12.5 %collective-permute-start.7 = (bf16[512,256]{1,0:T(8,128)(2,1)S(1)}, bf16[512,256]{1,0:T(8,128)(2,1)S(1)}, u32[]{:S(2)}, u32[]{:S(2)}) collective-permute-start(bf16[512,256]{1,0:T(8,128)(2,1)S(1)} %get-tuple-element.21.refs_0_), channel_id=1, source_target_pairs={{0,192},{1,57},{2,194},{3,59},{4,196},{5,61},{6,198},{7,63},{8,200... | collective-permute-start | bytes 786440 | tf_op jit(solution)/shard_map/ppermute | solution.py:332
  58.3 8.7 %collective-permute-start.8 = (bf16[512,256]{1,0:T(8,128)(2,1)S(1)}, bf16[512,256]{1,0:T(8,128)(2,1)S(1)}, u32[]{:S(2)}, u32[]{:S(2)}) collective-permute-start(bf16[512,256]{1,0:T(8,128)(2,1)S(1)} %get-tuple-element.22.refs_1_), channel_id=1, source_target_pairs={{0,56},{1,193},{2,58},{3,195},{4,60},{5,197},{6,62},{7,199},{8,16}... | collective-permute-start | bytes 786440 | tf_op jit(solution)/shard_map/ppermute | solution.py:332
  60.0 5.5 %collective-permute-start.12 = (bf16[512,256]{1,0:T(8,128)(2,1)S(1)}, bf16[512,256]{1,0:T(8,128)(2,1)S(1)}, u32[]{:S(2)}, u32[]{:S(2)}) collective-permute-start(bf16[512,256]{1,0:T(8,128)(2,1)S(1)} %get-tuple-element.26.refs_1_), channel_id=1, source_target_pairs={{0,8},{1,65},{2,10},{3,67},{4,12},{5,69},{6,14},{7,71},{8,0},{9,73... | collective-permute-start | bytes 786440 | tf_op jit(solution)/shard_map/ppermute | solution.py:332
  60.1 6.9 %collective-permute-start.9 = (bf16[512,256]{1,0:T(8,128)(2,1)S(1)}, bf16[512,256]{1,0:T(8,128)(2,1)S(1)}, u32[]{:S(2)}, u32[]{:S(2)}) collective-permute-start(bf16[512,256]{1,0:T(8,128)(2,1)S(1)} %get-tuple-element.23.refs_2_), channel_id=1, source_target_pairs={{0,7},{1,2},{2,1},{3,4},{4,3},{5,6},{6,5},{7,0},{8,15},{9,10},{10,... | collective-permute-start | bytes 786440 | tf_op jit(solution)/shard_map/ppermute | solution.py:332
  61.3 5.7 %collective-permute-start.10 = (bf16[512,256]{1,0:T(8,128)(2,1)S(1)}, bf16[512,256]{1,0:T(8,128)(2,1)S(1)}, u32[]{:S(2)}, u32[]{:S(2)}) collective-permute-start(bf16[512,256]{1,0:T(8,128)(2,1)S(1)} %get-tuple-element.24.refs_3_), channel_id=1, source_target_pairs={{0,1},{1,0},{2,3},{3,2},{4,5},{5,4},{6,7},{7,6},{8,9},{9,8},{10,11... | collective-permute-start | bytes 786440 | tf_op jit(solution)/shard_map/ppermute | solution.py:332

commit v5 on v4

--- a/solution.py
+++ b/solution.py
@@ -207,13 +207,27 @@
     )(group_res, group_inv, later)
 
 
-def solve_body(pack_ref, own_ref, hi_ref, lo_ref, *refs):
-    parts, (out_hbm, out_ref, sems) = refs[:-3], refs[-3:]
+def base_body(own_ref, hi_ref, lo_ref, part_ref, out_ref):
+    part = part_ref[...]
+    out_ref[...] = own_ref[...] + (mm(part, hi_ref[...]) + mm(part, lo_ref[...]))
+
+
+def base_kernel(own, map_hi, map_lo, part):
+    return call(
+        base_body,
+        jax.ShapeDtypeStruct((RZ, C2), f32),
+        0,
+        0,
+        vmem=SMALL,
+        in_specs=[VMEM] * 4,
+        out_specs=VMEM,
+    )(own, map_hi, map_lo, part)
+
+
+def solve_body(pack_ref, base_ref, hi_ref, lo_ref, got_ref, out_hbm, out_ref, sems):
     onehot = member_onehot(pack_ref)
-    top_res = sum(p[...].astype(f32) for p in parts)
-    t_hi, t_lo = split(top_res)
-    sol = own_ref[...] + mm(t_hi, hi_ref[...]) + (mm(t_hi, lo_ref[...]) + mm(t_lo, hi_ref[...]))
-    sol = sol.astype(bf16)
+    got = got_ref[...]
+    sol = (base_ref[...] + (mm(got, hi_ref[...]) + mm(got, lo_ref[...]))).astype(bf16)
     outs = []
     for i in range(SZ // 2):
         picked = mm(sol, onehot[:, 2 * i * NC : (2 * i + 2) * NC]).astype(bf16)
@@ -224,17 +238,17 @@
         c.wait()
 
 
-def solve_kernel(pack, own, map_hi, map_lo, parts):
+def solve_kernel(pack, base, map_hi, map_lo, got):
     return call(
         solve_body,
         jax.ShapeDtypeStruct((SZ, RZ, NC), bf16),
         0,
         0,
         vmem=8,
-        in_specs=[VMEM] * (4 + len(parts)),
+        in_specs=[VMEM] * 5,
         out_specs=HBM,
         scratch_shapes=[pltpu.VMEM((SZ, RZ, NC), bf16), DMA((SZ // 2,))],
-    )(pack, own, map_hi, map_lo, *parts)
+    )(pack, base, map_hi, map_lo, got)
 
 
 def sum_body(count, *refs):
@@ -271,9 +285,11 @@
     for e, send_ref in enumerate(refs[:FACES]):
         f = send_face(meta_ref, e)
         cols = pl.ds(pl.multiple_of(f * FACE, FACE), FACE)
-        update = local_ref[f].astype(f32) + mm(rows, basis_ref[:, cols])
-        turned = jnp.concatenate([update[:, BW:], update[:, :BW]], axis=1)
-        send_ref[...] = jnp.where(meta_ref[0, 2 * f] == 1, turned, update).astype(bf16)
+        update = (local_ref[f].astype(f32) + mm(rows, basis_ref[:, cols])).astype(bf16)
+        low, high = update[:, :BW], update[:, BW:]
+        swap = meta_ref[0, 2 * f] == 1
+        send_ref[:, :BW] = jnp.where(swap, high, low)
+        send_ref[:, BW:] = jnp.where(swap, low, high)
 
 
 def update_kernel(meta, back, basis, local):
@@ -383,8 +399,9 @@
         for d in (1, 3, 2):
             gots.append(permute(part, functools.partial(group_of_four, d=d, turn=turn)))
         part = sum_kernel(gots, *earlier)
-    parts = [part, permute(part, lambda a, b, c: (a, SY - 1 - b, c))]
-    back = solve_kernel(pack, own, *top_map, parts)
+    got = permute(part, lambda a, b, c: (a, SY - 1 - b, c))
+    base = base_kernel(own, *top_map, part)
+    back = solve_kernel(pack, base, *top_map, got)
     local = local_kernel(res, schur, back)
     back = lax.all_to_all(back, "gz", 0, 0)
     sends = update_kernel(meta, back, basis, local)

time: 69 us -> 68.9 us (level)
  no operation moved by 1% of the time
where the time goes in v5:
time: 68.9 us; the launch traced here: 68.5 us
  starting transfers between devices  36 us (52%)
  Pallas kernels  16.4 us (24%)
  waiting for transfers between devices  13.5 us (20%)
  local copies, waits for them, and re-layouts  2.46 us (4%)
    ppermute x13, starting transfers between devices, permute(): return lax.ppermute(x, ('gx', 'gy', 'gz'), pairs)  20.7 us
    ppermute x13, waiting for transfers between devices, permute(): return lax.ppermute(x, ('gx', 'gy', 'gz'), pairs)  11.3 us
    all_to_all x1, starting transfers between devices, per_device(): back = lax.all_to_all(back, 'gz', 0, 0)  8.63 us
    all_to_all x1, starting transfers between devices, per_device(): lax.all_to_all(pack, 'gz', 0, 0)  6.67 us
    pallas_call x1, Pallas kernels, map_kernel(): call(map_body, (jax.ShapeDtypeStruct((C2, C2), bf16),) * 2, 0, 0, vmem=BI...  3.7 us
    pallas_call x2, Pallas kernels, last_kernel(): call(functools.partial(last_body, slots), jax.ShapeDtypeStruct((R, NI), b...  3 us
    pallas_call x1, Pallas kernels, coarse_kernel(): call(coarse_body, jax.ShapeDtypeStruct((SZ, PACK, NC), bf16), 0, 0, vmem=...  2.82 us
    pallas_call x1, Pallas kernels, local_kernel(): call(local_body, jax.ShapeDtypeStruct((FACES, R, FACE), bf16), 0, 0, vmem...  2.59 us
  transfers between devices with their start and end apart: 15, of which 8 were waited for; matrix products, arithmetic and copies ran while one was open for 0% of the time, Pallas kernels for 12%

profile of v5, /device:TPU:1, one launch (start us, length us, event | category | flops | bytes accessed | tf_op | source)
XLA Modules:
  0.0 68.5 jit_solution(52546304783253084)
XLA Ops:
  0.0 2.8 %shard_map.82._ = bf16[8,80,128]{2,1,0:T(8,128)(2,1)} custom-call(s32[1,128]{1,0:T(1,128)} %bitcast.30, bf16[512,1536]{1,0:T(8,128)(2,1)} %bitcast.18, bf16[128,1536]{1,0:T(8,128)(2,1)} %bitcast.24), custom_call_target="tpu_custom_call" | custom-call | flops 1024 | bytes 1024 | tf_op jit(solution)/shard_map/pallas_call | solution.py:99
  2.8 0.0 copy-start.2
  2.8 6.7 %all-to-all-start = ((bf16[8,80,128]{2,1,0:T(8,128)(2,1)}), bf16[8,80,128]{2,1,0:T(8,128)(2,1)S(1)}, u32[]{:S(2)}, u32[]{:S(2)}) async-start(bf16[8,80,128]{2,1,0:T(8,128)(2,1)} %shard_map.82._), calls=%async_computation | async-start | bytes 327680 | tf_op jit(solution)/shard_map/all_to_all | solution.py:394
  9.5 0.0 copy-start
  9.5 3.7 %shard_map.83 = (bf16[512,512]{1,0:T(8,128)(2,1)}, bf16[512,512]{1,0:T(8,128)(2,1)}) custom-call(f32[512,512]{1,0:T(8,128)} %top_hbm.1, f32[512,512]{1,0:T(8,128)} %bitcast.22, bf16[8,80,128]{2,1,0:T(8,128)(2,1)} %shard_map.82._), custom_call_target="tpu_custom_call" | custom-call | flops 1024 | bytes 1024 | tf_op jit(solution)/shard_map/pallas_call | solution.py:176
  13.2 1.9 %all-to-all-done.pack_ref = bf16[8,80,128]{2,1,0:T(8,128)(2,1)S(1)} async-done(((bf16[8,80,128]{2,1,0:T(8,128)(2,1)}), bf16[8,80,128]{2,1,0:T(8,128)(2,1)S(1)}, u32[]{:S(2)}, u32[]{:S(2)}) %all-to-all-start) | async-done | bytes 163872 | tf_op jit(solution)/shard_map/all_to_all | solution.py:394
  15.1 0.0 copy-start.6
  15.1 0.0 copy-done.2
  15.1 0.8 %shard_map.84 = (f32[64,512]{1,0:T(8,128)S(1)}, bf16[64,512]{1,0:T(8,128)(2,1)S(1)}) custom-call(bf16[8,80,128]{2,1,0:T(8,128)(2,1)S(1)} %all-to-all-done.pack_ref, f32[512,512]{1,0:T(8,128)S(1)} %bitcast.23), custom_call_target="tpu_custom_call" | custom-call | flops 1024 | bytes 1024 | tf_op jit(solution)/shard_map/pallas_call | solution.py:152
  15.9 2.5 %collective-permute-start.2 = (bf16[64,512]{1,0:T(8,128)(2,1)S(1)}, bf16[64,512]{1,0:T(8,128)(2,1)S(1)}, u32[]{:S(2)}, u32[]{:S(2)}) collective-permute-start(bf16[64,512]{1,0:T(8,128)(2,1)S(1)} %get-tuple-element.20.refs_0_), channel_id=1, source_target_pairs={{0,128},{1,17},{2,130},{3,19},{4,132},{5,21},{6,134},{7,23},{8,136... | collective-permute-start | bytes 196616 | tf_op jit(solution)/shard_map/ppermute | solution.py:348
  18.4 1.4 %collective-permute-start.1 = (bf16[64,512]{1,0:T(8,128)(2,1)S(1)}, bf16[64,512]{1,0:T(8,128)(2,1)S(1)}, u32[]{:S(2)}, u32[]{:S(2)}) collective-permute-start(bf16[64,512]{1,0:T(8,128)(2,1)S(1)} %get-tuple-element.20.refs_0_), channel_id=1, source_target_pairs={{0,192},{1,25},{2,194},{3,27},{4,196},{5,29},{6,198},{7,31},{8,200... | collective-permute-start | bytes 196616 | tf_op jit(solution)/shard_map/ppermute | solution.py:348
  19.9 0.2 collective-permute-start
  20.1 0.0 collective-permute-done.2.refs_3_
  20.1 3.4 %collective-permute-done.1.refs_2_ = bf16[64,512]{1,0:T(8,128)(2,1)S(1)} collective-permute-done((bf16[64,512]{1,0:T(8,128)(2,1)S(1)}, bf16[64,512]{1,0:T(8,128)(2,1)S(1)}, u32[]{:S(2)}, u32[]{:S(2)}) %collective-permute-start.1) | collective-permute-done | bytes 65568 | tf_op jit(solution)/shard_map/ppermute | solution.py:348
  23.5 0.5 collective-permute-done.refs_1_
  24.0 2.5 %collective-permute-start.5 = (bf16[64,512]{1,0:T(8,128)(2,1)S(1)}, bf16[64,512]{1,0:T(8,128)(2,1)S(1)}, u32[]{:S(2)}, u32[]{:S(2)}) collective-permute-start(bf16[64,512]{1,0:T(8,128)(2,1)S(1)} %shard_map.86.refs_0_), channel_id=1, source_target_pairs={{0,16},{1,129},{2,18},{3,131},{4,20},{5,133},{6,22},{7,135},{8,24}... | collective-permute-start | bytes 196616 | tf_op jit(solution)/shard_map/ppermute | solution.py:348
  26.6 0.9 %collective-permute-start.4 = (bf16[64,512]{1,0:T(8,128)(2,1)S(1)}, bf16[64,512]{1,0:T(8,128)(2,1)S(1)}, u32[]{:S(2)}, u32[]{:S(2)}) collective-permute-start(bf16[64,512]{1,0:T(8,128)(2,1)S(1)} %shard_map.86.refs_0_), channel_id=1, source_target_pairs={{0,24},{1,193},{2,26},{3,195},{4,28},{5,197},{6,30},{7,199},{8,16}... | collective-permute-start | bytes 196616 | tf_op jit(solution)/shard_map/ppermute | solution.py:348
  27.4 0.0 collective-permute-start.3
  27.4 0.0 copy-done
  27.4 0.0 copy-done.6
  27.4 0.0 copy-start.3
  27.5 0.0 copy-start.4
  27.5 0.4 shard_map.85.refs_4_.own_ref
  27.9 0.9 %collective-permute-done.5.refs_3_ = bf16[64,512]{1,0:T(8,128)(2,1)S(1)} collective-permute-done((bf16[64,512]{1,0:T(8,128)(2,1)S(1)}, bf16[64,512]{1,0:T(8,128)(2,1)S(1)}, u32[]{:S(2)}, u32[]{:S(2)}) %collective-permute-start.5) | collective-permute-done | bytes 65568 | tf_op jit(solution)/shard_map/ppermute | solution.py:348
  28.7 2.2 %collective-permute-done.4.refs_2_ = bf16[64,512]{1,0:T(8,128)(2,1)S(1)} collective-permute-done((bf16[64,512]{1,0:T(8,128)(2,1)S(1)}, bf16[64,512]{1,0:T(8,128)(2,1)S(1)}, u32[]{:S(2)}, u32[]{:S(2)}) %collective-permute-start.4) | collective-permute-done | bytes 65568 | tf_op jit(solution)/shard_map/ppermute | solution.py:348
  30.9 0.0 collective-permute-done.3.refs_1_
  30.9 4.5 %collective-permute-start.6 = (bf16[64,512]{1,0:T(8,128)(2,1)S(1)}, bf16[64,512]{1,0:T(8,128)(2,1)S(1)}, u32[]{:S(2)}, u32[]{:S(2)}) collective-permute-start(bf16[64,512]{1,0:T(8,128)(2,1)S(1)} %shard_map.87.part_ref), channel_id=1, source_target_pairs={{0,56},{1,57},{2,58},{3,59},{4,60},{5,61},{6,62},{7,63},{8,48},{9,... | collective-permute-start | bytes 196616 | tf_op jit(solution)/shard_map/ppermute | solution.py:348
  35.4 0.0 copy-done.3
  35.4 0.0 copy-done.4
  35.4 0.0 copy-start.7
  35.4 0.3 shard_map.88.base_ref
  35.7 1.5 %collective-permute-done.6.got_ref = bf16[64,512]{1,0:T(8,128)(2,1)S(1)} collective-permute-done((bf16[64,512]{1,0:T(8,128)(2,1)S(1)}, bf16[64,512]{1,0:T(8,128)(2,1)S(1)}, u32[]{:S(2)}, u32[]{:S(2)}) %collective-permute-start.6) | collective-permute-done | bytes 65568 | tf_op jit(solution)/shard_map/ppermute | solution.py:348
  37.2 1.2 %shard_map.89._ = bf16[8,64,128]{2,1,0:T(8,128)(2,1)} custom-call(bf16[8,80,128]{2,1,0:T(8,128)(2,1)S(1)} %all-to-all-done.pack_ref, f32[64,512]{1,0:T(8,128)S(1)} %shard_map.88.base_ref, bf16[512,512]{1,0:T(8,128)(2,1)S(1)} %copy-done.3, bf16[512,512]{1,0:T(8,128)(2,1)S(1)} %copy-done.4, bf16[64,512]{1,0:T(8,128)(2,1)S(1)} %collective-permute-done.6.got_ref), custom_call_target="tpu_custom_call" | custom-call | flops 1024 | bytes 1024 | tf_op jit(solution)/shard_map/pallas_call | solution.py:242
  38.4 8.6 %all-to-all-start.1 = ((bf16[8,64,128]{2,1,0:T(8,128)(2,1)}), bf16[8,64,128]{2,1,0:T(8,128)(2,1)}, u32[]{:S(2)}, u32[]{:S(2)}) async-start(bf16[8,64,128]{2,1,0:T(8,128)(2,1)} %shard_map.89._), calls=%async_computation.1 | async-start | bytes 262144 | tf_op jit(solution)/shard_map/all_to_all | solution.py:406
  47.0 0.0 copy-done.7
  47.0 0.1 concatenate.3
  47.1 0.0 copy-start.1
  47.1 2.3 %copy-done.1 = bf16[1,1,1,1536,1536]{4,3,2,1,0:T(8,128)(2,1)S(1)} copy-done((bf16[1,1,1,1536,1536]{4,3,2,1,0:T(8,128)(2,1)S(1)}, bf16[1,1,1,1536,1536]{4,3,2,1,0:T(8,128)(2,1)}, u32[]{:S(2)}) %copy-start.1) | copy-done | bytes 4718616
  49.5 0.0 copy-start.5
  49.5 2.6 %shard_map.90.local_ref = bf16[6,512,256]{2,1,0:T(8,128)(2,1)S(1)} custom-call(bf16[512,1536]{1,0:T(8,128)(2,1)S(1)} %bitcast.20, bf16[1536,1536]{1,0:T(8,128)(2,1)S(1)} %bitcast.21, bf16[8,64,128]{2,1,0:T(8,128)(2,1)} %shard_map.89._), custom_call_target="tpu_custom_call" | custom-call | flops 1024 | bytes 1024 | tf_op jit(solution)/shard_map/pallas_call | solution.py:122
  52.1 0.4 all-to-all-done.1.back_ref
  52.4 0.0 copy-done.5
  52.4 1.5 %shard_map.91 = (bf16[512,256]{1,0:T(8,128)(2,1)S(1)}, bf16[512,256]{1,0:T(8,128)(2,1)S(1)}, bf16[512,256]{1,0:T(8,128)(2,1)S(1)}, bf16[512,256]{1,0:T(8,128)(2,...) custom-call(s32[1,21]{1,0:T(1,128)S(1)} %bitcast.27, bf16[8,64,128]{2,1,0:T(8,128)(2,1)} %all-to-all-done.1.back_ref, ...), custom_call_target="tpu_custom_call" | custom-call | flops 1024 | bytes 1024 | tf_op jit(solution)/shard_map/pallas_call | solution.py:296
  54.0 0.4 collective-permute-start.11
  54.4 3.8 %collective-permute-start.7 = (bf16[512,256]{1,0:T(8,128)(2,1)S(1)}, bf16[512,256]{1,0:T(8,128)(2,1)S(1)}, u32[]{:S(2)}, u32[]{:S(2)}) collective-permute-start(bf16[512,256]{1,0:T(8,128)(2,1)S(1)} %get-tuple-element.21.refs_0_), channel_id=1, source_target_pairs={{0,192},{1,57},{2,194},{3,59},{4,196},{5,61},{6,198},{7,63},{8,200... | collective-permute-start | bytes 786440 | tf_op jit(solution)/shard_map/ppermute | solution.py:348
  58.2 1.7 %collective-permute-start.8 = (bf16[512,256]{1,0:T(8,128)(2,1)S(1)}, bf16[512,256]{1,0:T(8,128)(2,1)S(1)}, u32[]{:S(2)}, u32[]{:S(2)}) collective-permute-start(bf16[512,256]{1,0:T(8,128)(2,1)S(1)} %get-tuple-element.22.refs_1_), channel_id=1, source_target_pairs={{0,56},{1,193},{2,58},{3,195},{4,60},{5,197},{6,62},{7,199},{8,16}... | collective-permute-start | bytes 786440 | tf_op jit(solution)/shard_map/ppermute | solution.py:348
  60.0 0.0 collective-permute-start.12
  60.0 1.3 %collective-permute-start.9 = (bf16[512,256]{1,0:T(8,128)(2,1)S(1)}, bf16[512,256]{1,0:T(8,128)(2,1)S(1)}, u32[]{:S(2)}, u32[]{:S(2)}) collective-permute-start(bf16[512,256]{1,0:T(8,128)(2,1)S(1)} %get-tuple-element.23.refs_2_), channel_id=1, source_target_pairs={{0,7},{1,2},{2,1},{3,4},{4,3},{5,6},{6,5},{7,0},{8,15},{9,10},{10,... | collective-permute-start | bytes 786440 | tf_op jit(solution)/shard_map/ppermute | solution.py:348
  61.2 0.0 collective-permute-done.11.refs_2_
  61.2 1.4 %collective-permute-start.10 = (bf16[512,256]{1,0:T(8,128)(2,1)S(1)}, bf16[512,256]{1,0:T(8,128)(2,1)S(1)}, u32[]{:S(2)}, u32[]{:S(2)}) collective-permute-start(bf16[512,256]{1,0:T(8,128)(2,1)S(1)} %get-tuple-element.24.refs_3_), channel_id=1, source_target_pairs={{0,1},{1,0},{2,3},{3,2},{4,5},{5,4},{6,7},{7,6},{8,9},{9,8},{10,11... | collective-permute-start | bytes 786440 | tf_op jit(solution)/shard_map/ppermute | solution.py:348
  62.7 2.8 %collective-permute-done.12.refs_3_ = bf16[512,256]{1,0:T(8,128)(2,1)S(1)} collective-permute-done((bf16[512,256]{1,0:T(8,128)(2,1)S(1)}, bf16[512,256]{1,0:T(8,128)(2,1)S(1)}, u32[]{:S(2)}, u32[]{:S(2)}) %collective-permute-start.12) | collective-permute-done | bytes 262176 | tf_op jit(solution)/shard_map/ppermute | solution.py:348
  65.5 1.4 %shard_map.92.refs_8_ = bf16[512,1536]{1,0:T(8,128)(2,1)} custom-call(s32[1,21]{1,0:T(1,128)S(1)} %bitcast.28, bf16[512,256]{1,0:T(8,128)(2,1)S(1)} %get-tuple-element.25.refs_0_, bf16[512,256]{1,0:T(8,128)(2,1)S(1)} %get-tuple-element.26.refs_1_, bf16[512,256]{1,0:T(8,128)(2,1)S(1)} %collective-permute-done.11.refs_2_, ...), custom_call_target="tpu_custom_call" | custom-call | flops 1024 | bytes 1024 | tf_op jit(solution)/shard_map/pallas_call | solution.py:328
  66.9 0.0 collective-permute-done.7.refs_4_
  66.9 0.0 collective-permute-done.8.refs_5_
  66.9 0.0 collective-permute-done.9.refs_6_
  66.9 0.0 collective-permute-done.10.refs_7_
  66.9 1.6 %shard_map.93 = bf16[512,1536]{1,0:T(8,128)(2,1)} custom-call(s32[1,21]{1,0:T(1,128)S(1)} %bitcast.29, bf16[512,256]{1,0:T(8,128)(2,1)S(1)} %get-tuple-element.21.refs_0_, bf16[512,256]{1,0:T(8,128)(2,1)S(1)} %get-tuple-element.22.refs_1_, bf16[512,256]{1,0:T(8,128)(2,1)S(1)} %get-tuple-element.23.refs_2_, ...), custom_call_target="tpu_custom_call", output_to_operand_aliasing={{}: (9, {})} | custom-call | flops 1024 | bytes 1024 | tf_op jit(solution)/shard_map/pallas_call | solution.py:328
  (2 shorter events, 0.1 us)
Async XLA Ops:
  2.8 12.3 %copy-start.2 = (f32[1,1,512,512]{3,2,1,0:T(8,128)S(1)}, f32[1,1,512,512]{3,2,1,0:T(8,128)}, u32[]{:S(2)}) copy-start(f32[1,1,512,512]{3,2,1,0:T(8,128)} %param.14) | copy-start | bytes 3145732
  2.8 12.3 %all-to-all-start = ((bf16[8,80,128]{2,1,0:T(8,128)(2,1)}), bf16[8,80,128]{2,1,0:T(8,128)(2,1)S(1)}, u32[]{:S(2)}, u32[]{:S(2)}) async-start(bf16[8,80,128]{2,1,0:T(8,128)(2,1)} %shard_map.82._), calls=%async_computation | async-start | bytes 327680 | tf_op jit(solution)/shard_map/all_to_all | solution.py:394
  9.5 17.9 %copy-start = (bf16[1,1,1,512,1536]{4,3,2,1,0:T(8,128)(2,1)S(1)}, bf16[1,1,1,512,1536]{4,3,2,1,0:T(8,128)(2,1)}, u32[]{:S(2)}) copy-start(bf16[1,1,1,512,1536]{4,3,2,1,0:T(8,128)(2,1)} %param.8) | copy-start | bytes 4718596
  15.1 12.3 %copy-start.6 = (f32[1,1,512,512]{3,2,1,0:T(8,128)S(1)}, f32[1,1,512,512]{3,2,1,0:T(8,128)}, u32[]{:S(2)}) copy-start(f32[1,1,512,512]{3,2,1,0:T(8,128)} %param.13) | copy-start | bytes 3145732
  15.9 4.2 %collective-permute-start.2 = (bf16[64,512]{1,0:T(8,128)(2,1)S(1)}, bf16[64,512]{1,0:T(8,128)(2,1)S(1)}, u32[]{:S(2)}, u32[]{:S(2)}) collective-permute-start(bf16[64,512]{1,0:T(8,128)(2,1)S(1)} %get-tuple-element.20.refs_0_), channel_id=1, source_target_pairs={{0,128},{1,17},{2,130},{3,19},{4,132},{5,21},{6,134},{7,23},{8,136... | collective-permute-start | bytes 196616 | tf_op jit(solution)/shard_map/ppermute | solution.py:348
  18.4 5.1 %collective-permute-start.1 = (bf16[64,512]{1,0:T(8,128)(2,1)S(1)}, bf16[64,512]{1,0:T(8,128)(2,1)S(1)}, u32[]{:S(2)}, u32[]{:S(2)}) collective-permute-start(bf16[64,512]{1,0:T(8,128)(2,1)S(1)} %get-tuple-element.20.refs_0_), channel_id=1, source_target_pairs={{0,192},{1,25},{2,194},{3,27},{4,196},{5,29},{6,198},{7,31},{8,200... | collective-permute-start | bytes 196616 | tf_op jit(solution)/shard_map/ppermute | solution.py:348
  19.9 4.1 %collective-permute-start = (bf16[64,512]{1,0:T(8,128)(2,1)S(1)}, bf16[64,512]{1,0:T(8,128)(2,1)S(1)}, u32[]{:S(2)}, u32[]{:S(2)}) collective-permute-start(bf16[64,512]{1,0:T(8,128)(2,1)S(1)} %get-tuple-element.20.refs_0_), channel_id=1, source_target_pairs={{0,64},{1,9},{2,66},{3,11},{4,68},{5,13},{6,70},{7,15},{8,72},{9,1... | collective-permute-start | bytes 196616 | tf_op jit(solution)/shard_map/ppermute | solution.py:348
  24.0 4.7 %collective-permute-start.5 = (bf16[64,512]{1,0:T(8,128)(2,1)S(1)}, bf16[64,512]{1,0:T(8,128)(2,1)S(1)}, u32[]{:S(2)}, u32[]{:S(2)}) collective-permute-start(bf16[64,512]{1,0:T(8,128)(2,1)S(1)} %shard_map.86.refs_0_), channel_id=1, source_target_pairs={{0,16},{1,129},{2,18},{3,131},{4,20},{5,133},{6,22},{7,135},{8,24}... | collective-permute-start | bytes 196616 | tf_op jit(solution)/shard_map/ppermute | solution.py:348
  26.6 4.3 %collective-permute-start.4 = (bf16[64,512]{1,0:T(8,128)(2,1)S(1)}, bf16[64,512]{1,0:T(8,128)(2,1)S(1)}, u32[]{:S(2)}, u32[]{:S(2)}) collective-permute-start(bf16[64,512]{1,0:T(8,128)(2,1)S(1)} %shard_map.86.refs_0_), channel_id=1, source_target_pairs={{0,24},{1,193},{2,26},{3,195},{4,28},{5,197},{6,30},{7,199},{8,16}... | collective-permute-start | bytes 196616 | tf_op jit(solution)/shard_map/ppermute | solution.py:348
  27.4 3.5 %collective-permute-start.3 = (bf16[64,512]{1,0:T(8,128)(2,1)S(1)}, bf16[64,512]{1,0:T(8,128)(2,1)S(1)}, u32[]{:S(2)}, u32[]{:S(2)}) collective-permute-start(bf16[64,512]{1,0:T(8,128)(2,1)S(1)} %shard_map.86.refs_0_), channel_id=1, source_target_pairs={{0,8},{1,65},{2,10},{3,67},{4,12},{5,69},{6,14},{7,71},{8,0},{9,73... | collective-permute-start | bytes 196616 | tf_op jit(solution)/shard_map/ppermute | solution.py:348
  27.4 8.0 %copy-start.3 = (bf16[512,512]{1,0:T(8,128)(2,1)S(1)}, bf16[512,512]{1,0:T(8,128)(2,1)}, u32[]{:S(2)}) copy-start(bf16[512,512]{1,0:T(8,128)(2,1)} %get-tuple-element.16.hi_ref) | copy-start | bytes 1572868
  27.5 7.9 %copy-start.4 = (bf16[512,512]{1,0:T(8,128)(2,1)S(1)}, bf16[512,512]{1,0:T(8,128)(2,1)}, u32[]{:S(2)}) copy-start(bf16[512,512]{1,0:T(8,128)(2,1)} %get-tuple-element.19.lo_ref) | copy-start | bytes 1572868
  30.9 6.3 %collective-permute-start.6 = (bf16[64,512]{1,0:T(8,128)(2,1)S(1)}, bf16[64,512]{1,0:T(8,128)(2,1)S(1)}, u32[]{:S(2)}, u32[]{:S(2)}) collective-permute-start(bf16[64,512]{1,0:T(8,128)(2,1)S(1)} %shard_map.87.part_ref), channel_id=1, source_target_pairs={{0,56},{1,57},{2,58},{3,59},{4,60},{5,61},{6,62},{7,63},{8,48},{9,... | collective-permute-start | bytes 196616 | tf_op jit(solution)/shard_map/ppermute | solution.py:348
  35.4 11.6 %copy-start.7 = (s32[1,1,1,12]{3,2,1,0:T(1,128)S(1)}, s32[1,1,1,12]{3,2,1,0:T(1,128)}, u32[]{:S(2)}) copy-start(s32[1,1,1,12]{3,2,1,0:T(1,128)} %param.12) | copy-start | bytes 148
  38.4 14.0 %all-to-all-start.1 = ((bf16[8,64,128]{2,1,0:T(8,128)(2,1)}), bf16[8,64,128]{2,1,0:T(8,128)(2,1)}, u32[]{:S(2)}, u32[]{:S(2)}) async-start(bf16[8,64,128]{2,1,0:T(8,128)(2,1)} %shard_map.89._), calls=%async_computation.1 | async-start | bytes 262144 | tf_op jit(solution)/shard_map/all_to_all | solution.py:406
  47.1 2.3 %copy-start.1 = (bf16[1,1,1,1536,1536]{4,3,2,1,0:T(8,128)(2,1)S(1)}, bf16[1,1,1,1536,1536]{4,3,2,1,0:T(8,128)(2,1)}, u32[]{:S(2)}) copy-start(bf16[1,1,1,1536,1536]{4,3,2,1,0:T(8,128)(2,1)} %param.9) | copy-start | bytes 14155780
  49.5 3.0 %copy-start.5 = (bf16[1,1,1,128,1536]{4,3,2,1,0:T(8,128)(2,1)S(1)}, bf16[1,1,1,128,1536]{4,3,2,1,0:T(8,128)(2,1)}, u32[]{:S(2)}) copy-start(bf16[1,1,1,128,1536]{4,3,2,1,0:T(8,128)(2,1)} %param.10) | copy-start | bytes 1179652
  54.0 7.3 %collective-permute-start.11 = (bf16[512,256]{1,0:T(8,128)(2,1)S(1)}, bf16[512,256]{1,0:T(8,128)(2,1)S(1)}, u32[]{:S(2)}, u32[]{:S(2)}) collective-permute-start(bf16[512,256]{1,0:T(8,128)(2,1)S(1)} %get-tuple-element.25.refs_0_), channel_id=1, source_target_pairs={{0,64},{1,9},{2,66},{3,11},{4,68},{5,13},{6,70},{7,15},{8,72},{9,1... | collective-permute-start | bytes 786440 | tf_op jit(solution)/shard_map/ppermute | solution.py:348
  54.4 12.5 %collective-permute-start.7 = (bf16[512,256]{1,0:T(8,128)(2,1)S(1)}, bf16[512,256]{1,0:T(8,128)(2,1)S(1)}, u32[]{:S(2)}, u32[]{:S(2)}) collective-permute-start(bf16[512,256]{1,0:T(8,128)(2,1)S(1)} %get-tuple-element.21.refs_0_), channel_id=1, source_target_pairs={{0,192},{1,57},{2,194},{3,59},{4,196},{5,61},{6,198},{7,63},{8,200... | collective-permute-start | bytes 786440 | tf_op jit(solution)/shard_map/ppermute | solution.py:348
  58.2 8.7 %collective-permute-start.8 = (bf16[512,256]{1,0:T(8,128)(2,1)S(1)}, bf16[512,256]{1,0:T(8,128)(2,1)S(1)}, u32[]{:S(2)}, u32[]{:S(2)}) collective-permute-start(bf16[512,256]{1,0:T(8,128)(2,1)S(1)} %get-tuple-element.22.refs_1_), channel_id=1, source_target_pairs={{0,56},{1,193},{2,58},{3,195},{4,60},{5,197},{6,62},{7,199},{8,16}... | collective-permute-start | bytes 786440 | tf_op jit(solution)/shard_map/ppermute | solution.py:348
  60.0 5.5 %collective-permute-start.12 = (bf16[512,256]{1,0:T(8,128)(2,1)S(1)}, bf16[512,256]{1,0:T(8,128)(2,1)S(1)}, u32[]{:S(2)}, u32[]{:S(2)}) collective-permute-start(bf16[512,256]{1,0:T(8,128)(2,1)S(1)} %get-tuple-element.26.refs_1_), channel_id=1, source_target_pairs={{0,8},{1,65},{2,10},{3,67},{4,12},{5,69},{6,14},{7,71},{8,0},{9,73... | collective-permute-start | bytes 786440 | tf_op jit(solution)/shard_map/ppermute | solution.py:348
  60.0 6.9 %collective-permute-start.9 = (bf16[512,256]{1,0:T(8,128)(2,1)S(1)}, bf16[512,256]{1,0:T(8,128)(2,1)S(1)}, u32[]{:S(2)}, u32[]{:S(2)}) collective-permute-start(bf16[512,256]{1,0:T(8,128)(2,1)S(1)} %get-tuple-element.23.refs_2_), channel_id=1, source_target_pairs={{0,7},{1,2},{2,1},{3,4},{4,3},{5,6},{6,5},{7,0},{8,15},{9,10},{10,... | collective-permute-start | bytes 786440 | tf_op jit(solution)/shard_map/ppermute | solution.py:348
  61.2 5.7 %collective-permute-start.10 = (bf16[512,256]{1,0:T(8,128)(2,1)S(1)}, bf16[512,256]{1,0:T(8,128)(2,1)S(1)}, u32[]{:S(2)}, u32[]{:S(2)}) collective-permute-start(bf16[512,256]{1,0:T(8,128)(2,1)S(1)} %get-tuple-element.24.refs_3_), channel_id=1, source_target_pairs={{0,1},{1,0},{2,3},{3,2},{4,5},{5,4},{6,7},{7,6},{8,9},{9,8},{10,11... | collective-permute-start | bytes 786440 | tf_op jit(solution)/shard_map/ppermute | solution.py:348

commit v6 on v5

--- a/solution.py
+++ b/solution.py
@@ -82,17 +82,18 @@
 
 def coarse_body(idx_hbm, res_hbm, basis_hbm, out_ref, idx_ref, res_ref, basis_ref, sems):
     copies = started([(idx_hbm, idx_ref), (basis_hbm, basis_ref), (res_hbm, res_ref)], sems)
-    for c in copies:
+    copies[0].wait()
+    idx = idx_ref[...]
+    row = lax.broadcasted_iota(jnp.int32, (TAIL, NC), 0)
+    digits = jnp.where(row == 0, idx >> 4, jnp.where(row == 1, idx & (BASE - 1), 0))
+    digits = digits.astype(f32).astype(bf16)
+    out_ref[:, RZ:, :] = jnp.broadcast_to(digits[None], (SZ, TAIL, NC))
+    for c in copies[1:]:
         c.wait()
     part = lax.dot_general(res_ref[...], basis_ref[...], LAST, preferred_element_type=f32)
     part = part.astype(bf16).reshape(SX, SZ, RX, NC)
     for a in range(SX):
         out_ref[:, a * RX : (a + 1) * RX, :] = part[a]
-    idx = idx_ref[...]
-    row = lax.broadcasted_iota(jnp.int32, (TAIL, NC), 0)
-    digits = jnp.where(row == 0, idx >> 4, jnp.where(row == 1, idx & (BASE - 1), 0))
-    digits = digits.astype(f32).astype(bf16)
-    out_ref[:, RZ:, :] = jnp.broadcast_to(digits[None], (SZ, TAIL, NC))
 
 
 def coarse_kernel(idx, res, basis):

time: 68.9 us -> 68.9 us (level)
  no operation moved by 1% of the time
where the time goes in v6:
time: 68.9 us; the launch traced here: 68.5 us
  starting transfers between devices  36 us (52%)
  Pallas kernels  16.4 us (24%)
  waiting for transfers between devices  13.5 us (20%)
  local copies, waits for them, and re-layouts  2.46 us (4%)
    ppermute x13, starting transfers between devices, permute(): return lax.ppermute(x, ('gx', 'gy', 'gz'), pairs)  20.7 us
    ppermute x13, waiting for transfers between devices, permute(): return lax.ppermute(x, ('gx', 'gy', 'gz'), pairs)  11.3 us
    all_to_all x1, starting transfers between devices, per_device(): back = lax.all_to_all(back, 'gz', 0, 0)  8.63 us
    all_to_all x1, starting transfers between devices, per_device(): lax.all_to_all(pack, 'gz', 0, 0)  6.67 us
    pallas_call x1, Pallas kernels, map_kernel(): call(map_body, (jax.ShapeDtypeStruct((C2, C2), bf16),) * 2, 0, 0, vmem=BI...  3.7 us
    pallas_call x2, Pallas kernels, last_kernel(): call(functools.partial(last_body, slots), jax.ShapeDtypeStruct((R, NI), b...  3 us
    pallas_call x1, Pallas kernels, coarse_kernel(): call(coarse_body, jax.ShapeDtypeStruct((SZ, PACK, NC), bf16), 0, 0, vmem=...  2.82 us
    pallas_call x1, Pallas kernels, local_kernel(): call(local_body, jax.ShapeDtypeStruct((FACES, R, FACE), bf16), 0, 0, vmem...  2.59 us
  transfers between devices with their start and end apart: 15, of which 8 were waited for; matrix products, arithmetic and copies ran while one was open for 0% of the time, Pallas kernels for 12%

profile of v6, /device:TPU:1, one launch (start us, length us, event | category | flops | bytes accessed | tf_op | source)
XLA Modules:
  0.0 68.5 jit_solution(4725776686183648081)
XLA Ops:
  0.0 2.8 %shard_map.82._ = bf16[8,80,128]{2,1,0:T(8,128)(2,1)} custom-call(s32[1,128]{1,0:T(1,128)} %bitcast.30, bf16[512,1536]{1,0:T(8,128)(2,1)} %bitcast.18, bf16[128,1536]{1,0:T(8,128)(2,1)} %bitcast.24), custom_call_target="tpu_custom_call" | custom-call | flops 1024 | bytes 1024 | tf_op jit(solution)/shard_map/pallas_call | solution.py:100
  2.8 0.0 copy-start.2
  2.8 6.7 %all-to-all-start = ((bf16[8,80,128]{2,1,0:T(8,128)(2,1)}), bf16[8,80,128]{2,1,0:T(8,128)(2,1)S(1)}, u32[]{:S(2)}, u32[]{:S(2)}) async-start(bf16[8,80,128]{2,1,0:T(8,128)(2,1)} %shard_map.82._), calls=%async_computation | async-start | bytes 327680 | tf_op jit(solution)/shard_map/all_to_all | solution.py:395
  9.5 0.0 copy-start
  9.5 3.7 %shard_map.83 = (bf16[512,512]{1,0:T(8,128)(2,1)}, bf16[512,512]{1,0:T(8,128)(2,1)}) custom-call(f32[512,512]{1,0:T(8,128)} %top_hbm.1, f32[512,512]{1,0:T(8,128)} %bitcast.22, bf16[8,80,128]{2,1,0:T(8,128)(2,1)} %shard_map.82._), custom_call_target="tpu_custom_call" | custom-call | flops 1024 | bytes 1024 | tf_op jit(solution)/shard_map/pallas_call | solution.py:177
  13.2 1.9 %all-to-all-done.pack_ref = bf16[8,80,128]{2,1,0:T(8,128)(2,1)S(1)} async-done(((bf16[8,80,128]{2,1,0:T(8,128)(2,1)}), bf16[8,80,128]{2,1,0:T(8,128)(2,1)S(1)}, u32[]{:S(2)}, u32[]{:S(2)}) %all-to-all-start) | async-done | bytes 163872 | tf_op jit(solution)/shard_map/all_to_all | solution.py:395
  15.1 0.0 copy-start.6
  15.1 0.0 copy-done.2
  15.1 0.8 %shard_map.84 = (f32[64,512]{1,0:T(8,128)S(1)}, bf16[64,512]{1,0:T(8,128)(2,1)S(1)}) custom-call(bf16[8,80,128]{2,1,0:T(8,128)(2,1)S(1)} %all-to-all-done.pack_ref, f32[512,512]{1,0:T(8,128)S(1)} %bitcast.23), custom_call_target="tpu_custom_call" | custom-call | flops 1024 | bytes 1024 | tf_op jit(solution)/shard_map/pallas_call | solution.py:153
  15.9 2.5 %collective-permute-start.2 = (bf16[64,512]{1,0:T(8,128)(2,1)S(1)}, bf16[64,512]{1,0:T(8,128)(2,1)S(1)}, u32[]{:S(2)}, u32[]{:S(2)}) collective-permute-start(bf16[64,512]{1,0:T(8,128)(2,1)S(1)} %get-tuple-element.20.refs_0_), channel_id=1, source_target_pairs={{0,128},{1,17},{2,130},{3,19},{4,132},{5,21},{6,134},{7,23},{8,136... | collective-permute-start | bytes 196616 | tf_op jit(solution)/shard_map/ppermute | solution.py:349
  18.4 1.4 %collective-permute-start.1 = (bf16[64,512]{1,0:T(8,128)(2,1)S(1)}, bf16[64,512]{1,0:T(8,128)(2,1)S(1)}, u32[]{:S(2)}, u32[]{:S(2)}) collective-permute-start(bf16[64,512]{1,0:T(8,128)(2,1)S(1)} %get-tuple-element.20.refs_0_), channel_id=1, source_target_pairs={{0,192},{1,25},{2,194},{3,27},{4,196},{5,29},{6,198},{7,31},{8,200... | collective-permute-start | bytes 196616 | tf_op jit(solution)/shard_map/ppermute | solution.py:349
  19.9 0.2 collective-permute-start
  20.1 0.0 collective-permute-done.2.refs_3_
  20.1 3.4 %collective-permute-done.1.refs_2_ = bf16[64,512]{1,0:T(8,128)(2,1)S(1)} collective-permute-done((bf16[64,512]{1,0:T(8,128)(2,1)S(1)}, bf16[64,512]{1,0:T(8,128)(2,1)S(1)}, u32[]{:S(2)}, u32[]{:S(2)}) %collective-permute-start.1) | collective-permute-done | bytes 65568 | tf_op jit(solution)/shard_map/ppermute | solution.py:349
  23.5 0.5 collective-permute-done.refs_1_
  24.0 2.5 %collective-permute-start.5 = (bf16[64,512]{1,0:T(8,128)(2,1)S(1)}, bf16[64,512]{1,0:T(8,128)(2,1)S(1)}, u32[]{:S(2)}, u32[]{:S(2)}) collective-permute-start(bf16[64,512]{1,0:T(8,128)(2,1)S(1)} %shard_map.86.refs_0_), channel_id=1, source_target_pairs={{0,16},{1,129},{2,18},{3,131},{4,20},{5,133},{6,22},{7,135},{8,24}... | collective-permute-start | bytes 196616 | tf_op jit(solution)/shard_map/ppermute | solution.py:349
  26.6 0.9 %collective-permute-start.4 = (bf16[64,512]{1,0:T(8,128)(2,1)S(1)}, bf16[64,512]{1,0:T(8,128)(2,1)S(1)}, u32[]{:S(2)}, u32[]{:S(2)}) collective-permute-start(bf16[64,512]{1,0:T(8,128)(2,1)S(1)} %shard_map.86.refs_0_), channel_id=1, source_target_pairs={{0,24},{1,193},{2,26},{3,195},{4,28},{5,197},{6,30},{7,199},{8,16}... | collective-permute-start | bytes 196616 | tf_op jit(solution)/shard_map/ppermute | solution.py:349
  27.4 0.0 collective-permute-start.3
  27.4 0.0 copy-done
  27.4 0.0 copy-done.6
  27.4 0.0 copy-start.3
  27.5 0.0 copy-start.4
  27.5 0.4 shard_map.85.refs_4_.own_ref
  27.9 0.9 %collective-permute-done.5.refs_3_ = bf16[64,512]{1,0:T(8,128)(2,1)S(1)} collective-permute-done((bf16[64,512]{1,0:T(8,128)(2,1)S(1)}, bf16[64,512]{1,0:T(8,128)(2,1)S(1)}, u32[]{:S(2)}, u32[]{:S(2)}) %collective-permute-start.5) | collective-permute-done | bytes 65568 | tf_op jit(solution)/shard_map/ppermute | solution.py:349
  28.7 2.2 %collective-permute-done.4.refs_2_ = bf16[64,512]{1,0:T(8,128)(2,1)S(1)} collective-permute-done((bf16[64,512]{1,0:T(8,128)(2,1)S(1)}, bf16[64,512]{1,0:T(8,128)(2,1)S(1)}, u32[]{:S(2)}, u32[]{:S(2)}) %collective-permute-start.4) | collective-permute-done | bytes 65568 | tf_op jit(solution)/shard_map/ppermute | solution.py:349
  30.9 0.0 collective-permute-done.3.refs_1_
  30.9 4.5 %collective-permute-start.6 = (bf16[64,512]{1,0:T(8,128)(2,1)S(1)}, bf16[64,512]{1,0:T(8,128)(2,1)S(1)}, u32[]{:S(2)}, u32[]{:S(2)}) collective-permute-start(bf16[64,512]{1,0:T(8,128)(2,1)S(1)} %shard_map.87.part_ref), channel_id=1, source_target_pairs={{0,56},{1,57},{2,58},{3,59},{4,60},{5,61},{6,62},{7,63},{8,48},{9,... | collective-permute-start | bytes 196616 | tf_op jit(solution)/shard_map/ppermute | solution.py:349
  35.4 0.0 copy-done.3
  35.4 0.0 copy-done.4
  35.4 0.0 copy-start.7
  35.4 0.3 shard_map.88.base_ref
  35.7 1.5 %collective-permute-done.6.got_ref = bf16[64,512]{1,0:T(8,128)(2,1)S(1)} collective-permute-done((bf16[64,512]{1,0:T(8,128)(2,1)S(1)}, bf16[64,512]{1,0:T(8,128)(2,1)S(1)}, u32[]{:S(2)}, u32[]{:S(2)}) %collective-permute-start.6) | collective-permute-done | bytes 65568 | tf_op jit(solution)/shard_map/ppermute | solution.py:349
  37.2 1.2 %shard_map.89._ = bf16[8,64,128]{2,1,0:T(8,128)(2,1)} custom-call(bf16[8,80,128]{2,1,0:T(8,128)(2,1)S(1)} %all-to-all-done.pack_ref, f32[64,512]{1,0:T(8,128)S(1)} %shard_map.88.base_ref, bf16[512,512]{1,0:T(8,128)(2,1)S(1)} %copy-done.3, bf16[512,512]{1,0:T(8,128)(2,1)S(1)} %copy-done.4, bf16[64,512]{1,0:T(8,128)(2,1)S(1)} %collective-permute-done.6.got_ref), custom_call_target="tpu_custom_call" | custom-call | flops 1024 | bytes 1024 | tf_op jit(solution)/shard_map/pallas_call | solution.py:243
  38.4 8.6 %all-to-all-start.1 = ((bf16[8,64,128]{2,1,0:T(8,128)(2,1)}), bf16[8,64,128]{2,1,0:T(8,128)(2,1)}, u32[]{:S(2)}, u32[]{:S(2)}) async-start(bf16[8,64,128]{2,1,0:T(8,128)(2,1)} %shard_map.89._), calls=%async_computation.1 | async-start | bytes 262144 | tf_op jit(solution)/shard_map/all_to_all | solution.py:407
  47.0 0.0 copy-done.7
  47.0 0.1 concatenate.3
  47.1 0.0 copy-start.1
  47.1 2.3 %copy-done.1 = bf16[1,1,1,1536,1536]{4,3,2,1,0:T(8,128)(2,1)S(1)} copy-done((bf16[1,1,1,1536,1536]{4,3,2,1,0:T(8,128)(2,1)S(1)}, bf16[1,1,1,1536,1536]{4,3,2,1,0:T(8,128)(2,1)}, u32[]{:S(2)}) %copy-start.1) | copy-done | bytes 4718616
  49.5 0.0 copy-start.5
  49.5 2.6 %shard_map.90.local_ref = bf16[6,512,256]{2,1,0:T(8,128)(2,1)S(1)} custom-call(bf16[512,1536]{1,0:T(8,128)(2,1)S(1)} %bitcast.20, bf16[1536,1536]{1,0:T(8,128)(2,1)S(1)} %bitcast.21, bf16[8,64,128]{2,1,0:T(8,128)(2,1)} %shard_map.89._), custom_call_target="tpu_custom_call" | custom-call | flops 1024 | bytes 1024 | tf_op jit(solution)/shard_map/pallas_call | solution.py:123
  52.1 0.4 all-to-all-done.1.back_ref
  52.4 0.0 copy-done.5
  52.4 1.5 %shard_map.91 = (bf16[512,256]{1,0:T(8,128)(2,1)S(1)}, bf16[512,256]{1,0:T(8,128)(2,1)S(1)}, bf16[512,256]{1,0:T(8,128)(2,1)S(1)}, bf16[512,256]{1,0:T(8,128)(2,...) custom-call(s32[1,21]{1,0:T(1,128)S(1)} %bitcast.27, bf16[8,64,128]{2,1,0:T(8,128)(2,1)} %all-to-all-done.1.back_ref, ...), custom_call_target="tpu_custom_call" | custom-call | flops 1024 | bytes 1024 | tf_op jit(solution)/shard_map/pallas_call | solution.py:297
  54.0 0.4 collective-permute-start.11
  54.4 3.8 %collective-permute-start.7 = (bf16[512,256]{1,0:T(8,128)(2,1)S(1)}, bf16[512,256]{1,0:T(8,128)(2,1)S(1)}, u32[]{:S(2)}, u32[]{:S(2)}) collective-permute-start(bf16[512,256]{1,0:T(8,128)(2,1)S(1)} %get-tuple-element.21.refs_0_), channel_id=1, source_target_pairs={{0,192},{1,57},{2,194},{3,59},{4,196},{5,61},{6,198},{7,63},{8,200... | collective-permute-start | bytes 786440 | tf_op jit(solution)/shard_map/ppermute | solution.py:349
  58.2 1.7 %collective-permute-start.8 = (bf16[512,256]{1,0:T(8,128)(2,1)S(1)}, bf16[512,256]{1,0:T(8,128)(2,1)S(1)}, u32[]{:S(2)}, u32[]{:S(2)}) collective-permute-start(bf16[512,256]{1,0:T(8,128)(2,1)S(1)} %get-tuple-element.22.refs_1_), channel_id=1, source_target_pairs={{0,56},{1,193},{2,58},{3,195},{4,60},{5,197},{6,62},{7,199},{8,16}... | collective-permute-start | bytes 786440 | tf_op jit(solution)/shard_map/ppermute | solution.py:349
  60.0 0.0 collective-permute-start.12
  60.0 1.3 %collective-permute-start.9 = (bf16[512,256]{1,0:T(8,128)(2,1)S(1)}, bf16[512,256]{1,0:T(8,128)(2,1)S(1)}, u32[]{:S(2)}, u32[]{:S(2)}) collective-permute-start(bf16[512,256]{1,0:T(8,128)(2,1)S(1)} %get-tuple-element.23.refs_2_), channel_id=1, source_target_pairs={{0,7},{1,2},{2,1},{3,4},{4,3},{5,6},{6,5},{7,0},{8,15},{9,10},{10,... | collective-permute-start | bytes 786440 | tf_op jit(solution)/shard_map/ppermute | solution.py:349
  61.2 0.0 collective-permute-done.11.refs_2_
  61.2 1.4 %collective-permute-start.10 = (bf16[512,256]{1,0:T(8,128)(2,1)S(1)}, bf16[512,256]{1,0:T(8,128)(2,1)S(1)}, u32[]{:S(2)}, u32[]{:S(2)}) collective-permute-start(bf16[512,256]{1,0:T(8,128)(2,1)S(1)} %get-tuple-element.24.refs_3_), channel_id=1, source_target_pairs={{0,1},{1,0},{2,3},{3,2},{4,5},{5,4},{6,7},{7,6},{8,9},{9,8},{10,11... | collective-permute-start | bytes 786440 | tf_op jit(solution)/shard_map/ppermute | solution.py:349
  62.7 2.8 %collective-permute-done.12.refs_3_ = bf16[512,256]{1,0:T(8,128)(2,1)S(1)} collective-permute-done((bf16[512,256]{1,0:T(8,128)(2,1)S(1)}, bf16[512,256]{1,0:T(8,128)(2,1)S(1)}, u32[]{:S(2)}, u32[]{:S(2)}) %collective-permute-start.12) | collective-permute-done | bytes 262176 | tf_op jit(solution)/shard_map/ppermute | solution.py:349
  65.5 1.4 %shard_map.92.refs_8_ = bf16[512,1536]{1,0:T(8,128)(2,1)} custom-call(s32[1,21]{1,0:T(1,128)S(1)} %bitcast.28, bf16[512,256]{1,0:T(8,128)(2,1)S(1)} %get-tuple-element.25.refs_0_, bf16[512,256]{1,0:T(8,128)(2,1)S(1)} %get-tuple-element.26.refs_1_, bf16[512,256]{1,0:T(8,128)(2,1)S(1)} %collective-permute-done.11.refs_2_, ...), custom_call_target="tpu_custom_call" | custom-call | flops 1024 | bytes 1024 | tf_op jit(solution)/shard_map/pallas_call | solution.py:329
  66.9 0.0 collective-permute-done.7.refs_4_
  66.9 0.0 collective-permute-done.8.refs_5_
  66.9 0.0 collective-permute-done.9.refs_6_
  66.9 0.0 collective-permute-done.10.refs_7_
  66.9 1.6 %shard_map.93 = bf16[512,1536]{1,0:T(8,128)(2,1)} custom-call(s32[1,21]{1,0:T(1,128)S(1)} %bitcast.29, bf16[512,256]{1,0:T(8,128)(2,1)S(1)} %get-tuple-element.21.refs_0_, bf16[512,256]{1,0:T(8,128)(2,1)S(1)} %get-tuple-element.22.refs_1_, bf16[512,256]{1,0:T(8,128)(2,1)S(1)} %get-tuple-element.23.refs_2_, ...), custom_call_target="tpu_custom_call", output_to_operand_aliasing={{}: (9, {})} | custom-call | flops 1024 | bytes 1024 | tf_op jit(solution)/shard_map/pallas_call | solution.py:329
  (2 shorter events, 0.1 us)
Async XLA Ops:
  2.8 12.3 %copy-start.2 = (f32[1,1,512,512]{3,2,1,0:T(8,128)S(1)}, f32[1,1,512,512]{3,2,1,0:T(8,128)}, u32[]{:S(2)}) copy-start(f32[1,1,512,512]{3,2,1,0:T(8,128)} %param.14) | copy-start | bytes 3145732
  2.8 12.3 %all-to-all-start = ((bf16[8,80,128]{2,1,0:T(8,128)(2,1)}), bf16[8,80,128]{2,1,0:T(8,128)(2,1)S(1)}, u32[]{:S(2)}, u32[]{:S(2)}) async-start(bf16[8,80,128]{2,1,0:T(8,128)(2,1)} %shard_map.82._), calls=%async_computation | async-start | bytes 327680 | tf_op jit(solution)/shard_map/all_to_all | solution.py:395
  9.5 17.9 %copy-start = (bf16[1,1,1,512,1536]{4,3,2,1,0:T(8,128)(2,1)S(1)}, bf16[1,1,1,512,1536]{4,3,2,1,0:T(8,128)(2,1)}, u32[]{:S(2)}) copy-start(bf16[1,1,1,512,1536]{4,3,2,1,0:T(8,128)(2,1)} %param.8) | copy-start | bytes 4718596
  15.1 12.3 %copy-start.6 = (f32[1,1,512,512]{3,2,1,0:T(8,128)S(1)}, f32[1,1,512,512]{3,2,1,0:T(8,128)}, u32[]{:S(2)}) copy-start(f32[1,1,512,512]{3,2,1,0:T(8,128)} %param.13) | copy-start | bytes 3145732
  15.9 4.2 %collective-permute-start.2 = (bf16[64,512]{1,0:T(8,128)(2,1)S(1)}, bf16[64,512]{1,0:T(8,128)(2,1)S(1)}, u32[]{:S(2)}, u32[]{:S(2)}) collective-permute-start(bf16[64,512]{1,0:T(8,128)(2,1)S(1)} %get-tuple-element.20.refs_0_), channel_id=1, source_target_pairs={{0,128},{1,17},{2,130},{3,19},{4,132},{5,21},{6,134},{7,23},{8,136... | collective-permute-start | bytes 196616 | tf_op jit(solution)/shard_map/ppermute | solution.py:349
  18.4 5.1 %collective-permute-start.1 = (bf16[64,512]{1,0:T(8,128)(2,1)S(1)}, bf16[64,512]{1,0:T(8,128)(2,1)S(1)}, u32[]{:S(2)}, u32[]{:S(2)}) collective-permute-start(bf16[64,512]{1,0:T(8,128)(2,1)S(1)} %get-tuple-element.20.refs_0_), channel_id=1, source_target_pairs={{0,192},{1,25},{2,194},{3,27},{4,196},{5,29},{6,198},{7,31},{8,200... | collective-permute-start | bytes 196616 | tf_op jit(solution)/shard_map/ppermute | solution.py:349
  19.9 4.1 %collective-permute-start = (bf16[64,512]{1,0:T(8,128)(2,1)S(1)}, bf16[64,512]{1,0:T(8,128)(2,1)S(1)}, u32[]{:S(2)}, u32[]{:S(2)}) collective-permute-start(bf16[64,512]{1,0:T(8,128)(2,1)S(1)} %get-tuple-element.20.refs_0_), channel_id=1, source_target_pairs={{0,64},{1,9},{2,66},{3,11},{4,68},{5,13},{6,70},{7,15},{8,72},{9,1... | collective-permute-start | bytes 196616 | tf_op jit(solution)/shard_map/ppermute | solution.py:349
  24.0 4.7 %collective-permute-start.5 = (bf16[64,512]{1,0:T(8,128)(2,1)S(1)}, bf16[64,512]{1,0:T(8,128)(2,1)S(1)}, u32[]{:S(2)}, u32[]{:S(2)}) collective-permute-start(bf16[64,512]{1,0:T(8,128)(2,1)S(1)} %shard_map.86.refs_0_), channel_id=1, source_target_pairs={{0,16},{1,129},{2,18},{3,131},{4,20},{5,133},{6,22},{7,135},{8,24}... | collective-permute-start | bytes 196616 | tf_op jit(solution)/shard_map/ppermute | solution.py:349
  26.6 4.3 %collective-permute-start.4 = (bf16[64,512]{1,0:T(8,128)(2,1)S(1)}, bf16[64,512]{1,0:T(8,128)(2,1)S(1)}, u32[]{:S(2)}, u32[]{:S(2)}) collective-permute-start(bf16[64,512]{1,0:T(8,128)(2,1)S(1)} %shard_map.86.refs_0_), channel_id=1, source_target_pairs={{0,24},{1,193},{2,26},{3,195},{4,28},{5,197},{6,30},{7,199},{8,16}... | collective-permute-start | bytes 196616 | tf_op jit(solution)/shard_map/ppermute | solution.py:349
  27.4 3.5 %collective-permute-start.3 = (bf16[64,512]{1,0:T(8,128)(2,1)S(1)}, bf16[64,512]{1,0:T(8,128)(2,1)S(1)}, u32[]{:S(2)}, u32[]{:S(2)}) collective-permute-start(bf16[64,512]{1,0:T(8,128)(2,1)S(1)} %shard_map.86.refs_0_), channel_id=1, source_target_pairs={{0,8},{1,65},{2,10},{3,67},{4,12},{5,69},{6,14},{7,71},{8,0},{9,73... | collective-permute-start | bytes 196616 | tf_op jit(solution)/shard_map/ppermute | solution.py:349
  27.4 8.0 %copy-start.3 = (bf16[512,512]{1,0:T(8,128)(2,1)S(1)}, bf16[512,512]{1,0:T(8,128)(2,1)}, u32[]{:S(2)}) copy-start(bf16[512,512]{1,0:T(8,128)(2,1)} %get-tuple-element.16.hi_ref) | copy-start | bytes 1572868
  27.5 7.9 %copy-start.4 = (bf16[512,512]{1,0:T(8,128)(2,1)S(1)}, bf16[512,512]{1,0:T(8,128)(2,1)}, u32[]{:S(2)}) copy-start(bf16[512,512]{1,0:T(8,128)(2,1)} %get-tuple-element.19.lo_ref) | copy-start | bytes 1572868
  30.9 6.3 %collective-permute-start.6 = (bf16[64,512]{1,0:T(8,128)(2,1)S(1)}, bf16[64,512]{1,0:T(8,128)(2,1)S(1)}, u32[]{:S(2)}, u32[]{:S(2)}) collective-permute-start(bf16[64,512]{1,0:T(8,128)(2,1)S(1)} %shard_map.87.part_ref), channel_id=1, source_target_pairs={{0,56},{1,57},{2,58},{3,59},{4,60},{5,61},{6,62},{7,63},{8,48},{9,... | collective-permute-start | bytes 196616 | tf_op jit(solution)/shard_map/ppermute | solution.py:349
  35.4 11.6 %copy-start.7 = (s32[1,1,1,12]{3,2,1,0:T(1,128)S(1)}, s32[1,1,1,12]{3,2,1,0:T(1,128)}, u32[]{:S(2)}) copy-start(s32[1,1,1,12]{3,2,1,0:T(1,128)} %param.12) | copy-start | bytes 148
  38.4 14.0 %all-to-all-start.1 = ((bf16[8,64,128]{2,1,0:T(8,128)(2,1)}), bf16[8,64,128]{2,1,0:T(8,128)(2,1)}, u32[]{:S(2)}, u32[]{:S(2)}) async-start(bf16[8,64,128]{2,1,0:T(8,128)(2,1)} %shard_map.89._), calls=%async_computation.1 | async-start | bytes 262144 | tf_op jit(solution)/shard_map/all_to_all | solution.py:407
  47.1 2.3 %copy-start.1 = (bf16[1,1,1,1536,1536]{4,3,2,1,0:T(8,128)(2,1)S(1)}, bf16[1,1,1,1536,1536]{4,3,2,1,0:T(8,128)(2,1)}, u32[]{:S(2)}) copy-start(bf16[1,1,1,1536,1536]{4,3,2,1,0:T(8,128)(2,1)} %param.9) | copy-start | bytes 14155780
  49.5 3.0 %copy-start.5 = (bf16[1,1,1,128,1536]{4,3,2,1,0:T(8,128)(2,1)S(1)}, bf16[1,1,1,128,1536]{4,3,2,1,0:T(8,128)(2,1)}, u32[]{:S(2)}) copy-start(bf16[1,1,1,128,1536]{4,3,2,1,0:T(8,128)(2,1)} %param.10) | copy-start | bytes 1179652
  54.0 7.3 %collective-permute-start.11 = (bf16[512,256]{1,0:T(8,128)(2,1)S(1)}, bf16[512,256]{1,0:T(8,128)(2,1)S(1)}, u32[]{:S(2)}, u32[]{:S(2)}) collective-permute-start(bf16[512,256]{1,0:T(8,128)(2,1)S(1)} %get-tuple-element.25.refs_0_), channel_id=1, source_target_pairs={{0,64},{1,9},{2,66},{3,11},{4,68},{5,13},{6,70},{7,15},{8,72},{9,1... | collective-permute-start | bytes 786440 | tf_op jit(solution)/shard_map/ppermute | solution.py:349
  54.4 12.5 %collective-permute-start.7 = (bf16[512,256]{1,0:T(8,128)(2,1)S(1)}, bf16[512,256]{1,0:T(8,128)(2,1)S(1)}, u32[]{:S(2)}, u32[]{:S(2)}) collective-permute-start(bf16[512,256]{1,0:T(8,128)(2,1)S(1)} %get-tuple-element.21.refs_0_), channel_id=1, source_target_pairs={{0,192},{1,57},{2,194},{3,59},{4,196},{5,61},{6,198},{7,63},{8,200... | collective-permute-start | bytes 786440 | tf_op jit(solution)/shard_map/ppermute | solution.py:349
  58.2 8.7 %collective-permute-start.8 = (bf16[512,256]{1,0:T(8,128)(2,1)S(1)}, bf16[512,256]{1,0:T(8,128)(2,1)S(1)}, u32[]{:S(2)}, u32[]{:S(2)}) collective-permute-start(bf16[512,256]{1,0:T(8,128)(2,1)S(1)} %get-tuple-element.22.refs_1_), channel_id=1, source_target_pairs={{0,56},{1,193},{2,58},{3,195},{4,60},{5,197},{6,62},{7,199},{8,16}... | collective-permute-start | bytes 786440 | tf_op jit(solution)/shard_map/ppermute | solution.py:349
  60.0 5.5 %collective-permute-start.12 = (bf16[512,256]{1,0:T(8,128)(2,1)S(1)}, bf16[512,256]{1,0:T(8,128)(2,1)S(1)}, u32[]{:S(2)}, u32[]{:S(2)}) collective-permute-start(bf16[512,256]{1,0:T(8,128)(2,1)S(1)} %get-tuple-element.26.refs_1_), channel_id=1, source_target_pairs={{0,8},{1,65},{2,10},{3,67},{4,12},{5,69},{6,14},{7,71},{8,0},{9,73... | collective-permute-start | bytes 786440 | tf_op jit(solution)/shard_map/ppermute | solution.py:349
  60.0 6.9 %collective-permute-start.9 = (bf16[512,256]{1,0:T(8,128)(2,1)S(1)}, bf16[512,256]{1,0:T(8,128)(2,1)S(1)}, u32[]{:S(2)}, u32[]{:S(2)}) collective-permute-start(bf16[512,256]{1,0:T(8,128)(2,1)S(1)} %get-tuple-element.23.refs_2_), channel_id=1, source_target_pairs={{0,7},{1,2},{2,1},{3,4},{4,3},{5,6},{6,5},{7,0},{8,15},{9,10},{10,... | collective-permute-start | bytes 786440 | tf_op jit(solution)/shard_map/ppermute | solution.py:349
  61.2 5.7 %collective-permute-start.10 = (bf16[512,256]{1,0:T(8,128)(2,1)S(1)}, bf16[512,256]{1,0:T(8,128)(2,1)S(1)}, u32[]{:S(2)}, u32[]{:S(2)}) collective-permute-start(bf16[512,256]{1,0:T(8,128)(2,1)S(1)} %get-tuple-element.24.refs_3_), channel_id=1, source_target_pairs={{0,1},{1,0},{2,3},{3,2},{4,5},{5,4},{6,7},{7,6},{8,9},{9,8},{10,11... | collective-permute-start | bytes 786440 | tf_op jit(solution)/shard_map/ppermute | solution.py:349
